TPU v7x, 32 devices: a whole 2x2x4 slice. The times are simulated.
32 devices in a mesh: zone: 4 (over y, x), block: 8 (over z, core).
Axes of the slice: x: 2, y: 2, z: 4, core: 2. Of those that a mesh axis runs over, the one named last changes fastest.
Arguments:
- start_state: float32 [5, 4, 1024, 512], P(None, 'zone', 'block'), may hold values from -6 to 6
- diffusivity: float32 [4, 1024, 512], P('zone', 'block'), may hold values from 0.02 to 0.2
- donor_map: int32 [4, 4, 1024], P(None, 'zone'), may hold values from 0 to 1023, as said below
- donor_weight: float32 [4, 4, 1024], P(None, 'zone'), may hold values from 0 to 1
- coupling: float32 [5, 5], replicated, may hold values from -0.15 to 0.15
- final_cotangent: float32 [5, 4, 1024, 512], P(None, 'zone', 'block'), may hold values from -6 to 6
- wall_area: float32 [4, 3072], P('zone', 'block'), may hold values from 0.5 to 2
- wall_projection: float32 [3, 5], replicated, may hold values from -2.5 to 2.5
- center_ids: int32 [4, 8, 3072], P('zone', None, 'block'), may hold values from 0 to 8191
- center_dist: float32 [4, 8, 3072], P('zone', None, 'block'), may hold values from 0 to 0.95
Outputs:
- adjoint_start: float32 [5, 4, 1024, 512], P(None, 'zone', 'block')
- shape_gradient: float32 [3, 8192], P(None, ('zone', 'block'))
Inputs may be any that keep to these rules, and one draw needn't show every extreme that they name: For each step n and zone z there is an offset t, and donor_map[n, z, a] = (a + t + e) mod 1024 with e in 0 to 4.
All inputs are finite; a program needn't handle non-finite values.
Results may differ from a plain program's by a relative error of at most 0.0003.
Values sent between devices are 32-bit elements; how exact they have to be, the bound alone decides.
No kernel may reach another device: no remote copies, remote signals or barrier semaphores. Data moves between devices by JAX's collectives and lax.ppermute only.
A program may use at most 128 MiB of HBM per device.

v0:
```python
import jax
import jax.numpy as jnp
from jax import lax
from jax.sharding import PartitionSpec as P

CP_DEV = 256


def swapped(value, axis, bit):
    mask = 2**bit
    pairs = [(source, source ^ mask) for source in range(lax.axis_size(axis))]
    return lax.ppermute(value, axis, pairs)


def extended(x, sides, width):
    for axis, dim in sides:
        size, length = (lax.axis_size(axis), x.shape[dim])
        up = [(i, (i + 1) % size) for i in range(size)]
        down = [(j, i) for i, j in up]
        last = lax.slice_in_dim(x, length - width, length, axis=dim)
        leading = lax.slice_in_dim(x, 0, width, axis=dim)
        before = lax.ppermute(last, axis, up)
        after = lax.ppermute(leading, axis, down)
        x = jnp.concatenate([before, x, after], axis=dim)
    return x


def advance(
    current, kappa_rows, partner_face, donor_rows, donor_share, first_row, total_rows, coupling
):
    middle = current[:, :, 1:-1]
    row_count = middle.shape[2]
    global_rows = (first_row + jnp.arange(row_count, dtype=jnp.int32)) % total_rows
    first_donor = jnp.take(donor_rows, global_rows)
    donor_part = jnp.take(donor_share, global_rows)
    second_donor = (first_donor + 1) % total_rows
    ghost = donor_part * jnp.take(partner_face, first_donor, axis=1) + (
        1.0 - donor_part
    ) * jnp.take(partner_face, second_donor, axis=1)
    outward = jnp.concatenate([middle[..., 1:], ghost[:, None, :, None]], axis=-1)
    inward = jnp.concatenate([jnp.zeros_like(middle[..., :1]), middle[..., :-1]], axis=-1)
    laplace = current[:, :, 2:] + current[:, :, :-2] + outward + inward - 4.0 * middle
    reaction = jnp.einsum(
        "vw,wzar->vzar", coupling, jnp.tanh(middle), precision=lax.Precision.HIGHEST
    )
    return middle + kappa_rows[:, :, 1:-1] * laplace - reaction


def gather_face(outer_face):
    mirrored = swapped(outer_face, "zone", 0)
    partner_face = lax.all_gather(mirrored, "block", axis=1, tiled=True)
    return partner_face


def return_face(ghost_adjoint, donor_rows, donor_share, own_global, total_rows):
    first_donor = jnp.take(donor_rows, own_global)
    donor_part = jnp.take(donor_share, own_global)
    second_donor = (first_donor + 1) % total_rows
    variables = ghost_adjoint.shape[0]
    collected = jnp.zeros((variables, total_rows), jnp.float32)
    collected = collected.at[:, first_donor].add(donor_part * ghost_adjoint)
    collected = collected.at[:, second_donor].add((1.0 - donor_part) * ghost_adjoint)
    partial_rows = lax.psum_scatter(collected, "block", scatter_dimension=1, tiled=True)
    owned = swapped(partial_rows, "zone", 0)
    return owned


def local(
    start_state,
    diffusivity,
    donor_map,
    donor_weight,
    coupling,
    final_cotangent,
    wall_area,
    wall_projection,
    center_ids,
    center_dist,
):
    variables, _, own_rows, radial = start_state.shape
    block_count = lax.axis_size("block")
    zone_count = lax.axis_size("zone")
    total_rows = own_rows * block_count
    block_index = lax.axis_index("block")
    step_count = donor_map.shape[0]
    kappa_own = diffusivity[None]
    stacked = jnp.concatenate([start_state, kappa_own], axis=0)
    rim_width = 1
    widened = extended(stacked, (("block", 2),), rim_width)
    kappa_wide = widened[variables:]
    current = widened[:variables]
    history = []
    for time_step in range(step_count - 1):
        margin = 1
        if time_step > 0:
            current = extended(current, (("block", 2),), 1)
        interior = current[:, :, margin : margin + own_rows]
        history.append(interior)
        partner_face = gather_face(interior[:, 0, :, radial - 1])
        current = advance(
            current,
            kappa_wide,
            partner_face,
            donor_map[time_step, 0],
            donor_weight[time_step, 0],
            block_index * own_rows - margin + 1,
            total_rows,
            coupling,
        )
    history.append(current)
    own_global = block_index * own_rows + jnp.arange(own_rows, dtype=jnp.int32)
    adjoint = final_cotangent
    wall_product = jnp.zeros((variables, own_rows), jnp.float32)
    for time_step in reversed(range(step_count)):
        state = history[time_step]
        wall_product = wall_product + adjoint[:, 0, :, 0] * state[:, 0, :, 0]
        scaled = kappa_own * adjoint
        scaled_wide = extended(scaled, (("block", 2),), 1)
        outward = jnp.concatenate([scaled[..., 1:], jnp.zeros_like(scaled[..., :1])], axis=-1)
        inward = jnp.concatenate([jnp.zeros_like(scaled[..., :1]), scaled[..., :-1]], axis=-1)
        transposed = (
            scaled_wide[:, :, 2:] + scaled_wide[:, :, :-2] + outward + inward - 4.0 * scaled
        )
        tangent = jnp.tanh(state)
        pulled = jnp.einsum("wv,wzar->vzar", coupling, adjoint, precision=lax.Precision.HIGHEST)
        face_back = return_face(
            scaled[:, 0, :, radial - 1],
            donor_map[time_step, 0],
            donor_weight[time_step, 0],
            own_global,
            total_rows,
        )
        adjoint = adjoint + transposed - (1.0 - tangent * tangent) * pulled
        adjoint = adjoint.at[:, 0, :, radial - 1].add(face_back)
    per_cell = wall_area.shape[1] // own_rows
    repeated = jnp.repeat(wall_product, per_cell, axis=1)
    sensitivity = wall_area * jnp.einsum(
        "cv,vw->cw", wall_projection, repeated, precision=lax.Precision.HIGHEST
    )
    distance = center_dist[0]
    kernel = (1.0 - distance) ** 4 * (4.0 * distance + 1.0)
    weighted = kernel[None] * sensitivity[:, None, :]
    point_total = CP_DEV * zone_count * block_count
    accumulated = (
        jnp.zeros((3, point_total), jnp.float32)
        .at[:, center_ids[0].reshape(-1)]
        .add(weighted.reshape(3, -1))
    )
    owned_points = lax.psum_scatter(accumulated, ("zone", "block"), scatter_dimension=1, tiled=True)
    return (adjoint, owned_points)


def solution(mesh):
    return jax.shard_map(
        local,
        mesh=mesh,
        in_specs=(
            P(None, "zone", "block", None),
            P("zone", "block", None),
            P(None, "zone", None),
            P(None, "zone", None),
            P(),
            P(None, "zone", "block", None),
            P("zone", "block"),
            P(),
            P("zone", None, "block"),
            P("zone", None, "block"),
        ),
        out_specs=(P(None, "zone", "block", None), P(None, ("zone", "block"))),
        check_vma=False,
    )
```

profile of v0, /device:TPU:0, one launch (start us, length us, event | category | flops | bytes accessed | tf_op | source)
XLA Modules:
  0.0 518.4 jit_solution(14841676855573381864)
XLA Ops:
  9.8 2.9 collective-permute-start.4
  20.9 3.5 collective-permute-start
  33.8 3.1 scatter_fusion
  37.0 4.9 fusion.139
  67.7 16.3 %all_gather.9 = f32[5,1024]{0,1:T(8,128)} all-gather(f32[5,128]{0,1:T(8,128)} %collective-permute-done.4), channel_id=1, replica_groups=mesh['zone'=4,'block'=8] {'block'}, dimensions={1}, use_global_device_ids=true | all-gather | bytes 23040 | tf_op jit(solution)/shard_map/all_gather | solution.py:51
  89.3 8.1 %fusion.38 = f32[5,1,128,512]{3,0,2,1:T(8,128)S(1)} fusion(f32[5,1,128,512]{3,0,2,1:T(8,128)} %copy-done.1, f32[6,1,1,512]{3,0,2,1:T(8,128)} %collective-permute-done.3, f32[1,1,128,512]{3,0,2,1:T(1,128)} %copy-done.12, f32[6,1,1,512]{3,0,2,1:T(8,128)} %collective-permute-done.2, f32[5,1,128,1]{3,0,2,1:T(8,128)} %copy.89, ...), kind=kOutput, calls=%fused_computation.78 | convolution fusion | flops 23920640 | bytes 5789284 | tf_op jit(solution)/shard_map/vw,wzar->vzar/dot_general | solution.py:43
  107.5 15.8 %all_gather.10 = f32[5,1024]{0,1:T(8,128)} all-gather(f32[5,128]{0,1:T(8,128)S(1)} %collective-permute-done.7), channel_id=1, replica_groups=mesh['zone'=4,'block'=8] {'block'}, dimensions={1}, use_global_device_ids=true | all-gather | bytes 23040 | tf_op jit(solution)/shard_map/all_gather | solution.py:51
  128.7 8.1 %fusion.31 = f32[5,1,128,512]{3,0,2,1:T(8,128)S(1)} fusion(f32[5,1,128,512]{3,0,2,1:T(8,128)} %copy-done.2, f32[5,1,1,512]{3,0,2,1:T(8,128)} %collective-permute-done.6, f32[5,1,1,512]{3,0,2,1:T(8,128)} %collective-permute-done.5, f32[5,1,128,1]{3,0,2,1:T(8,128)} %copy.98, f32[5,1,128,511]{3,0,2,1:T(8,128)} %get-tuple-element.106, ...), kind=kOutput, calls=%fused_computation.69 | convolution fusion | flops 23265280 | bytes 5523044 | tf_op jit(solution)/shard_map/vw,wzar->vzar/dot_general | solution.py:43
  146.8 16.0 %all_gather.11 = f32[5,1024]{0,1:T(8,128)} all-gather(f32[5,128]{0,1:T(8,128)S(1)} %collective-permute-done.10), channel_id=1, replica_groups=mesh['zone'=4,'block'=8] {'block'}, dimensions={1}, use_global_device_ids=true | all-gather | bytes 23040 | tf_op jit(solution)/shard_map/all_gather | solution.py:51
  168.1 10.0 %fusion.24 = f32[5,1,128,512]{3,0,2,1:T(8,128)} fusion(f32[5,1,128,512]{3,0,2,1:T(8,128)} %copy-done.3, f32[5,1,1,512]{3,0,2,1:T(8,128)} %collective-permute-done.9, f32[5,1,1,512]{3,0,2,1:T(8,128)} %collective-permute-done.8, f32[5,1,128,1]{3,0,2,1:T(8,128)} %copy.103, f32[5,1,128,511]{3,0,2,1:T(8,128)} %get-tuple-element.102, ...), kind=kOutput, calls=%fused_computation.60 | convolution fusion | flops 23265280 | bytes 5523044 | tf_op jit(solution)/shard_map/vw,wzar->vzar/dot_general | solution.py:43
  178.7 8.5 %fusion.44 = f32[5,1,128,512]{3,0,2,1:T(8,128)} fusion(f32[5,1,128,512]{3,0,2,1:T(8,128)S(1)} %get-tuple-element.114, f32[5,1,1,512]{3,0,2,1:T(8,128)} %collective-permute-done.1, f32[5,1,1,512]{3,0,2,1:T(8,128)} %collective-permute-done, f32[5,1,128,512]{3,0,2,1:T(8,128)} %fusion.24, f32[5,1,128,511]{3,0,2,1:T(8,128)} %get-tuple-element.100, ...), kind=kOutput, calls=%fused_computation.88 | convolution fusion | flops 23592960 | bytes 9190500 | tf_op jit(solution)/shard_map/wv,wzar->vzar/dot_general | solution.py:125
  190.6 12.6 %scatter-add.85 = f32[5,1,128,512]{3,0,2,1:T(8,128)} dynamic-update-slice(f32[5,1,128,512]{3,0,2,1:T(8,128)} %fusion.44, f32[5,1,128,1]{3,0,2,1:T(8,128)S(1)} %add_select_fusion.3, s32[]{:T(128)} %constant.194.clone.1, s32[]{:T(128)} %constant.194.clone.1, s32[]{:T(128)} %constant.194.clone.1, s32[]{:T(128)} %bitcast.33) | dynamic-update-slice | bytes 5124 | tf_op jit(solution)/shard_map/scatter-add | solution.py:134
  214.7 25.2 %reduce-scatter.8.cloned.1.call-done = f32[5,128]{0,1:T(8,128)} async-done(((f32[5,1024]{0,1:T(8,128)}), f32[5,128]{0,1:T(8,128)}) %reduce-scatter.8.cloned.1.call-update) | async-done | bytes 2576 | tf_op jit(solution)/shard_map/reduce_scatter | solution.py:63
  241.4 8.5 %fusion.17 = f32[5,1,128,512]{3,0,2,1:T(8,128)} fusion(f32[5,1,128,512]{3,0,2,1:T(8,128)} %scatter-add.85, f32[5,1,128,512]{3,0,2,1:T(8,128)S(1)} %broadcast_multiply_fusion.2, f32[5,1,1,512]{3,0,2,1:T(8,128)S(1)} %collective-permute-done.13, f32[5,1,1,512]{3,0,2,1:T(8,128)S(1)} %collective-permute-done.12, f32[5,1,128,511]{3,0,2,1:T(8,128)} %get-tuple-element.96, ...), kind=kOutput, calls=%fused_computation.51 | convolution fusion | flops 23592960 | bytes 7879780 | tf_op jit(solution)/shard_map/wv,wzar->vzar/dot_general | solution.py:125
  253.2 12.6 %scatter-add.88 = f32[5,1,128,512]{3,0,2,1:T(8,128)} dynamic-update-slice(f32[5,1,128,512]{3,0,2,1:T(8,128)} %fusion.17, f32[5,1,128,1]{3,0,2,1:T(8,128)S(1)} %add_select_fusion.2, s32[]{:T(128)} %constant.194.clone.1, s32[]{:T(128)} %constant.194.clone.1, s32[]{:T(128)} %constant.194.clone.1, s32[]{:T(128)} %bitcast.33) | dynamic-update-slice | bytes 5124 | tf_op jit(solution)/shard_map/scatter-add | solution.py:134
  272.9 2.8 fusion.130
  275.7 24.7 %reduce-scatter.10.cloned.1.call-done = f32[5,128]{0,1:T(8,128)} async-done(((f32[5,1024]{0,1:T(8,128)}), f32[5,128]{0,1:T(8,128)}) %reduce-scatter.10.cloned.1.call-update) | async-done | bytes 2576 | tf_op jit(solution)/shard_map/reduce_scatter | solution.py:63
  302.0 8.5 %fusion.11 = f32[5,1,128,512]{3,0,2,1:T(8,128)} fusion(f32[5,1,128,512]{3,0,2,1:T(8,128)} %scatter-add.88, f32[5,1,128,512]{3,0,2,1:T(8,128)S(1)} %broadcast_multiply_fusion.1, f32[5,1,1,512]{3,0,2,1:T(8,128)S(1)} %collective-permute-done.16, f32[5,1,1,512]{3,0,2,1:T(8,128)S(1)} %collective-permute-done.15, f32[5,1,128,511]{3,0,2,1:T(8,128)} %get-tuple-element.92, ...), kind=kOutput, calls=%fused_computation.43 | convolution fusion | flops 23592960 | bytes 7879780 | tf_op jit(solution)/shard_map/wv,wzar->vzar/dot_general | solution.py:125
  313.8 12.6 %scatter-add.91 = f32[5,1,128,512]{3,0,2,1:T(8,128)} dynamic-update-slice(f32[5,1,128,512]{3,0,2,1:T(8,128)} %fusion.11, f32[5,1,128,1]{3,0,2,1:T(8,128)S(1)} %add_select_fusion.1, s32[]{:T(128)} %constant.194.clone.1, s32[]{:T(128)} %constant.194.clone.1, s32[]{:T(128)} %constant.194.clone.1, s32[]{:T(128)} %bitcast.33) | dynamic-update-slice | bytes 5124 | tf_op jit(solution)/shard_map/scatter-add | solution.py:134
  341.1 18.1 %scatter_custom_fusion.8 = f32[3,8192]{0,1:T(8,128)} fusion(s32[3072]{0:T(1024)} %bitcast.234, f32[]{:T(128)} %constant.189.clone.1, f32[3,3072]{0,1:T(8,128)} %bitcast_multiply_fusion.4), kind=kCustom, calls=%fused_computation.108 | custom fusion | flops 9216 | bytes 1671680 | tf_op jit(solution)/shard_map/scatter-add | solution.py:147
  359.3 7.6 %reduce-scatter.12.cloned.1.call-done = f32[5,128]{0,1:T(8,128)} async-done(((f32[5,1024]{0,1:T(8,128)}), f32[5,128]{0,1:T(8,128)}) %reduce-scatter.12.cloned.1.call-update) | async-done | bytes 2576 | tf_op jit(solution)/shard_map/reduce_scatter | solution.py:63
  368.4 8.6 %fusion.5 = f32[5,1,128,512]{3,0,2,1:T(8,128)} fusion(f32[5,1,128,512]{3,0,2,1:T(8,128)} %scatter-add.91, f32[5,1,128,512]{3,0,2,1:T(8,128)S(1)} %broadcast_multiply_fusion, f32[5,1,1,512]{3,0,2,1:T(8,128)S(1)} %collective-permute-done.19, f32[5,1,1,512]{3,0,2,1:T(8,128)S(1)} %collective-permute-done.18, f32[5,1,128,511]{3,0,2,1:T(8,128)} %get-tuple-element.88, ...), kind=kOutput, calls=%fused_computation.35 | convolution fusion | flops 23592960 | bytes 7879780 | tf_op jit(solution)/shard_map/wv,wzar->vzar/dot_general | solution.py:125
  380.4 11.2 %scatter-add.94 = f32[5,1,128,512]{3,0,2,1:T(8,128)S(1)} dynamic-update-slice(f32[5,1,128,512]{3,0,2,1:T(8,128)S(1)} %copy-done.6, f32[5,1,128,1]{3,0,2,1:T(8,128)S(1)} %add_select_fusion, s32[]{:T(128)} %constant.194.clone.1, s32[]{:T(128)} %constant.194.clone.1, s32[]{:T(128)} %constant.194.clone.1, s32[]{:T(128)} %bitcast.33) | dynamic-update-slice | bytes 5124 | tf_op jit(solution)/shard_map/scatter-add | solution.py:134
  393.4 116.7 %reduce-scatter.14.cloned.1.call-done = f32[3,256]{0,1:T(8,128)} async-done(((f32[3,8192]{0,1:T(8,128)}), f32[3,256]{0,1:T(8,128)}) %reduce-scatter.14.cloned.1.call-update) | async-done | bytes 3088 | tf_op jit(solution)/shard_map/reduce_scatter | solution.py:149
  (245 shorter events, 136.8 us)
Async XLA Ops:
  7.2 171.0 %reduce-scatter.6.cloned.1.call-start = ((), (), s32[]{:S(2)}) async-start(), calls=%async_computation.5 | async-start | bytes 589824 | tf_op jit(solution)/shard_map/reduce_scatter | solution.py:63
  9.8 57.9 %collective-permute-start.4 = (f32[5,128]{0,1:T(8,128)}, f32[5,128]{0,1:T(8,128)}, u32[]{:S(2)}, u32[]{:S(2)}) collective-permute-start(f32[5,128]{0,1:T(8,128)} %bitcast.3), channel_id=1, source_target_pairs={{0,8},{8,0},{16,24},{24,16},{1,9},{9,1},{17,25},{25,17},{2,10},{10... | collective-permute-start | bytes 7688 | tf_op jit(solution)/shard_map/ppermute | solution.py:12
  15.1 74.1 %collective-permute-start.2 = (f32[6,1,1,512]{3,0,2,1:T(8,128)S(1)}, f32[6,1,1,512]{3,0,2,1:T(8,128)}, u32[]{:S(2)}, u32[]{:S(2)}) collective-permute-start(f32[6,1,1,512]{3,0,2,1:T(8,128)S(1)} %get-tuple-element.85), channel_id=1, source_target_pairs={{1,0},{2,1},{3,2},{4,3},{5,4},{6,5},{7,6},{0,7},{9,8},{10,9},{11,1... | collective-permute-start | bytes 36872 | tf_op jit(solution)/shard_map/ppermute | solution.py:23
  18.0 71.3 %collective-permute-start.3 = (f32[6,1,1,512]{3,0,2,1:T(8,128)S(1)}, f32[6,1,1,512]{3,0,2,1:T(8,128)}, u32[]{:S(2)}, u32[]{:S(2)}) collective-permute-start(f32[6,1,1,512]{3,0,2,1:T(8,128)S(1)} %get-tuple-element.86), channel_id=1, source_target_pairs={{0,1},{1,2},{2,3},{3,4},{4,5},{5,6},{6,7},{7,0},{8,9},{9,10},{10,1... | collective-permute-start | bytes 36872 | tf_op jit(solution)/shard_map/ppermute | solution.py:22
  20.9 157.8 %collective-permute-start = (f32[5,1,1,512]{3,0,2,1:T(8,128)}, f32[5,1,1,512]{3,0,2,1:T(8,128)}, u32[]{:S(2)}, u32[]{:S(2)}) collective-permute-start(f32[5,1,1,512]{3,0,2,1:T(8,128)} %get-tuple-element.111), channel_id=1, source_target_pairs={{1,0},{2,1},{3,2},{4,3},{5,4},{6,5},{7,6},{0,7},{9,8},{10,9},{11,1... | collective-permute-start | bytes 30728 | tf_op jit(solution)/shard_map/ppermute | solution.py:23
  24.4 154.3 %collective-permute-start.1 = (f32[5,1,1,512]{3,0,2,1:T(8,128)S(1)}, f32[5,1,1,512]{3,0,2,1:T(8,128)}, u32[]{:S(2)}, u32[]{:S(2)}) collective-permute-start(f32[5,1,1,512]{3,0,2,1:T(8,128)S(1)} %get-tuple-element.112), channel_id=1, source_target_pairs={{0,1},{1,2},{2,3},{3,4},{4,5},{5,6},{6,7},{7,0},{8,9},{9,10},{10,1... | collective-permute-start | bytes 30728 | tf_op jit(solution)/shard_map/ppermute | solution.py:22
  36.9 202.9 %reduce-scatter.8.cloned.1.call-start = ((), (), s32[]{:S(2)}) async-start(), calls=%async_computation.6 | async-start | bytes 589824 | tf_op jit(solution)/shard_map/reduce_scatter | solution.py:63
  104.4 24.3 %collective-permute-start.5 = (f32[5,1,1,512]{3,0,2,1:T(8,128)S(1)}, f32[5,1,1,512]{3,0,2,1:T(8,128)}, u32[]{:S(2)}, u32[]{:S(2)}) collective-permute-start(f32[5,1,1,512]{3,0,2,1:T(8,128)S(1)} %get-tuple-element.107), channel_id=1, source_target_pairs={{1,0},{2,1},{3,2},{4,3},{5,4},{6,5},{7,6},{0,7},{9,8},{10,9},{11,1... | collective-permute-start | bytes 30728 | tf_op jit(solution)/shard_map/ppermute | solution.py:23
  104.7 24.0 %collective-permute-start.6 = (f32[5,1,1,512]{3,0,2,1:T(8,128)S(1)}, f32[5,1,1,512]{3,0,2,1:T(8,128)}, u32[]{:S(2)}, u32[]{:S(2)}) collective-permute-start(f32[5,1,1,512]{3,0,2,1:T(8,128)S(1)} %get-tuple-element.108), channel_id=1, source_target_pairs={{0,1},{1,2},{2,3},{3,4},{4,5},{5,6},{6,7},{7,0},{8,9},{9,10},{10,1... | collective-permute-start | bytes 30728 | tf_op jit(solution)/shard_map/ppermute | solution.py:22
  143.8 24.4 %collective-permute-start.8 = (f32[5,1,1,512]{3,0,2,1:T(8,128)S(1)}, f32[5,1,1,512]{3,0,2,1:T(8,128)}, u32[]{:S(2)}, u32[]{:S(2)}) collective-permute-start(f32[5,1,1,512]{3,0,2,1:T(8,128)S(1)} %get-tuple-element.103), channel_id=1, source_target_pairs={{1,0},{2,1},{3,2},{4,3},{5,4},{6,5},{7,6},{0,7},{9,8},{10,9},{11,1... | collective-permute-start | bytes 30728 | tf_op jit(solution)/shard_map/ppermute | solution.py:23
  144.8 23.3 %collective-permute-start.9 = (f32[5,1,1,512]{3,0,2,1:T(8,128)S(1)}, f32[5,1,1,512]{3,0,2,1:T(8,128)}, u32[]{:S(2)}, u32[]{:S(2)}) collective-permute-start(f32[5,1,1,512]{3,0,2,1:T(8,128)S(1)} %get-tuple-element.104), channel_id=1, source_target_pairs={{0,1},{1,2},{2,3},{3,4},{4,5},{5,6},{6,7},{7,0},{8,9},{9,10},{10,1... | collective-permute-start | bytes 30728 | tf_op jit(solution)/shard_map/ppermute | solution.py:22
  178.1 9.1 %collective-permute-start.11 = (f32[5,128]{0,1:T(8,128)}, f32[5,128]{0,1:T(8,128)S(1)}, u32[]{:S(2)}, u32[]{:S(2)}) collective-permute-start(f32[5,128]{0,1:T(8,128)} %reduce-scatter.6.cloned.1.call-done), channel_id=1, source_target_pairs={{0,8},{8,0},{16,24},{24,16},{1,9},{9,1},{17,25},{25,17},{2,10},{10... | collective-permute-start | bytes 7688 | tf_op jit(solution)/shard_map/ppermute | solution.py:12
  209.5 90.9 %reduce-scatter.10.cloned.1.call-start = ((), (), s32[]{:S(2)}) async-start(), calls=%async_computation.7 | async-start | bytes 589824 | tf_op jit(solution)/shard_map/reduce_scatter | solution.py:63
  209.6 31.8 %collective-permute-start.12 = (f32[5,1,1,512]{3,0,2,1:T(8,128)S(1)}, f32[5,1,1,512]{3,0,2,1:T(8,128)S(1)}, u32[]{:S(2)}, u32[]{:S(2)}) collective-permute-start(f32[5,1,1,512]{3,0,2,1:T(8,128)S(1)} %get-tuple-element.97), channel_id=1, source_target_pairs={{1,0},{2,1},{3,2},{4,3},{5,4},{6,5},{7,6},{0,7},{9,8},{10,9},{11,1... | collective-permute-start | bytes 30728 | tf_op jit(solution)/shard_map/ppermute | solution.py:23
  211.5 29.9 %collective-permute-start.13 = (f32[5,1,1,512]{3,0,2,1:T(8,128)S(1)}, f32[5,1,1,512]{3,0,2,1:T(8,128)S(1)}, u32[]{:S(2)}, u32[]{:S(2)}) collective-permute-start(f32[5,1,1,512]{3,0,2,1:T(8,128)S(1)} %get-tuple-element.98), channel_id=1, source_target_pairs={{0,1},{1,2},{2,3},{3,4},{4,5},{5,6},{6,7},{7,0},{8,9},{9,10},{10,1... | collective-permute-start | bytes 30728 | tf_op jit(solution)/shard_map/ppermute | solution.py:22
  239.8 10.0 %collective-permute-start.14 = (f32[5,128]{0,1:T(8,128)}, f32[5,128]{0,1:T(8,128)S(1)}, u32[]{:S(2)}, u32[]{:S(2)}) collective-permute-start(f32[5,128]{0,1:T(8,128)} %reduce-scatter.8.cloned.1.call-done), channel_id=1, source_target_pairs={{0,8},{8,0},{16,24},{24,16},{1,9},{9,1},{17,25},{25,17},{2,10},{10... | collective-permute-start | bytes 7688 | tf_op jit(solution)/shard_map/ppermute | solution.py:12
  272.2 94.8 %reduce-scatter.12.cloned.1.call-start = ((), (), s32[]{:S(2)}) async-start(), calls=%async_computation.8 | async-start | bytes 589824 | tf_op jit(solution)/shard_map/reduce_scatter | solution.py:63
  272.2 29.8 %collective-permute-start.15 = (f32[5,1,1,512]{3,0,2,1:T(8,128)S(1)}, f32[5,1,1,512]{3,0,2,1:T(8,128)S(1)}, u32[]{:S(2)}, u32[]{:S(2)}) collective-permute-start(f32[5,1,1,512]{3,0,2,1:T(8,128)S(1)} %get-tuple-element.93), channel_id=1, source_target_pairs={{1,0},{2,1},{3,2},{4,3},{5,4},{6,5},{7,6},{0,7},{9,8},{10,9},{11,1... | collective-permute-start | bytes 30728 | tf_op jit(solution)/shard_map/ppermute | solution.py:23
  272.3 29.7 %collective-permute-start.16 = (f32[5,1,1,512]{3,0,2,1:T(8,128)S(1)}, f32[5,1,1,512]{3,0,2,1:T(8,128)S(1)}, u32[]{:S(2)}, u32[]{:S(2)}) collective-permute-start(f32[5,1,1,512]{3,0,2,1:T(8,128)S(1)} %get-tuple-element.94), channel_id=1, source_target_pairs={{0,1},{1,2},{2,3},{3,4},{4,5},{5,6},{6,7},{7,0},{8,9},{9,10},{10,1... | collective-permute-start | bytes 30728 | tf_op jit(solution)/shard_map/ppermute | solution.py:22
  300.5 10.0 %collective-permute-start.17 = (f32[5,128]{0,1:T(8,128)}, f32[5,128]{0,1:T(8,128)S(1)}, u32[]{:S(2)}, u32[]{:S(2)}) collective-permute-start(f32[5,128]{0,1:T(8,128)} %reduce-scatter.10.cloned.1.call-done), channel_id=1, source_target_pairs={{0,8},{8,0},{16,24},{24,16},{1,9},{9,1},{17,25},{25,17},{2,10},{10... | collective-permute-start | bytes 7688 | tf_op jit(solution)/shard_map/ppermute | solution.py:12
  338.6 171.5 %reduce-scatter.14.cloned.1.call-start = ((), (), s32[]{:S(2)}) async-start(), calls=%async_computation.9 | async-start | bytes 4325376 | tf_op jit(solution)/shard_map/reduce_scatter | solution.py:149
  338.6 29.8 %collective-permute-start.18 = (f32[5,1,1,512]{3,0,2,1:T(8,128)S(1)}, f32[5,1,1,512]{3,0,2,1:T(8,128)S(1)}, u32[]{:S(2)}, u32[]{:S(2)}) collective-permute-start(f32[5,1,1,512]{3,0,2,1:T(8,128)S(1)} %get-tuple-element.89), channel_id=1, source_target_pairs={{1,0},{2,1},{3,2},{4,3},{5,4},{6,5},{7,6},{0,7},{9,8},{10,9},{11,1... | collective-permute-start | bytes 30728 | tf_op jit(solution)/shard_map/ppermute | solution.py:23
  338.7 29.7 %collective-permute-start.19 = (f32[5,1,1,512]{3,0,2,1:T(8,128)S(1)}, f32[5,1,1,512]{3,0,2,1:T(8,128)S(1)}, u32[]{:S(2)}, u32[]{:S(2)}) collective-permute-start(f32[5,1,1,512]{3,0,2,1:T(8,128)S(1)} %get-tuple-element.90), channel_id=1, source_target_pairs={{0,1},{1,2},{2,3},{3,4},{4,5},{5,6},{6,7},{7,0},{8,9},{9,10},{10,1... | collective-permute-start | bytes 30728 | tf_op jit(solution)/shard_map/ppermute | solution.py:22
  366.9 10.1 %collective-permute-start.20 = (f32[5,128]{0,1:T(8,128)}, f32[5,128]{0,1:T(8,128)S(1)}, u32[]{:S(2)}, u32[]{:S(2)}) collective-permute-start(f32[5,128]{0,1:T(8,128)} %reduce-scatter.12.cloned.1.call-done), channel_id=1, source_target_pairs={{0,8},{8,0},{16,24},{24,16},{1,9},{9,1},{17,25},{25,17},{2,10},{10... | collective-permute-start | bytes 7688 | tf_op jit(solution)/shard_map/ppermute | solution.py:12
  (34 other events, 280.6 us)
Sparse Core Ops, SparseCore 0:
  37.0 31.2 reduce-scatter.5
  209.6 30.1 reduce-scatter.7
  272.3 28.1 reduce-scatter.9
  338.7 28.1 reduce-scatter.11
  369.0 141.0 reduce-scatter.13
where the time goes:
time: 527 us; the launch traced here: 518 us
  waiting for transfers between devices  179 us (34%)
  local copies, waits for them, and re-layouts  127 us (24%)
  other arithmetic  68.8 us (13%)
  matrix products  60.4 us (11%)
  blocking collectives  48 us (9%)
  starting transfers between devices  20.9 us (4%)
  between operations  14.7 us (3%)
    reduce_scatter x1, waiting for transfers between devices, local(): lax.psum_scatter(accumulated, ('zone', 'block'), scatter_dimension=1, til...  117 us
    reduce_scatter x4, waiting for transfers between devices, return_face(): lax.psum_scatter(collected, 'block', scatter_dimension=1, tiled=True)  57.5 us
    scatter-add x4, local copies, waits for them, and re-layouts, local(): adjoint = adjoint.at[:, 0, :, radial - 1].add(face_back)  49.1 us
    all_gather x3, blocking collectives, gather_face(): partner_face = lax.all_gather(mirrored, 'block', axis=1, tiled=True)  48 us
    dot_general x4, matrix products, local(): jnp.einsum('wv,wzar->vzar', coupling, adjoint, precision=lax.Precision.HI...  34 us
    dot_general x3, matrix products, advance(): jnp.einsum('vw,wzar->vzar', coupling, jnp.tanh(middle), precision=lax.Pre...  26.2 us
    scatter-add x1, other arithmetic, local(): accumulated = jnp.zeros((3, point_total), jnp.float32).at[:, center_ids[0...  18.1 us
    another operation x6, other arithmetic  12.6 us
  transfers between devices with their start and end apart: 26, of which 6 were waited for; matrix products, arithmetic and copies ran while one was open for 35% of the time, Pallas kernels for 0%

commit v1 on v0

v1 whole, which is shorter than its diff:
```python
import functools

import jax
import jax.numpy as jnp
from jax import lax
from jax.experimental import pallas as pl
from jax.experimental.pallas import tpu as pltpu
from jax.sharding import PartitionSpec as P

CP_DEV = 256
LANES = 128
SUB = 8
STEPS = 4
NV = 5
UCOLS = STEPS + 2
LCOLS = STEPS
HALO = SUB
ROW_K = 2 * STEPS
ROW_U = ROW_K + UCOLS
ROW_L = ROW_U + NV * UCOLS
STRIP = ROW_L + NV * LCOLS
VMEM_LIMIT = 48 * 1024 * 1024


def params(**kw):
    return pltpu.CompilerParams(vmem_limit_bytes=VMEM_LIMIT, **kw)


def pack_kernel(
    u_in, u_out, l_in, l_out, k_in, k_out, u_lo, u_hi, l_lo, l_hi, k_lo, k_hi, dmap, dweight,
    strip, wall, low, high,
):
    rows = u_in.shape[2]
    block = lax.axis_index("block")
    own = pl.ds(pl.multiple_of(block * rows, LANES), rows)
    strip[0:STEPS, :] = dmap[:, 0, own].astype(jnp.float32)
    strip[STEPS : 2 * STEPS, :] = dweight[:, 0, own]
    kt = k_out[0].T
    strip[ROW_K : ROW_K + UCOLS, :] = kt[LANES - UCOLS :]
    wall[ROW_K : ROW_K + UCOLS, :] = k_in[0].T[:UCOLS]
    wall[0:ROW_K, :] = jnp.zeros((ROW_K, rows), jnp.float32)
    for v in range(NV):
        a, b = ROW_U + v * UCOLS, ROW_L + v * LCOLS
        strip[a : a + UCOLS, :] = u_out[v, 0].T[LANES - UCOLS :]
        strip[b : b + LCOLS, :] = l_out[v, 0].T[LANES - LCOLS :]
        wall[a : a + UCOLS, :] = u_in[v, 0].T[:UCOLS]
        wall[b : b + LCOLS, :] = l_in[v, 0].T[:LCOLS]
    for ref, u, l, k in ((low, u_lo, l_lo, k_lo), (high, u_hi, l_hi, k_hi)):
        ref[0:NV] = u[:, 0]
        ref[NV : 2 * NV] = l[:, 0]
        ref[2 * NV] = k[0]


def pack(start_state, final_cotangent, diffusivity, donor_map, donor_weight):
    _, _, rows, radial = start_state.shape
    last_tile, last_rows = radial // LANES - 1, rows // HALO - 1

    def side(tile):
        return pl.BlockSpec((NV, 1, rows, LANES), lambda i: (0, 0, 0, tile))

    def kside(tile):
        return pl.BlockSpec((1, rows, LANES), lambda i: (0, 0, tile))

    def edge(index):
        return pl.BlockSpec((NV, 1, HALO, radial), lambda i: (0, 0, index, 0))

    def kedge(index):
        return pl.BlockSpec((1, HALO, radial), lambda i: (0, index, 0))

    def whole(shape):
        return pl.BlockSpec(shape, lambda i: (0,) * len(shape))

    f32 = jnp.float32
    outs = ((STRIP, rows), (STRIP, rows), (2 * NV + 1, HALO, radial), (2 * NV + 1, HALO, radial))
    u, l, k = start_state, final_cotangent, diffusivity
    return pl.pallas_call(
        pack_kernel,
        grid=(1,),
        in_specs=[
            side(0), side(last_tile), side(0), side(last_tile), kside(0), kside(last_tile),
            edge(0), edge(last_rows), edge(0), edge(last_rows), kedge(0), kedge(last_rows),
            whole(donor_map.shape), whole(donor_weight.shape),
        ],
        out_specs=[whole(s) for s in outs],
        out_shape=[jax.ShapeDtypeStruct(s, f32) for s in outs],
        compiler_params=params(),
        name="pack",
    )(u, u, l, l, k, k, u, u, l, l, k, k, donor_map, donor_weight)


def iota(shape, axis):
    return lax.broadcasted_iota(jnp.int32, shape, axis)


def left(x, by=1):
    return pltpu.roll(x, x.shape[-1] - by, x.ndim - 1)


def right(x, by=1):
    return pltpu.roll(x, by, x.ndim - 1)


def stencil(x, inner, outer):
    sub = iota(x.shape, 0)
    out = pltpu.roll(x, SUB - 1, 0)
    inn = pltpu.roll(x, 1, 0)
    if outer is not None:
        out = jnp.where(sub == SUB - 1, outer, out)
    if inner is not None:
        inn = jnp.where(sub == 0, inner, inn)
    return left(x) + right(x) + out + inn - 4.0 * x


def strip_forward(u, t, kappa, c, inner, outer):
    new = []
    for v in range(NV):
        reaction = sum(c[v, w] * t[w] for w in range(NV))
        lap = stencil(u[v], inner, None if outer is None else outer[v])
        new.append(u[v] + kappa * lap - reaction)
    return new


def strip_backward(lam, t, kappa, c, inner, outer):
    new = []
    for v in range(NV):
        pulled = sum(c[w, v] * lam[w] for w in range(NV))
        lap = stencil(kappa * lam[v], inner, None if outer is None else outer[v])
        new.append(lam[v] + lap - (1.0 - t[v] * t[v]) * pulled)
    return new


def wall_kernel(own, before, after, c, proj, area, ids, dist, out, *, count):
    rows = own.shape[1]

    def rows_of(a, b):
        return jnp.concatenate([before[a:b, :], own[a:b, :], after[a:b, :]], axis=1)

    def first(start, cols):
        piece = rows_of(start, start + cols)
        pad = jnp.zeros((SUB - cols, piece.shape[1]), jnp.float32)
        return jnp.concatenate([piece, pad], axis=0)

    kappa = first(ROW_K, UCOLS)
    u = [first(ROW_U + v * UCOLS, UCOLS) for v in range(NV)]
    lam = [first(ROW_L + v * LCOLS, LCOLS) for v in range(NV)]
    history = []
    for n in range(STEPS):
        t = [jnp.tanh(x) for x in u]
        history.append((u, t))
        if n < STEPS - 1:
            u = strip_forward(u, t, kappa, c, 0.0, None)
    h = [0.0] * NV
    for n in reversed(range(STEPS)):
        u, t = history[n]
        h = [h[v] + (lam[v] * u[v])[0:1, rows : 2 * rows] for v in range(NV)]
        if n > 0:
            lam = strip_backward(lam, t, kappa, c, 0.0, None)
    nodes = area.shape[1]
    per_row = nodes // rows
    s_rows = [sum(proj[i, v] * h[v] for v in range(NV)) for i in range(3)]
    s_rows = jnp.concatenate(s_rows + [jnp.zeros((SUB - 3, rows), jnp.float32)], axis=0)
    spread = (iota((rows, nodes), 1) // per_row == iota((rows, nodes), 0)).astype(jnp.float32)
    s = jnp.dot(s_rows, spread, precision=lax.Precision.HIGHEST, preferred_element_type=jnp.float32)
    s = s * area[...]
    d = dist[0]
    q = 1.0 - d
    q = q * q
    phi = q * q * (4.0 * d + 1.0)
    key = ids[0]
    major, minor = key // LANES, key % LANES
    groups = count // LANES
    total = jnp.zeros((3 * groups, LANES), jnp.float32)
    bf = jnp.bfloat16
    for k in range(d.shape[0]):
        lo = (iota((LANES, nodes), 0) == minor[k : k + 1]).astype(bf)
        hit = iota((groups, nodes), 0) == major[k : k + 1]
        w = s[0:3] * phi[k : k + 1]
        for piece in range(3):
            part = w.astype(bf).astype(jnp.float32)
            w = w - part
            a = jnp.concatenate([jnp.where(hit, part[i : i + 1], 0.0) for i in range(3)], axis=0)
            total += lax.dot_general(
                a.astype(bf), lo, (((1,), (1,)), ((), ())), preferred_element_type=jnp.float32
            )
    out[...] = total


def wall_gradient(own, before, after, coupling, proj, area, ids, dist, count):
    vm = pl.BlockSpec(memory_space=pltpu.VMEM)
    sm = pl.BlockSpec(memory_space=pltpu.SMEM)
    return pl.pallas_call(
        functools.partial(wall_kernel, count=count),
        in_specs=[vm, vm, vm, sm, sm, vm, vm, vm],
        out_specs=vm,
        out_shape=jax.ShapeDtypeStruct((3 * count // LANES, LANES), jnp.float32),
        compiler_params=params(),
        name="wall_gradient",
    )(own, before, after, coupling, proj, area, ids, dist)


def face_kernel(pieces, c, out, face, flip, *, rows):
    block = lax.axis_index("block")
    blocks = pieces.shape[0] // 2
    half = blocks // 2
    total = blocks * rows

    def piece(q, a, b):
        parts = []
        for j in range(blocks):
            rel = block ^ j
            slot = (rel & 1) * blocks + q * half + (rel >> 1)
            parts.append(pieces[slot, a:b, :])
        return jnp.concatenate(parts, axis=1)

    def last(q, end):
        return piece(q, end - SUB, end)

    lane = iota((SUB, total), 1).astype(jnp.float32)
    sub = iota((SUB, total), 0)
    size = float(total)
    shift, taps = [], []
    for q in range(2):
        donors = piece(q, 0, SUB)
        share = jnp.concatenate([donors[STEPS:], donors[STEPS:]], axis=0)
        delta = donors - lane
        delta = jnp.where(delta < 0.0, delta + size, delta)
        rel = delta - delta[:, 0:1] + float(STEPS)
        rel = jnp.where(rel < 0.0, rel + size, rel)
        rel = jnp.where(rel >= size, rel - size, rel)
        least = jnp.min(rel, axis=1, keepdims=True)
        e = rel - least
        t = delta[:, 0:1] - float(STEPS) + least
        t = jnp.where(t < 0.0, t + size, t)
        t = jnp.where(t >= size, t - size, t).astype(jnp.int32)
        shift.append([t[n, 0] for n in range(STEPS)])
        coefs = [
            jnp.where(e == float(i), share, 0.0) + jnp.where(e == float(i - 1), 1.0 - share, 0.0)
            for i in range(6)
        ]
        taps.append([[coefs[i][n : n + 1] for i in range(6)] for n in range(STEPS)])

    kappa = [last(q, ROW_K + UCOLS) for q in range(2)]
    u = [[last(q, ROW_U + (v + 1) * UCOLS) for v in range(NV)] for q in range(2)]
    lam = [[last(q, ROW_L + (v + 1) * LCOLS) for v in range(NV)] for q in range(2)]
    face[...] = jnp.zeros_like(face)

    def gather_faces(q, x):
        for v in range(NV):
            face[q, v : v + 1, :] = x[v][SUB - 1 : SUB, :]
        return face[q]

    def ghost(q, n, f):
        f = pltpu.roll(f, (total - shift[q][n]) % total, 1)
        acc = taps[q][n][0] * f
        for i in range(1, 6):
            f = left(f)
            acc = acc + taps[q][n][i] * f
        return acc

    def back(q, n, f):
        acc = taps[q][n][5] * f
        for i in reversed(range(5)):
            acc = right(acc) + taps[q][n][i] * f
        return pltpu.roll(acc, shift[q][n], 1)

    def rows_apart(g):
        return [jnp.broadcast_to(g[v : v + 1], (SUB, total)) for v in range(NV)]

    offset = (total + HALO - block * rows) % total
    width = 2 * LANES

    def emit(index, g):
        g = pltpu.roll(g, offset, 1)
        flip[index * SUB : (index + 1) * SUB, :] = g[:, :width]

    flip[...] = jnp.zeros_like(flip)
    history = []
    for n in range(STEPS):
        t = [[jnp.tanh(x) for x in u[q]] for q in range(2)]
        history.append(t)
        if n < STEPS - 1:
            faces = [gather_faces(q, u[q]) for q in range(2)]
            g = [ghost(q, n, faces[1 - q]) for q in range(2)]
            emit(n, g[0])
            u = [
                strip_forward(u[q], t[q], kappa[q], c, None, rows_apart(g[q])) for q in range(2)
            ]
    for n in reversed(range(STEPS)):
        t = history[n]
        faces = [gather_faces(q, [kappa[q] * x for x in lam[q]]) for q in range(2)]
        g = [back(1 - q, n, faces[1 - q]) if n > 0 or q == 0 else None for q in range(2)]
        emit(STEPS - 1 + n, g[0])
        if n > 0:
            lam = [
                strip_backward(lam[q], t[q], kappa[q], c, None, rows_apart(g[q]))
                for q in range(2)
            ]
    for j in range(2):
        out[j * LANES : (j + 1) * LANES, :] = flip[:, j * LANES : (j + 1) * LANES].T


def face_terms(pieces, coupling, rows):
    vm = pl.BlockSpec(memory_space=pltpu.VMEM)
    sm = pl.BlockSpec(memory_space=pltpu.SMEM)
    total = pieces.shape[0] // 2 * rows
    return pl.pallas_call(
        functools.partial(face_kernel, rows=rows),
        in_specs=[vm, sm],
        out_specs=vm,
        out_shape=jax.ShapeDtypeStruct((2 * LANES, LANES), jnp.float32),
        scratch_shapes=[
            pltpu.VMEM((2, SUB, total), jnp.float32),
            pltpu.VMEM((LANES, 2 * LANES), jnp.float32),
        ],
        compiler_params=params(),
        name="face_terms",
    )(pieces, coupling)


def field_kernel(
    u_hbm, l_hbm, k_hbm, before, after, terms, c, out,
    ext_u, ext_l, ext_k, kap, states, tanhs, lam, scaled, sems,
):
    rows, radial = u_hbm.shape[2], u_hbm.shape[3]
    chunks = kap.shape[0]
    tiles = radial // LANES
    own = pl.ds(HALO, rows)

    def cut(j):
        return slice(j * LANES, (j + 1) * LANES)

    copies = []
    for j in range(tiles):
        lanes = pl.ds(j * LANES, LANES)
        copies += [
            pltpu.make_async_copy(u_hbm.at[:, 0, :, lanes], ext_u.at[:, j, own], sems.at[0, j]),
            pltpu.make_async_copy(l_hbm.at[:, 0, :, lanes], ext_l.at[:, j, own], sems.at[1, j]),
            pltpu.make_async_copy(k_hbm.at[0, :, lanes], ext_k.at[j, own], sems.at[2, j]),
        ]
    for copy in copies:
        copy.start()
    for ref, at in ((before, 0), (after, HALO + rows)):
        for j in range(tiles):
            ext_u[:, j, at : at + HALO] = ref[0:NV, :, cut(j)]
            ext_l[:, j, at : at + HALO] = ref[NV : 2 * NV, :, cut(j)]
            ext_k[j, at : at + HALO] = ref[2 * NV, :, cut(j)]
    for copy in copies:
        copy.wait()

    def load(i, carry):
        at = pl.ds(i, SUB, stride=chunks)
        for j in range(tiles):
            kappa = ext_k[j, at, :]
            kap[i, :, cut(j)] = kappa
            for v in range(NV):
                states[0, v, i + 1, :, cut(j)] = ext_u[v, j, at, :]
                x = ext_l[v, j, at, :]
                lam[v, i, :, cut(j)] = x
                scaled[0, v, i + 1, :, cut(j)] = kappa * x
        return carry

    lax.fori_loop(0, chunks, load, 0)

    def wrap(ref):
        for v in range(NV):
            ref[v, 0] = pltpu.roll(ref[v, chunks], 1, 0)
            ref[v, chunks + 1] = pltpu.roll(ref[v, 1], SUB - 1, 0)

    wrap(states.at[0])
    wrap(scaled.at[0])
    lane = iota((SUB, LANES), 1)
    is_first, is_last = lane == 0, lane == LANES - 1

    def neighbours(ref, v, i, j, edge, cache):
        def tile(b):
            if (v, b) not in cache:
                x = ref[v, i + 1, :, cut(b)]
                cache[v, b] = (x, pltpu.roll(x, 1, 1), pltpu.roll(x, LANES - 1, 1))
            return cache[v, b]

        x, r, l = tile(j)
        inn = jnp.where(is_first, tile(j - 1)[1] if j > 0 else 0.0, r)
        outv = jnp.where(is_last, tile(j + 1)[2] if j < tiles - 1 else edge, l)
        return ref[v, i, :, cut(j)] + ref[v, i + 2, :, cut(j)] + inn + outv, x

    def edges(i, n):
        e = terms[pl.ds(i, SUB, stride=chunks), :]
        return [pltpu.roll(e, (2 * LANES - 1 - (n * SUB + v)) % LANES, 1) for v in range(NV)]

    def forward(n):
        def body(i, carry):
            edge = edges(i, n)
            cache = {}
            for j in range(tiles):
                kappa = kap[i, :, cut(j)]
                pairs = [neighbours(states.at[n], v, i, j, edge[v], cache) for v in range(NV)]
                t = [jnp.tanh(x) for _, x in pairs]
                for v in range(NV):
                    around, x = pairs[v]
                    tanhs[n, v, i, :, cut(j)] = t[v]
                    reaction = sum(c[v, w] * t[w] for w in range(NV))
                    states[n + 1, v, i + 1, :, cut(j)] = (
                        x + kappa * (around - 4.0 * x) - reaction
                    )
            return carry

        lax.fori_loop(0, chunks, body, 0)
        if n + 1 < STEPS - 1:
            wrap(states.at[n + 1])

    def backward(n, source, target):
        def body(i, carry):
            edge = edges(i, STEPS - 1 + n)
            cache = {}
            for j in range(tiles):
                kappa = kap[i, :, cut(j)]
                pairs = [neighbours(scaled.at[source], v, i, j, edge[v], cache) for v in range(NV)]
                x = [lam[v, i, :, cut(j)] for v in range(NV)]
                for v in range(NV):
                    if n < STEPS - 1:
                        t = tanhs[n, v, i, :, cut(j)]
                    else:
                        t = jnp.tanh(states[n, v, i + 1, :, cut(j)])
                    around, s = pairs[v]
                    pulled = sum(c[w, v] * x[w] for w in range(NV))
                    new = x[v] + (around - 4.0 * s) - (1.0 - t * t) * pulled
                    if n > 0:
                        lam[v, i, :, cut(j)] = new
                        scaled[target, v, i + 1, :, cut(j)] = kappa * new
                    else:
                        ext_l[v, j, pl.ds(i, SUB, stride=chunks), :] = new
            return carry

        lax.fori_loop(0, chunks, body, 0)
        if n > 0:
            wrap(scaled.at[target])

    for n in range(STEPS - 1):
        forward(n)
    source = 0
    for n in reversed(range(STEPS)):
        backward(n, source, 1 - source)
        source = 1 - source
    copies = [
        pltpu.make_async_copy(
            ext_l.at[:, j, own], out.at[:, 0, :, pl.ds(j * LANES, LANES)], sems.at[3, j]
        )
        for j in range(tiles)
    ]
    for copy in copies:
        copy.start()
    for copy in copies:
        copy.wait()


def field(start_state, final_cotangent, diffusivity, before, after, terms, coupling):
    _, _, rows, radial = start_state.shape
    ext = rows + 2 * HALO
    chunks, tiles = ext // SUB, radial // LANES
    vm = pl.BlockSpec(memory_space=pltpu.VMEM)
    hbm = pl.BlockSpec(memory_space=pl.ANY)
    f32 = jnp.float32
    return pl.pallas_call(
        field_kernel,
        in_specs=[hbm, hbm, hbm, vm, vm, vm, pl.BlockSpec(memory_space=pltpu.SMEM)],
        out_specs=hbm,
        out_shape=jax.ShapeDtypeStruct(start_state.shape, f32),
        scratch_shapes=[
            pltpu.VMEM((NV, tiles, ext, LANES), f32),
            pltpu.VMEM((NV, tiles, ext, LANES), f32),
            pltpu.VMEM((tiles, ext, LANES), f32),
            pltpu.VMEM((chunks, SUB, radial), f32),
            pltpu.VMEM((STEPS, NV, chunks + 2, SUB, radial), f32),
            pltpu.VMEM((STEPS - 1, NV, chunks, SUB, radial), f32),
            pltpu.VMEM((NV, chunks, SUB, radial), f32),
            pltpu.VMEM((2, NV, chunks + 2, SUB, radial), f32),
            pltpu.SemaphoreType.DMA((4, tiles)),
        ],
        compiler_params=params(),
        name="field",
    )(start_state, final_cotangent, diffusivity, before, after, terms, coupling)


def ring(x, step):
    size = lax.axis_size("block")
    return lax.ppermute(x, "block", [(i, (i + step) % size) for i in range(size)])


def crossed(x, mask):
    return lax.ppermute(x, "block", [(i, i ^ mask) for i in range(lax.axis_size("block"))])


def swapped(x):
    return lax.ppermute(x, "zone", [(i, i ^ 1) for i in range(lax.axis_size("zone"))])


def gather_pair(strip):
    x = strip[None]
    bit, size = 1, lax.axis_size("block")
    while 2**bit < size:
        wide = 4 if 2 ** (bit + 1) < size else 2
        x = jnp.concatenate([x] + [crossed(x, k << bit) for k in range(1, wide)], axis=0)
        bit += 2 if wide == 4 else 1
    x = jnp.concatenate([x, swapped(x)], axis=0)
    return jnp.concatenate([x, crossed(x, 1)], axis=0)


def local(
    start_state,
    diffusivity,
    donor_map,
    donor_weight,
    coupling,
    final_cotangent,
    wall_area,
    wall_projection,
    center_ids,
    center_dist,
):
    rows = start_state.shape[2]
    devices = lax.axis_size("zone") * lax.axis_size("block")
    strip, wall, low, high = pack(
        start_state, final_cotangent, diffusivity, donor_map, donor_weight
    )
    wall_before, wall_after = ring(wall, 1), ring(wall, -1)
    before, after = ring(high, 1), ring(low, -1)
    pieces = gather_pair(strip)
    points = wall_gradient(
        wall, wall_before, wall_after, coupling, wall_projection, wall_area, center_ids,
        center_dist, CP_DEV * devices,
    )
    groups = CP_DEV // LANES
    points = points.reshape(3, devices, groups, LANES).transpose(1, 0, 2, 3)
    points = lax.all_to_all(points, ("zone", "block"), 0, 0, tiled=True)
    gradient = points.sum(axis=0).reshape(3, CP_DEV)
    terms = face_terms(pieces, coupling, rows)
    adjoint = field(start_state, final_cotangent, diffusivity, before, after, terms, coupling)
    return adjoint, gradient


def solution(mesh):
    return jax.shard_map(
        local,
        mesh=mesh,
        in_specs=(
            P(None, "zone", "block", None),
            P("zone", "block", None),
            P(None, "zone", None),
            P(None, "zone", None),
            P(),
            P(None, "zone", "block", None),
            P("zone", "block"),
            P(),
            P("zone", None, "block"),
            P("zone", None, "block"),
        ),
        out_specs=(P(None, "zone", "block", None), P(None, ("zone", "block"))),
        check_vma=False,
    )
```

time: 527 us -> 71.9 us (0.14); the launches traced: 518 us -> 71.3 us
  waiting for transfers between devices: 179 us -> 12.6 us
  local copies, waits for them, and re-layouts: 127 us -> 10.4 us
  other arithmetic: 68.8 us -> 0.06 us
  matrix products: 60.4 us -> 0 us
  blocking collectives: 48 us -> 0 us
  Pallas kernels: 0 us -> 27.3 us
  between operations: 14.7 us -> 0.78 us
    reduce_scatter x5 -> x0, waiting for transfers between devices: 174 us -> none  [the longest x1 117 us: local(): lax.psum_scatter(accumulated, ('zone', 'block'), scatter_dimension=1, til...]
    dot_general x8 -> x0, matrix products: 60.4 us -> none  [the longest x4 34 us: local(): jnp.einsum('wv,wzar->vzar', coupling, adjoint, precision=lax.Precision.HI...]
    scatter-add x4 -> x0, local copies, waits for them, and re-layouts: 49.1 us -> none  [local(): adjoint = adjoint.at[:, 0, :, radial - 1].add(face_back)]
    all_gather x3 -> x0, blocking collectives: 48 us -> none  [gather_face(): partner_face = lax.all_gather(mirrored, 'block', axis=1, tiled=True)]
    scatter-add x9 -> x0, other arithmetic: 31.5 us -> none  [the longest x1 18.1 us: local(): accumulated = jnp.zeros((3, point_total), jnp.float32).at[:, center_ids[0...]
    slice x26 -> x0, local copies, waits for them, and re-layouts: 30.2 us -> none  [the longest x4 11.2 us: local(): scaled[..., 1:]]
    pallas_call x0 -> x4, Pallas kernels: none -> 27.3 us  [the longest x1 19.3 us: field(): pl.pallas_call(field_kernel, in_specs=[hbm, hbm, hbm, vm, vm, vm, pl.Bloc...]
    gather x26 -> x0, local copies, waits for them, and re-layouts: 24.5 us -> none  [the longest x6 5.55 us: advance(): jnp.take(partner_face, second_donor, axis=1)]
  transfers between devices with their start and end apart: 26 -> 10, of which waited for: 6 -> 5; matrix products, arithmetic and copies ran while one was open for 35% -> 7% of each run, Pallas kernels for 0% -> 11%
where the time goes in v1:
time: 71.9 us; the launch traced here: 71.3 us
  Pallas kernels  27.3 us (38%)
  starting transfers between devices  20.2 us (28%)
  waiting for transfers between devices  12.6 us (18%)
  local copies, waits for them, and re-layouts  10.4 us (14%)
  between operations  0.78 us (1%)
    pallas_call x1, Pallas kernels, field(): pl.pallas_call(field_kernel, in_specs=[hbm, hbm, hbm, vm, vm, vm, pl.Bloc...  19.3 us
    unnamed x35, local copies, waits for them, and re-layouts  8.12 us
    ppermute x4, starting transfers between devices, ring(): lax.ppermute(x, 'block', [(i, (i + step) % size) for i in range(size)])  7.14 us
    all_to_all x1, starting transfers between devices, local(): points = lax.all_to_all(points, ('zone', 'block'), 0, 0, tiled=True)  5.78 us
    ppermute x4, starting transfers between devices, crossed(): lax.ppermute(x, 'block', [(i, i ^ mask) for i in range(lax.axis_size('blo...  5.68 us
    pallas_call x1, Pallas kernels, face_terms(): pl.pallas_call(functools.partial(face_kernel, rows=rows), in_specs=[vm, s...  5.21 us
    ppermute x4, waiting for transfers between devices, crossed(): lax.ppermute(x, 'block', [(i, i ^ mask) for i in range(lax.axis_size('blo...  5.09 us
    all_to_all x1, waiting for transfers between devices, local(): points = lax.all_to_all(points, ('zone', 'block'), 0, 0, tiled=True)  4.3 us
  transfers between devices with their start and end apart: 10, of which 5 were waited for; matrix products, arithmetic and copies ran while one was open for 7% of the time, Pallas kernels for 11%

profile of v1, /device:TPU:0, one launch (start us, length us, event | category | flops | bytes accessed | tf_op | source)
XLA Modules:
  0.0 71.3 jit_solution(6508664188684321693)
XLA Ops:
  0.6 1.3 %copy-done = f32[5,1,128,512]{3,2,1,0:T(8,128)S(1)} copy-done((f32[5,1,128,512]{3,2,1,0:T(8,128)S(1)}, f32[5,1,128,512]{3,2,1,0:T(8,128)}, u32[]{:S(2)}) %copy-start) | copy-done | bytes 1310744
  2.0 1.3 %copy-done.2 = f32[5,1,128,512]{3,2,1,0:T(8,128)S(1)} copy-done((f32[5,1,128,512]{3,2,1,0:T(8,128)S(1)}, f32[5,1,128,512]{3,2,1,0:T(8,128)}, u32[]{:S(2)}) %copy-start.2) | copy-done | bytes 1310744
  3.3 0.9 %copy-done.4 = f32[1,128,512]{2,1,0:T(8,128)S(1)} copy-done((f32[1,128,512]{2,1,0:T(8,128)S(1)}, f32[1,128,512]{2,1,0:T(8,128)}, u32[]{:S(2)}) %copy-start.4) | copy-done | bytes 262168
  4.2 0.7 %copy-done.7 = s32[4,1,1024]{2,1,0:T(1,128)S(1)} copy-done((s32[4,1,1024]{2,1,0:T(1,128)S(1)}, s32[4,1,1024]{2,1,0:T(1,128)}, u32[]{:S(2)}) %copy-start.7) | copy-done | bytes 16408
  4.9 0.7 %copy-done.8 = f32[4,1,1024]{2,1,0:T(1,128)S(1)} copy-done((f32[4,1,1024]{2,1,0:T(1,128)S(1)}, f32[4,1,1024]{2,1,0:T(1,128)}, u32[]{:S(2)}) %copy-start.8) | copy-done | bytes 16408
  6.1 3.1 %collective-permute-start.2 = (f32[1,64,128]{2,1,0:T(8,128)S(1)}, f32[1,64,128]{2,1,0:T(8,128)S(1)}, u32[]{:S(2)}, u32[]{:S(2)}) collective-permute-start(f32[1,64,128]{2,1,0:T(8,128)S(1)} %bitcast.12), channel_id=1, source_target_pairs={{0,2},{1,3},{2,0},{3,1},{4,6},{5,7},{6,4},{7,5},{8,10},{9,11},{10,... | collective-permute-start | bytes 98312 | tf_op jit(solution)/shard_map/ppermute | solution.py:490
  9.2 2.6 %collective-permute-start.3 = (f32[1,64,128]{2,1,0:T(8,128)S(1)}, f32[1,64,128]{2,1,0:T(8,128)S(1)}, u32[]{:S(2)}, u32[]{:S(2)}) collective-permute-start(f32[1,64,128]{2,1,0:T(8,128)S(1)} %bitcast.13), channel_id=1, source_target_pairs={{0,4},{1,5},{2,6},{3,7},{4,0},{5,1},{6,2},{7,3},{8,12},{9,13},{10,... | collective-permute-start | bytes 98312 | tf_op jit(solution)/shard_map/ppermute | solution.py:490
  11.8 0.6 constant_dynamic-update-slice_fusion.4
  12.4 2.2 %collective-permute-done.3 = f32[1,64,128]{2,1,0:T(8,128)S(1)} collective-permute-done((f32[1,64,128]{2,1,0:T(8,128)S(1)}, f32[1,64,128]{2,1,0:T(8,128)S(1)}, u32[]{:S(2)}, u32[]{:S(2)}) %collective-permute-start.3) | collective-permute-done | bytes 32800 | tf_op jit(solution)/shard_map/ppermute | solution.py:490
  14.6 2.9 %collective-permute-done.4 = f32[1,64,128]{2,1,0:T(8,128)S(1)} collective-permute-done((f32[1,64,128]{2,1,0:T(8,128)S(1)}, f32[1,64,128]{2,1,0:T(8,128)S(1)}, u32[]{:S(2)}, u32[]{:S(2)}) %collective-permute-start.4) | collective-permute-done | bytes 32800 | tf_op jit(solution)/shard_map/ppermute | solution.py:490
  17.5 1.6 %collective-permute-start.5 = (f32[4,64,128]{2,1,0:T(8,128)S(1)}, f32[4,64,128]{2,1,0:T(8,128)S(1)}, u32[]{:S(2)}, u32[]{:S(2)}) collective-permute-start(f32[4,64,128]{2,1,0:T(8,128)S(1)} %pad_maximum_fusion), channel_id=1, source_target_pairs={{0,8},{8,0},{16,24},{24,16},{1,9},{9,1},{17,25},{25,17},{2,10},{10... | collective-permute-start | bytes 393224 | tf_op jit(solution)/shard_map/ppermute | solution.py:494
  20.3 0.6 constant_dynamic-update-slice_fusion.1
  20.9 1.6 %collective-permute-done.5 = f32[4,64,128]{2,1,0:T(8,128)S(1)} collective-permute-done((f32[4,64,128]{2,1,0:T(8,128)S(1)}, f32[4,64,128]{2,1,0:T(8,128)S(1)}, u32[]{:S(2)}, u32[]{:S(2)}) %collective-permute-start.5) | collective-permute-done | bytes 131104 | tf_op jit(solution)/shard_map/ppermute | solution.py:494
  22.5 0.7 constant_dynamic-update-slice_fusion
  23.7 3.0 %collective-permute-start.8 = (f32[64,128]{1,0:T(8,128)S(1)}, f32[64,128]{1,0:T(8,128)S(1)}, u32[]{:S(2)}, u32[]{:S(2)}) collective-permute-start(f32[64,128]{1,0:T(8,128)S(1)} %get-tuple-element.9.own), channel_id=1, source_target_pairs={{0,7},{1,0},{2,1},{3,2},{4,3},{5,4},{6,5},{7,6},{8,15},{9,8},{10,9... | collective-permute-start | bytes 98312 | tf_op jit(solution)/shard_map/ppermute | solution.py:486
  26.7 1.6 %collective-permute-done.7.before = f32[64,128]{1,0:T(8,128)S(1)} collective-permute-done((f32[64,128]{1,0:T(8,128)S(1)}, f32[64,128]{1,0:T(8,128)S(1)}, u32[]{:S(2)}, u32[]{:S(2)}) %collective-permute-start.7) | collective-permute-done | bytes 32800 | tf_op jit(solution)/shard_map/ppermute | solution.py:486
  28.4 2.4 %wall_gradient.1 = f32[192,128]{1,0:T(8,128)S(1)} custom-call(f32[64,128]{1,0:T(8,128)S(1)} %get-tuple-element.9.own, f32[64,128]{1,0:T(8,128)S(1)} %collective-permute-done.7.before, f32[64,128]{1,0:T(8,128)S(1)} %collective-permute-done.8.after, f32[5,5]{1,0:T(8,128)S(1)} %copy-done.6, f32[3,5]{1,0:T(4,128)S(1)} %copy-done.11, f32[1,384]{1,0:T(1,128)S(1)} %copy-done.12, ...), custom_call_target="tpu_custom_call" | custom-call | tf_op jit(solution)/shard_map/wall_gradient/pallas_call | solution.py:191
  30.8 0.7 copy.16
  31.5 5.8 %all-to-all-start = ((f32[32,3,2,128]{3,2,1,0:T(2,128)}), f32[32,3,2,128]{3,2,1,0:T(2,128)S(1)}, u32[]{:S(2)}, u32[]{:S(2)}) async-start(f32[32,3,2,128]{3,2,1,0:T(2,128)} %bitcast.16), calls=%async_computation | async-start | bytes 196608 | tf_op jit(solution)/shard_map/all_to_all | solution.py:534
  37.6 3.3 %collective-permute-start.1 = (f32[11,8,512]{2,1,0:T(8,128)}, f32[11,8,512]{2,1,0:T(8,128)}, u32[]{:S(2)}, u32[]{:S(2)}) collective-permute-start(f32[11,8,512]{2,1,0:T(8,128)} %copy-done.13), channel_id=1, source_target_pairs={{0,7},{1,0},{2,1},{3,2},{4,3},{5,4},{6,5},{7,6},{8,15},{9,8},{10,9... | collective-permute-start | bytes 540680 | tf_op jit(solution)/shard_map/ppermute | solution.py:486
  40.9 4.3 %all-to-all-done = f32[32,3,2,128]{3,2,1,0:T(2,128)S(1)} async-done(((f32[32,3,2,128]{3,2,1,0:T(2,128)}), f32[32,3,2,128]{3,2,1,0:T(2,128)S(1)}, u32[]{:S(2)}, u32[]{:S(2)}) %all-to-all-start) | async-done | bytes 98336 | tf_op jit(solution)/shard_map/all_to_all | solution.py:534
  45.8 1.0 %constant_dynamic-update-slice_fusion.5.pieces = f32[16,64,128]{2,1,0:T(8,128)S(1)} fusion(f32[16,64,128]{2,1,0:T(8,128)S(1)} %get-tuple-element.11, f32[8,64,128]{2,1,0:T(8,128)} %collective-permute-done.6), kind=kLoop, calls=%fused_computation.7 | loop fusion | bytes 524288 | tf_op jit(solution)/shard_map/concatenate | solution.py:505
  46.8 5.2 %face_terms.1.terms = f32[256,128]{1,0:T(8,128)S(1)} custom-call(f32[16,64,128]{2,1,0:T(8,128)S(1)} %constant_dynamic-update-slice_fusion.5.pieces, f32[5,5]{1,0:T(8,128)S(1)} %copy-done.6), custom_call_target="tpu_custom_call" | custom-call | tf_op jit(solution)/shard_map/face_terms/pallas_call | solution.py:306
  52.1 19.3 %field.1 = f32[5,1,128,512]{3,2,1,0:T(8,128)} custom-call(f32[5,1,128,512]{3,2,1,0:T(8,128)S(1)} %copy-done.1, f32[5,1,128,512]{3,2,1,0:T(8,128)S(1)} %copy-done.3, f32[1,128,512]{2,1,0:T(8,128)S(1)} %copy-done.5, f32[11,8,512]{2,1,0:T(8,128)} %collective-permute-done.before, f32[11,8,512]{2,1,0:T(8,128)} %collective-permute-done.1.after, ...), custom_call_target="tpu_custom_call" | custom-call | tf_op jit(solution)/shard_map/field/pallas_call | solution.py:463
  (40 shorter events, 3.2 us)
Async XLA Ops:
  0.6 1.3 %copy-start = (f32[5,1,128,512]{3,2,1,0:T(8,128)S(1)}, f32[5,1,128,512]{3,2,1,0:T(8,128)}, u32[]{:S(2)}) copy-start(f32[5,1,128,512]{3,2,1,0:T(8,128)} %u_hbm.1) | copy-start | bytes 3932164
  2.0 1.3 %copy-start.2 = (f32[5,1,128,512]{3,2,1,0:T(8,128)S(1)}, f32[5,1,128,512]{3,2,1,0:T(8,128)}, u32[]{:S(2)}) copy-start(f32[5,1,128,512]{3,2,1,0:T(8,128)} %l_hbm.1) | copy-start | bytes 3932164
  3.3 0.9 %copy-start.4 = (f32[1,128,512]{2,1,0:T(8,128)S(1)}, f32[1,128,512]{2,1,0:T(8,128)}, u32[]{:S(2)}) copy-start(f32[1,128,512]{2,1,0:T(8,128)} %k_hbm.1) | copy-start | bytes 786436
  4.2 0.7 %copy-start.7 = (s32[4,1,1024]{2,1,0:T(1,128)S(1)}, s32[4,1,1024]{2,1,0:T(1,128)}, u32[]{:S(2)}) copy-start(s32[4,1,1024]{2,1,0:T(1,128)} %dmap.1) | copy-start | bytes 49156
  5.7 22.7 %copy-start.6 = (f32[5,5]{1,0:T(8,128)S(1)}, f32[5,5]{1,0:T(8,128)}, u32[]{:S(2)}) copy-start(f32[5,5]{1,0:T(8,128)} %c.5) | copy-start | bytes 304
  5.7 22.7 %copy-start.9 = (s32[1,8,384]{2,1,0:T(8,128)S(1)}, s32[1,8,384]{2,1,0:T(8,128)}, u32[]{:S(2)}) copy-start(s32[1,8,384]{2,1,0:T(8,128)} %ids.1) | copy-start | bytes 36868
  5.7 22.7 %copy-start.10 = (f32[1,8,384]{2,1,0:T(8,128)S(1)}, f32[1,8,384]{2,1,0:T(8,128)}, u32[]{:S(2)}) copy-start(f32[1,8,384]{2,1,0:T(8,128)} %dist.1) | copy-start | bytes 36868
  5.7 22.7 %copy-start.11 = (f32[3,5]{1,0:T(4,128)S(1)}, f32[3,5]{1,0:T(4,128)}, u32[]{:S(2)}) copy-start(f32[3,5]{1,0:T(4,128)} %proj.1) | copy-start | bytes 184
  5.7 22.7 %copy-start.12 = (f32[1,384]{1,0:T(1,128)S(1)}, f32[1,384]{1,0:T(1,128)}, u32[]{:S(2)}) copy-start(f32[1,384]{1,0:T(1,128)} %area.1) | copy-start | bytes 4612
  6.1 25.4 %copy-start.13 = (f32[11,8,512]{2,1,0:T(8,128)}, f32[11,8,512]{2,1,0:T(8,128)S(1)}, u32[]{:S(2)}) copy-start(f32[11,8,512]{2,1,0:T(8,128)S(1)} %get-tuple-element.7) | copy-start | bytes 540676
  6.1 25.4 %copy-start.14 = (f32[11,8,512]{2,1,0:T(8,128)}, f32[11,8,512]{2,1,0:T(8,128)S(1)}, u32[]{:S(2)}) copy-start(f32[11,8,512]{2,1,0:T(8,128)S(1)} %get-tuple-element.6) | copy-start | bytes 540676
  6.1 6.3 %collective-permute-start.2 = (f32[1,64,128]{2,1,0:T(8,128)S(1)}, f32[1,64,128]{2,1,0:T(8,128)S(1)}, u32[]{:S(2)}, u32[]{:S(2)}) collective-permute-start(f32[1,64,128]{2,1,0:T(8,128)S(1)} %bitcast.12), channel_id=1, source_target_pairs={{0,2},{1,3},{2,0},{3,1},{4,6},{5,7},{6,4},{7,5},{8,10},{9,11},{10,... | collective-permute-start | bytes 98312 | tf_op jit(solution)/shard_map/ppermute | solution.py:490
  9.2 5.4 %collective-permute-start.3 = (f32[1,64,128]{2,1,0:T(8,128)S(1)}, f32[1,64,128]{2,1,0:T(8,128)S(1)}, u32[]{:S(2)}, u32[]{:S(2)}) collective-permute-start(f32[1,64,128]{2,1,0:T(8,128)S(1)} %bitcast.13), channel_id=1, source_target_pairs={{0,4},{1,5},{2,6},{3,7},{4,0},{5,1},{6,2},{7,3},{8,12},{9,13},{10,... | collective-permute-start | bytes 98312 | tf_op jit(solution)/shard_map/ppermute | solution.py:490
  11.8 5.7 %collective-permute-start.4 = (f32[1,64,128]{2,1,0:T(8,128)S(1)}, f32[1,64,128]{2,1,0:T(8,128)S(1)}, u32[]{:S(2)}, u32[]{:S(2)}) collective-permute-start(f32[1,64,128]{2,1,0:T(8,128)S(1)} %bitcast.14), channel_id=1, source_target_pairs={{0,6},{1,7},{2,4},{3,5},{4,2},{5,3},{6,0},{7,1},{8,14},{9,15},{10,... | collective-permute-start | bytes 98312 | tf_op jit(solution)/shard_map/ppermute | solution.py:490
  17.5 34.6 %copy-start.5 = (f32[1,128,512]{2,1,0:T(8,128)S(1)}, f32[1,128,512]{2,1,0:T(8,128)}, u32[]{:S(2)}) copy-start(f32[1,128,512]{2,1,0:T(8,128)} %k_hbm.1) | copy-start | bytes 786436
  17.5 5.0 %collective-permute-start.5 = (f32[4,64,128]{2,1,0:T(8,128)S(1)}, f32[4,64,128]{2,1,0:T(8,128)S(1)}, u32[]{:S(2)}, u32[]{:S(2)}) collective-permute-start(f32[4,64,128]{2,1,0:T(8,128)S(1)} %pad_maximum_fusion), channel_id=1, source_target_pairs={{0,8},{8,0},{16,24},{24,16},{1,9},{9,1},{17,25},{25,17},{2,10},{10... | collective-permute-start | bytes 393224 | tf_op jit(solution)/shard_map/ppermute | solution.py:494
  19.1 33.0 %copy-start.1 = (f32[5,1,128,512]{3,2,1,0:T(8,128)S(1)}, f32[5,1,128,512]{3,2,1,0:T(8,128)}, u32[]{:S(2)}) copy-start(f32[5,1,128,512]{3,2,1,0:T(8,128)} %u_hbm.1) | copy-start | bytes 3932164
  19.1 33.0 %copy-start.3 = (f32[5,1,128,512]{3,2,1,0:T(8,128)S(1)}, f32[5,1,128,512]{3,2,1,0:T(8,128)}, u32[]{:S(2)}) copy-start(f32[5,1,128,512]{3,2,1,0:T(8,128)} %l_hbm.1) | copy-start | bytes 3932164
  23.2 22.6 %collective-permute-start.6 = (f32[8,64,128]{2,1,0:T(8,128)}, f32[8,64,128]{2,1,0:T(8,128)}, u32[]{:S(2)}, u32[]{:S(2)}) collective-permute-start(f32[8,64,128]{2,1,0:T(8,128)} %get-tuple-element.10), channel_id=1, source_target_pairs={{0,1},{1,0},{2,3},{3,2},{4,5},{5,4},{6,7},{7,6},{8,9},{9,8},{10,11... | collective-permute-start | bytes 786440 | tf_op jit(solution)/shard_map/ppermute | solution.py:490
  23.2 5.1 %collective-permute-start.7 = (f32[64,128]{1,0:T(8,128)S(1)}, f32[64,128]{1,0:T(8,128)S(1)}, u32[]{:S(2)}, u32[]{:S(2)}) collective-permute-start(f32[64,128]{1,0:T(8,128)S(1)} %get-tuple-element.9.own), channel_id=1, source_target_pairs={{0,1},{1,2},{2,3},{3,4},{4,5},{5,6},{6,7},{7,0},{8,9},{9,10},{10,1... | collective-permute-start | bytes 98312 | tf_op jit(solution)/shard_map/ppermute | solution.py:486
  23.7 4.6 %collective-permute-start.8 = (f32[64,128]{1,0:T(8,128)S(1)}, f32[64,128]{1,0:T(8,128)S(1)}, u32[]{:S(2)}, u32[]{:S(2)}) collective-permute-start(f32[64,128]{1,0:T(8,128)S(1)} %get-tuple-element.9.own), channel_id=1, source_target_pairs={{0,7},{1,0},{2,1},{3,2},{4,3},{5,4},{6,5},{7,6},{8,15},{9,8},{10,9... | collective-permute-start | bytes 98312 | tf_op jit(solution)/shard_map/ppermute | solution.py:486
  31.5 13.7 %all-to-all-start = ((f32[32,3,2,128]{3,2,1,0:T(2,128)}), f32[32,3,2,128]{3,2,1,0:T(2,128)S(1)}, u32[]{:S(2)}, u32[]{:S(2)}) async-start(f32[32,3,2,128]{3,2,1,0:T(2,128)} %bitcast.16), calls=%async_computation | async-start | bytes 196608 | tf_op jit(solution)/shard_map/all_to_all | solution.py:534
  37.3 14.7 %collective-permute-start = (f32[11,8,512]{2,1,0:T(8,128)}, f32[11,8,512]{2,1,0:T(8,128)}, u32[]{:S(2)}, u32[]{:S(2)}) collective-permute-start(f32[11,8,512]{2,1,0:T(8,128)} %copy-done.14), channel_id=1, source_target_pairs={{0,1},{1,2},{2,3},{3,4},{4,5},{5,6},{6,7},{7,0},{8,9},{9,10},{10,1... | collective-permute-start | bytes 540680 | tf_op jit(solution)/shard_map/ppermute | solution.py:486
  37.6 14.4 %collective-permute-start.1 = (f32[11,8,512]{2,1,0:T(8,128)}, f32[11,8,512]{2,1,0:T(8,128)}, u32[]{:S(2)}, u32[]{:S(2)}) collective-permute-start(f32[11,8,512]{2,1,0:T(8,128)} %copy-done.13), channel_id=1, source_target_pairs={{0,7},{1,0},{2,1},{3,2},{4,3},{5,4},{6,5},{7,6},{8,15},{9,8},{10,9... | collective-permute-start | bytes 540680 | tf_op jit(solution)/shard_map/ppermute | solution.py:486
  (1 other events, 0.7 us)

commit v2 on v1

v2 whole, which is shorter than its diff:
```python
import functools

import jax
import jax.numpy as jnp
from jax import lax
from jax.experimental import pallas as pl
from jax.experimental.pallas import tpu as pltpu
from jax.sharding import PartitionSpec as P

CP_DEV = 256
LANES = 128
SUB = 8
STEPS = 4
NV = 5
UCOLS = STEPS + 2
LCOLS = STEPS
HALO = SUB
ROW_K = 2 * STEPS
ROW_U = ROW_K + UCOLS
ROW_L = ROW_U + NV * UCOLS
STRIP = ROW_L + NV * LCOLS
WALL = STRIP - ROW_K
EDGE_L = NV * UCOLS
EDGE_K = EDGE_L + NV * LCOLS
EDGE_W = EDGE_K + UCOLS
WALL_ROWS = 2 * SUB
EDGE = EDGE_W + WALL_ROWS
TAPS = 6
VMEM_LIMIT = 48 * 1024 * 1024


def params(**kw):
    return pltpu.CompilerParams(vmem_limit_bytes=VMEM_LIMIT, **kw)


def pack_kernel(
    u_hbm, l_hbm, k_hbm, map_hbm, weight_hbm, strip, wall, low, high,
    u_side, l_side, k_side, u_edge, l_edge, k_edge, dmap, dweight, sems,
):
    rows, radial = u_hbm.shape[2], u_hbm.shape[3]
    tiles = radial // LANES
    block = lax.axis_index("block")
    own = pl.ds(pl.multiple_of(block * rows, LANES), rows)
    copies = [
        pltpu.make_async_copy(map_hbm.at[:, 0, own], dmap, sems.at[0, 0]),
        pltpu.make_async_copy(weight_hbm.at[:, 0, own], dweight, sems.at[0, 1]),
    ]
    for i, start in enumerate((0, radial - LANES)):
        lanes = pl.ds(start, LANES)
        copies += [
            pltpu.make_async_copy(u_hbm.at[:, 0, :, lanes], u_side.at[i], sems.at[1, i]),
            pltpu.make_async_copy(l_hbm.at[:, 0, :, lanes], l_side.at[i], sems.at[2, i]),
            pltpu.make_async_copy(k_hbm.at[0, :, lanes], k_side.at[i], sems.at[3, i]),
        ]
    for i, start in enumerate((0, rows - SUB)):
        some = pl.ds(start, SUB)
        copies += [
            pltpu.make_async_copy(u_hbm.at[:, 0, some], u_edge.at[i], sems.at[4, i]),
            pltpu.make_async_copy(l_hbm.at[:, 0, some], l_edge.at[i], sems.at[5, i]),
            pltpu.make_async_copy(k_hbm.at[0, some], k_edge.at[i], sems.at[6, i]),
        ]
    for copy in copies:
        copy.start()
    for copy in copies:
        copy.wait()
    strip[0:STEPS, :] = dmap[...].astype(jnp.float32)
    strip[STEPS : 2 * STEPS, :] = dweight[...]
    strip[ROW_K : ROW_K + UCOLS, :] = k_side[1].T[LANES - UCOLS :]
    wall[0:UCOLS, :] = k_side[0].T[:UCOLS]
    for v in range(NV):
        a, b = ROW_U + v * UCOLS, ROW_L + v * LCOLS
        strip[a : a + UCOLS, :] = u_side[1, v].T[LANES - UCOLS :]
        strip[b : b + LCOLS, :] = l_side[1, v].T[LANES - LCOLS :]
        a, b = a - ROW_K, b - ROW_K
        wall[a : a + UCOLS, :] = u_side[0, v].T[:UCOLS]
        wall[b : b + LCOLS, :] = l_side[0, v].T[:LCOLS]
    for i, ref in enumerate((low, high)):
        few = slice(0, UCOLS) if i == 0 else slice(SUB - UCOLS, SUB)
        fewer = slice(0, LCOLS) if i == 0 else slice(SUB - LCOLS, SUB)
        for v in range(NV):
            ref[v * UCOLS : (v + 1) * UCOLS, :] = u_edge[i, v, few, :]
            ref[EDGE_L + v * LCOLS : EDGE_L + (v + 1) * LCOLS, :] = l_edge[i, v, fewer, :]
        ref[EDGE_K:EDGE_W, :] = k_edge[i, few, :]
        for j in range(tiles):
            some = wall[min(j * WALL_ROWS, WALL) : min((j + 1) * WALL_ROWS, WALL), :]
            if some.shape[0] < WALL_ROWS:
                gap = jnp.zeros((WALL_ROWS - some.shape[0], rows), jnp.float32)
                some = jnp.concatenate([some, gap], axis=0) if some.shape[0] else gap
            ref[EDGE_W:EDGE, j * LANES : (j + 1) * LANES] = some


def pack(start_state, final_cotangent, diffusivity, donor_map, donor_weight):
    _, _, rows, radial = start_state.shape
    f32 = jnp.float32
    outs = ((STRIP, rows), (WALL, rows), (EDGE, radial), (EDGE, radial))
    return pl.pallas_call(
        pack_kernel,
        in_specs=[pl.BlockSpec(memory_space=pltpu.HBM)] * 5,
        out_specs=[pl.BlockSpec(memory_space=pltpu.VMEM)] * 4,
        out_shape=[jax.ShapeDtypeStruct(s, f32) for s in outs],
        scratch_shapes=[
            pltpu.VMEM((2, NV, rows, LANES), f32),
            pltpu.VMEM((2, NV, rows, LANES), f32),
            pltpu.VMEM((2, rows, LANES), f32),
            pltpu.VMEM((2, NV, SUB, radial), f32),
            pltpu.VMEM((2, NV, SUB, radial), f32),
            pltpu.VMEM((2, SUB, radial), f32),
            pltpu.VMEM((STEPS, rows), jnp.int32),
            pltpu.VMEM((STEPS, rows), f32),
            pltpu.SemaphoreType.DMA((7, 2)),
        ],
        compiler_params=params(),
        name="pack",
    )(start_state, final_cotangent, diffusivity, donor_map, donor_weight)


def iota(shape, axis):
    return lax.broadcasted_iota(jnp.int32, shape, axis)


def left(x, by=1):
    return pltpu.roll(x, x.shape[-1] - by, x.ndim - 1)


def right(x, by=1):
    return pltpu.roll(x, by, x.ndim - 1)


def stencil(x):
    inn = jnp.where(iota(x.shape, 0) == 0, 0.0, pltpu.roll(x, 1, 0))
    return left(x) + right(x) + pltpu.roll(x, SUB - 1, 0) + inn - 4.0 * x


def strip_forward(u, t, kappa, c):
    new = []
    for v in range(NV):
        reaction = sum(c[v, w] * t[w] for w in range(NV))
        new.append(u[v] + kappa * stencil(u[v]) - reaction)
    return new


def strip_backward(lam, t, kappa, c):
    new = []
    for v in range(NV):
        pulled = sum(c[w, v] * lam[w] for w in range(NV))
        new.append(lam[v] + stencil(kappa * lam[v]) - (1.0 - t[v] * t[v]) * pulled)
    return new


def wall_kernel(own, before, after, c, proj, area, ids, dist, out, sides, *, devices):
    rows, nodes = own.shape[1], area.shape[1]
    for i, ref in enumerate((before, after)):
        for j in range(-(-WALL // WALL_ROWS)):
            a, b = j * WALL_ROWS, min((j + 1) * WALL_ROWS, WALL)
            sides[i, a:b, :] = ref[EDGE_W : EDGE_W + b - a, j * LANES : (j + 1) * LANES]

    def first(start, cols):
        start = start - ROW_K
        piece = jnp.concatenate(
            [ref[start : start + cols, :] for ref in (sides.at[0], own, sides.at[1])], axis=1
        )
        pad = jnp.zeros((SUB - cols, piece.shape[1]), jnp.float32)
        return jnp.concatenate([piece, pad], axis=0)

    kappa = first(ROW_K, UCOLS)
    u = [first(ROW_U + v * UCOLS, UCOLS) for v in range(NV)]
    lam = [first(ROW_L + v * LCOLS, LCOLS) for v in range(NV)]
    history = []
    for n in range(STEPS):
        t = [jnp.tanh(x) for x in u]
        history.append((u, t))
        if n < STEPS - 1:
            u = strip_forward(u, t, kappa, c)
    h = [0.0] * NV
    for n in reversed(range(STEPS)):
        u, t = history[n]
        h = [h[v] + (lam[v] * u[v])[0:1, rows : 2 * rows] for v in range(NV)]
        if n > 0:
            lam = strip_backward(lam, t, kappa, c)
    per_row = nodes // rows
    groups = CP_DEV // LANES
    s_rows = [sum(proj[i // groups, v] * h[v] for v in range(NV)) for i in range(3 * groups)]
    s_rows += [jnp.zeros((SUB - 3 * groups, rows), jnp.float32)]
    spread = (iota((rows, nodes), 1) // per_row == iota((rows, nodes), 0)).astype(jnp.float32)
    s = jnp.dot(
        jnp.concatenate(s_rows, axis=0), spread,
        precision=lax.Precision.HIGHEST, preferred_element_type=jnp.float32,
    )
    s = s * area[...]
    d = dist[0]
    q = 1.0 - d
    q = q * q
    phi = q * q * (4.0 * d + 1.0)
    key = ids[0]
    major, minor = key // LANES, key % LANES
    shape = (devices, SUB, nodes)
    target = iota(shape, 0) * groups + iota(shape, 1) % groups
    total = jnp.zeros((devices * SUB, LANES), jnp.float32)
    bf = jnp.bfloat16
    for k in range(d.shape[0]):
        lo = (iota((LANES, nodes), 0) == minor[k : k + 1]).astype(bf)
        hit = target == major[k : k + 1][None]
        w = s * phi[k : k + 1]
        for piece in range(3):
            part = w.astype(bf).astype(jnp.float32)
            w = w - part
            a = jnp.where(hit, part[None], 0.0).reshape(devices * SUB, nodes).astype(bf)
            total += lax.dot_general(
                a, lo, (((1,), (1,)), ((), ())), preferred_element_type=jnp.float32
            )
    out[...] = total.reshape(devices, SUB, LANES)


def wall_gradient(own, before, after, coupling, proj, area, ids, dist, devices):
    vm = pl.BlockSpec(memory_space=pltpu.VMEM)
    sm = pl.BlockSpec(memory_space=pltpu.SMEM)
    return pl.pallas_call(
        functools.partial(wall_kernel, devices=devices),
        in_specs=[vm, vm, vm, sm, sm, vm, vm, vm],
        out_specs=vm,
        out_shape=jax.ShapeDtypeStruct((devices, SUB, LANES), jnp.float32),
        scratch_shapes=[pltpu.VMEM((2, WALL, own.shape[1]), jnp.float32)],
        compiler_params=params(),
        name="wall_gradient",
    )(own, before, after, coupling, proj, area, ids, dist)


def sum_kernel(parts, out):
    total = parts[...].sum(axis=0)
    groups = CP_DEV // LANES
    for i in range(3 * groups):
        c, g = i // groups, i % groups
        out[c : c + 1, g * LANES : (g + 1) * LANES] = total[i : i + 1]


def sum_points(parts):
    vm = pl.BlockSpec(memory_space=pltpu.VMEM)
    return pl.pallas_call(
        sum_kernel,
        in_specs=[vm],
        out_specs=vm,
        out_shape=jax.ShapeDtypeStruct((3, CP_DEV), jnp.float32),
        compiler_params=params(),
        name="sum_points",
    )(parts)


def face_kernel(same, other, c, out, buf, turned, flip, *, rows):
    block = lax.axis_index("block")
    blocks = same.shape[0] // 2 * 2
    shape = (blocks, LANES)
    for m in range(blocks // 2):
        at = block ^ (2 * m)
        for q in range(2):
            start = q * STRIP * blocks
            buf[pl.ds(start + at, STRIP, stride=blocks), :] = same[2 * m + q]
            buf[pl.ds(start + (at ^ 1), STRIP, stride=blocks), :] = other[2 * m + q]

    def load(q, row):
        return buf[pl.ds((q * STRIP + row) * blocks, blocks), :]

    lane = iota(shape, 1)
    place = (iota(shape, 0) * LANES + lane).astype(jnp.float32)
    size = float(blocks * rows)

    def later(x, by=1):
        y = jnp.where(lane >= by, x, pltpu.roll(x, blocks - 1, 0))
        return pltpu.roll(y, LANES - by, 1)

    def earlier(x, by=1):
        y = jnp.where(lane < LANES - by, x, pltpu.roll(x, 1, 0))
        return pltpu.roll(y, by, 1)

    def later_far(x, whole, rest):
        near = pltpu.roll(x, (blocks - whole) % blocks, 0)
        y = jnp.where(lane >= rest, near, pltpu.roll(near, blocks - 1, 0))
        return pltpu.roll(y, (LANES - rest) % LANES, 1)

    def earlier_far(x, whole, rest):
        near = pltpu.roll(x, whole, 0)
        y = jnp.where(lane < LANES - rest, near, pltpu.roll(near, 1, 0))
        return pltpu.roll(y, rest, 1)

    far, taps = {}, {}
    for q in range(2):
        for n in range(STEPS):
            delta = load(q, n) - place
            delta = jnp.where(delta < 0.0, delta + size, delta)
            start = delta[0:1, 0:1]
            rel = delta - start + float(STEPS)
            rel = jnp.where(rel < 0.0, rel + size, rel)
            rel = jnp.where(rel >= size, rel - size, rel)
            least = jnp.min(jnp.min(rel, axis=0, keepdims=True), axis=1, keepdims=True)
            e = rel - least
            t = start - float(STEPS) + least
            t = jnp.where(t < 0.0, t + size, t)
            t = jnp.where(t >= size, t - size, t).astype(jnp.int32)[0, 0]
            far[q, n] = (t // LANES, t % LANES)
            share = load(q, STEPS + n)
            taps[q, n] = [
                jnp.where(e == float(i), share, 0.0)
                + jnp.where(e == float(i - 1), 1.0 - share, 0.0)
                for i in range(TAPS)
            ]

    def ghost(q, n, faces):
        result = []
        for f in faces:
            f = later_far(f, *far[q, n])
            after = pltpu.roll(f, blocks - 1, 0)
            acc = taps[q, n][0] * f
            for i in range(1, TAPS):
                y = pltpu.roll(jnp.where(lane >= i, f, after), LANES - i, 1)
                acc = acc + taps[q, n][i] * y
            result.append(acc)
        return result

    def back(q, n, faces):
        result = []
        for f in faces:
            here = taps[q, n][0] * f
            carried = jnp.zeros_like(here)
            for i in range(1, TAPS):
                y = pltpu.roll(taps[q, n][i] * f, i, 1)
                here = here + jnp.where(lane >= i, y, 0.0)
                carried = carried + jnp.where(lane < i, y, 0.0)
            result.append(earlier_far(here + pltpu.roll(carried, 1, 0), *far[q, n]))
        return result

    def emit(index, g):
        for v in range(NV):
            turned[pl.ds((index * SUB + v) * blocks, blocks), :] = g[v]

    last = UCOLS - 1
    kappa = [[load(q, ROW_K + k) for k in range(UCOLS)] for q in range(2)]
    u = [
        [{k: load(q, ROW_U + v * UCOLS + k) for k in range(UCOLS)} for v in range(NV)]
        for q in range(2)
    ]
    gap = UCOLS - LCOLS
    lam = [
        [{k: load(q, ROW_L + v * LCOLS + k - gap) for k in range(gap, UCOLS)} for v in range(NV)]
        for q in range(2)
    ]
    history = {}
    for n in range(STEPS):
        first = n + 1 if n < STEPS - 1 else STEPS - 1
        for q in range(2):
            history[n, q] = [
                {k: jnp.tanh(u[q][v][k]) for k in range(first, UCOLS)} for v in range(NV)
            ]
        if n == STEPS - 1:
            break
        g = [ghost(q, n, [u[1 - q][v][last] for v in range(NV)]) for q in range(2)]
        emit(n, g[0])
        new = []
        for q in range(2):
            side = []
            for v in range(NV):
                cols = {}
                for k in range(n + 1, UCOLS):
                    x = u[q][v][k]
                    outer = u[q][v][k + 1] if k < last else g[q][v]
                    lap = later(x) + earlier(x) + u[q][v][k - 1] + outer - 4.0 * x
                    reaction = sum(c[v, w] * history[n, q][w][k] for w in range(NV))
                    cols[k] = x + kappa[q][k] * lap - reaction
                side.append(cols)
            new.append(side)
        u = new
    for n in reversed(range(STEPS)):
        s = [
            [{k: kappa[q][k] * x for k, x in lam[q][v].items()} for v in range(NV)]
            for q in range(2)
        ]
        sides = (0, 1) if n > 1 else (1,) if n == 1 else ()
        g = {
            q: back(1 - q, n, [s[1 - q][v][last] for v in range(NV)]) for q in {0, *sides}
        }
        emit(STEPS - 1 + n, g[0])
        new = [None, None]
        for q in sides:
            side = []
            for v in range(NV):
                cols = {}
                for k in range(UCOLS - n, UCOLS):
                    x = lam[q][v][k]
                    y = s[q][v][k]
                    outer = s[q][v][k + 1] if k < last else g[q][v]
                    lap = later(y) + earlier(y) + s[q][v][k - 1] + outer - 4.0 * y
                    pulled = sum(c[w, v] * lam[q][w][k] for w in range(NV))
                    t = history[n, q][v][k]
                    cols[k] = x + lap - (1.0 - t * t) * pulled
                side.append(cols)
            new[q] = side
        if n == 1:
            new[0] = [{last: jnp.zeros(shape, jnp.float32)} for v in range(NV)]
        lam = new

    count = (2 * STEPS - 1) * SUB
    flip[...] = jnp.zeros_like(flip)
    around = [
        turned[pl.ds(lax.rem(block + shift + blocks, blocks), count, stride=blocks), :]
        for shift in (-1, 0, 1)
    ]
    wide = jnp.concatenate(around, axis=1)
    wide = pltpu.roll(wide, wide.shape[1] - (LANES - HALO), 1)
    flip[0:count, :] = wide[:, : 2 * LANES]
    for j in range(2):
        out[j * LANES : (j + 1) * LANES, :] = flip[:, j * LANES : (j + 1) * LANES].T


def face_terms(same, other, coupling, rows):
    vm = pl.BlockSpec(memory_space=pltpu.VMEM)
    sm = pl.BlockSpec(memory_space=pltpu.SMEM)
    blocks = same.shape[0]
    f32 = jnp.float32
    return pl.pallas_call(
        functools.partial(face_kernel, rows=rows),
        in_specs=[vm, vm, sm],
        out_specs=vm,
        out_shape=jax.ShapeDtypeStruct((2 * LANES, LANES), f32),
        scratch_shapes=[
            pltpu.VMEM((2 * STRIP * blocks, LANES), f32),
            pltpu.VMEM(((2 * STEPS - 1) * SUB * blocks, LANES), f32),
            pltpu.VMEM((LANES, 2 * LANES), f32),
        ],
        compiler_params=params(),
        name="face_terms",
    )(same, other, coupling)


def field_kernel(
    u_hbm, l_hbm, k_hbm, before, after, terms, c, out,
    ext_u, ext_l, ext_k, kap, states, tanhs, lam, scaled, sems,
):
    rows, radial = u_hbm.shape[2], u_hbm.shape[3]
    chunks = kap.shape[0]
    tiles = radial // LANES
    own = pl.ds(HALO, rows)

    def cut(j):
        return slice(j * LANES, (j + 1) * LANES)

    copies = []
    for j in range(tiles):
        lanes = pl.ds(j * LANES, LANES)
        copies += [
            pltpu.make_async_copy(u_hbm.at[:, 0, :, lanes], ext_u.at[:, j, own], sems.at[0, j]),
            pltpu.make_async_copy(l_hbm.at[:, 0, :, lanes], ext_l.at[:, j, own], sems.at[1, j]),
            pltpu.make_async_copy(k_hbm.at[0, :, lanes], ext_k.at[j, own], sems.at[2, j]),
        ]
    for copy in copies:
        copy.start()
    for ref, lower in ((before, True), (after, False)):
        start = 0 if lower else HALO + rows
        at = start + HALO - UCOLS if lower else start
        below = start + HALO - LCOLS if lower else start
        for j in range(tiles):
            for v in range(NV):
                ext_u[v, j, start : start + HALO] = jnp.zeros((HALO, LANES), jnp.float32)
                ext_l[v, j, start : start + HALO] = jnp.zeros((HALO, LANES), jnp.float32)
                ext_u[v, j, at : at + UCOLS] = ref[v * UCOLS : (v + 1) * UCOLS, cut(j)]
                ext_l[v, j, below : below + LCOLS] = ref[
                    EDGE_L + v * LCOLS : EDGE_L + (v + 1) * LCOLS, cut(j)
                ]
            ext_k[j, start : start + HALO] = jnp.zeros((HALO, LANES), jnp.float32)
            ext_k[j, at : at + UCOLS] = ref[EDGE_K:EDGE_W, cut(j)]
    for copy in copies:
        copy.wait()

    def load(i, carry):
        at = pl.ds(i, SUB, stride=chunks)
        for j in range(tiles):
            kappa = ext_k[j, at, :]
            kap[i, :, cut(j)] = kappa
            for v in range(NV):
                states[0, v, i + 1, :, cut(j)] = ext_u[v, j, at, :]
                x = ext_l[v, j, at, :]
                lam[v, i, :, cut(j)] = x
                scaled[0, v, i + 1, :, cut(j)] = kappa * x
        return carry

    lax.fori_loop(0, chunks, load, 0, unroll=2)

    def wrap(ref):
        for v in range(NV):
            ref[v, 0] = pltpu.roll(ref[v, chunks], 1, 0)
            ref[v, chunks + 1] = pltpu.roll(ref[v, 1], SUB - 1, 0)

    wrap(states.at[0])
    wrap(scaled.at[0])
    lane = iota((SUB, LANES), 1)
    is_first, is_last = lane == 0, lane == LANES - 1

    def neighbours(ref, v, i, j, edge, cache):
        def tile(b):
            if (v, b) not in cache:
                x = ref[v, i + 1, :, cut(b)]
                cache[v, b] = (x, pltpu.roll(x, 1, 1), pltpu.roll(x, LANES - 1, 1))
            return cache[v, b]

        x, r, l = tile(j)
        inn = jnp.where(is_first, tile(j - 1)[1] if j > 0 else 0.0, r)
        outv = jnp.where(is_last, tile(j + 1)[2] if j < tiles - 1 else edge, l)
        return ref[v, i, :, cut(j)] + ref[v, i + 2, :, cut(j)] + inn + outv, x

    def edges(i, n):
        e = terms[pl.ds(i, SUB, stride=chunks), :]
        return [pltpu.roll(e, (2 * LANES - 1 - (n * SUB + v)) % LANES, 1) for v in range(NV)]

    def forward(n):
        def body(i, carry):
            edge = edges(i, n)
            cache = {}
            for j in range(tiles):
                kappa = kap[i, :, cut(j)]
                pairs = [neighbours(states.at[n], v, i, j, edge[v], cache) for v in range(NV)]
                t = [jnp.tanh(x) for _, x in pairs]
                for v in range(NV):
                    around, x = pairs[v]
                    tanhs[n, v, i, :, cut(j)] = t[v]
                    reaction = sum(c[v, w] * t[w] for w in range(NV))
                    states[n + 1, v, i + 1, :, cut(j)] = (
                        x + kappa * (around - 4.0 * x) - reaction
                    )
            return carry

        lax.fori_loop(0, chunks, body, 0, unroll=6)
        if n + 1 < STEPS - 1:
            wrap(states.at[n + 1])

    def backward(n, source, target):
        def body(i, carry):
            edge = edges(i, STEPS - 1 + n)
            cache = {}
            for j in range(tiles):
                kappa = kap[i, :, cut(j)]
                pairs = [neighbours(scaled.at[source], v, i, j, edge[v], cache) for v in range(NV)]
                x = [lam[v, i, :, cut(j)] for v in range(NV)]
                for v in range(NV):
                    if n < STEPS - 1:
                        t = tanhs[n, v, i, :, cut(j)]
                    else:
                        t = jnp.tanh(states[n, v, i + 1, :, cut(j)])
                    around, s = pairs[v]
                    pulled = sum(c[w, v] * x[w] for w in range(NV))
                    new = x[v] + (around - 4.0 * s) - (1.0 - t * t) * pulled
                    if n > 0:
                        lam[v, i, :, cut(j)] = new
                        scaled[target, v, i + 1, :, cut(j)] = kappa * new
                    else:
                        ext_l[v, j, pl.ds(i, SUB, stride=chunks), :] = new
            return carry

        lax.fori_loop(0, chunks, body, 0, unroll=6)
        if n > 0:
            wrap(scaled.at[target])

    for n in range(STEPS - 1):
        forward(n)
    source = 0
    for n in reversed(range(STEPS)):
        backward(n, source, 1 - source)
        source = 1 - source
    copies = [
        pltpu.make_async_copy(
            ext_l.at[:, j, own], out.at[:, 0, :, pl.ds(j * LANES, LANES)], sems.at[3, j]
        )
        for j in range(tiles)
    ]
    for copy in copies:
        copy.start()
    for copy in copies:
        copy.wait()


def field(start_state, final_cotangent, diffusivity, before, after, terms, coupling):
    _, _, rows, radial = start_state.shape
    ext = rows + 2 * HALO
    chunks, tiles = ext // SUB, radial // LANES
    vm = pl.BlockSpec(memory_space=pltpu.VMEM)
    hbm = pl.BlockSpec(memory_space=pl.ANY)
    f32 = jnp.float32
    return pl.pallas_call(
        field_kernel,
        in_specs=[hbm, hbm, hbm, vm, vm, vm, pl.BlockSpec(memory_space=pltpu.SMEM)],
        out_specs=hbm,
        out_shape=jax.ShapeDtypeStruct(start_state.shape, f32),
        scratch_shapes=[
            pltpu.VMEM((NV, tiles, ext, LANES), f32),
            pltpu.VMEM((NV, tiles, ext, LANES), f32),
            pltpu.VMEM((tiles, ext, LANES), f32),
            pltpu.VMEM((chunks, SUB, radial), f32),
            pltpu.VMEM((STEPS, NV, chunks + 2, SUB, radial), f32),
            pltpu.VMEM((STEPS - 1, NV, chunks, SUB, radial), f32),
            pltpu.VMEM((NV, chunks, SUB, radial), f32),
            pltpu.VMEM((2, NV, chunks + 2, SUB, radial), f32),
            pltpu.SemaphoreType.DMA((4, tiles)),
        ],
        compiler_params=params(),
        name="field",
    )(start_state, final_cotangent, diffusivity, before, after, terms, coupling)


def ring(x, step):
    size = lax.axis_size("block")
    return lax.ppermute(x, "block", [(i, (i + step) % size) for i in range(size)])


def crossed(x, mask):
    return lax.ppermute(x, "block", [(i, i ^ mask) for i in range(lax.axis_size("block"))])


def swapped(x):
    return lax.ppermute(x, "zone", [(i, i ^ 1) for i in range(lax.axis_size("zone"))])


def gather_pair(strip):
    x = jnp.stack([strip, swapped(strip)])
    bit, size = 1, lax.axis_size("block")
    while 2**bit < size:
        wide = 4 if 2 ** (bit + 1) < size else 2
        x = jnp.concatenate([x] + [crossed(x, k << bit) for k in range(1, wide)], axis=0)
        bit += 2 if wide == 4 else 1
    return x, crossed(x, 1)


def local(
    start_state,
    diffusivity,
    donor_map,
    donor_weight,
    coupling,
    final_cotangent,
    wall_area,
    wall_projection,
    center_ids,
    center_dist,
):
    rows = start_state.shape[2]
    devices = lax.axis_size("zone") * lax.axis_size("block")
    strip, wall, low, high = pack(
        start_state, final_cotangent, diffusivity, donor_map, donor_weight
    )
    before, after = ring(high, 1), ring(low, -1)
    same, other = gather_pair(strip)
    points = wall_gradient(
        wall, before, after, coupling, wall_projection, wall_area, center_ids, center_dist, devices
    )
    points = lax.all_to_all(points, ("zone", "block"), 0, 0, tiled=True)
    gradient = sum_points(points)
    terms = face_terms(same, other, coupling, rows)
    adjoint = field(start_state, final_cotangent, diffusivity, before, after, terms, coupling)
    return adjoint, gradient


def solution(mesh):
    return jax.shard_map(
        local,
        mesh=mesh,
        in_specs=(
            P(None, "zone", "block", None),
            P("zone", "block", None),
            P(None, "zone", None),
            P(None, "zone", None),
            P(),
            P(None, "zone", "block", None),
            P("zone", "block"),
            P(),
            P("zone", None, "block"),
            P("zone", None, "block"),
        ),
        out_specs=(P(None, "zone", "block", None), P(None, ("zone", "block"))),
        check_vma=False,
    )
```

time: 71.9 us -> 47 us (0.65)
  waiting for transfers between devices: 12.6 us -> 3.7 us
  Pallas kernels: 27.3 us -> 19.4 us
  starting transfers between devices: 20.2 us -> 14.5 us
  local copies, waits for them, and re-layouts: 10.4 us -> 8.18 us
    pallas_call x1, Pallas kernels: 19.3 us -> 11.3 us  [field(): pl.pallas_call(field_kernel, in_specs=[hbm, hbm, hbm, vm, vm, vm, pl.Bloc...]
    all_to_all x1, waiting for transfers between devices: 4.3 us -> 0.01 us  [local(): points = lax.all_to_all(points, ('zone', 'block'), 0, 0, tiled=True)]
    ppermute x4 -> x2, starting transfers between devices: 7.14 us -> 3.54 us  [ring(): lax.ppermute(x, 'block', [(i, (i + step) % size) for i in range(size)])]
    all_to_all x1, starting transfers between devices: 5.78 us -> 3.53 us  [local(): points = lax.all_to_all(points, ('zone', 'block'), 0, 0, tiled=True)]
    ppermute x1, waiting for transfers between devices: 1.61 us -> 0.01 us  [swapped(): lax.ppermute(x, 'zone', [(i, i ^ 1) for i in range(lax.axis_size('zone'))])]
    ppermute x4 -> x2, waiting for transfers between devices: 1.6 us -> 0.01 us  [ring(): lax.ppermute(x, 'block', [(i, (i + step) % size) for i in range(size)])]
    ppermute x1, starting transfers between devices: 1.56 us -> 3 us  [swapped(): lax.ppermute(x, 'zone', [(i, i ^ 1) for i in range(lax.axis_size('zone'))])]
    ppermute x4, waiting for transfers between devices: 5.09 us -> 3.69 us  [crossed(): lax.ppermute(x, 'block', [(i, i ^ mask) for i in range(lax.axis_size('blo...]
  transfers between devices with their start and end apart: 10 -> 8, of which waited for: 5 -> 2; matrix products, arithmetic and copies ran while one was open for 7% -> 7% of each run, Pallas kernels for 11% -> 38%
where the time goes in v2:
time: 47 us; the launch traced here: 46.6 us
  Pallas kernels  19.4 us (41%)
  starting transfers between devices  14.5 us (31%)
  local copies, waits for them, and re-layouts  8.18 us (17%)
  waiting for transfers between devices  3.7 us (8%)
  between operations  0.8 us (2%)
    pallas_call x1, Pallas kernels, field(): pl.pallas_call(field_kernel, in_specs=[hbm, hbm, hbm, vm, vm, vm, pl.Bloc...  11.3 us
    unnamed x30, local copies, waits for them, and re-layouts  7.55 us
    ppermute x4, starting transfers between devices, crossed(): lax.ppermute(x, 'block', [(i, i ^ mask) for i in range(lax.axis_size('blo...  4.46 us
    ppermute x4, waiting for transfers between devices, crossed(): lax.ppermute(x, 'block', [(i, i ^ mask) for i in range(lax.axis_size('blo...  3.69 us
    ppermute x2, starting transfers between devices, ring(): lax.ppermute(x, 'block', [(i, (i + step) % size) for i in range(size)])  3.54 us
    all_to_all x1, starting transfers between devices, local(): points = lax.all_to_all(points, ('zone', 'block'), 0, 0, tiled=True)  3.53 us
    pallas_call x1, Pallas kernels, wall_gradient(): pl.pallas_call(functools.partial(wall_kernel, devices=devices), in_specs=...  3.32 us
    pallas_call x1, Pallas kernels, face_terms(): pl.pallas_call(functools.partial(face_kernel, rows=rows), in_specs=[vm, v...  3.18 us
  transfers between devices with their start and end apart: 8, of which 2 were waited for; matrix products, arithmetic and copies ran while one was open for 7% of the time, Pallas kernels for 38%

profile of v2, /device:TPU:0, one launch (start us, length us, event | category | flops | bytes accessed | tf_op | source)
XLA Modules:
  0.0 46.6 jit_solution(14555239153764870194)
XLA Ops:
  0.6 1.3 %copy-done = f32[5,1,128,512]{3,2,1,0:T(8,128)S(1)} copy-done((f32[5,1,128,512]{3,2,1,0:T(8,128)S(1)}, f32[5,1,128,512]{3,2,1,0:T(8,128)}, u32[]{:S(2)}) %copy-start) | copy-done | bytes 1310744
  2.0 1.3 %copy-done.2 = f32[5,1,128,512]{3,2,1,0:T(8,128)S(1)} copy-done((f32[5,1,128,512]{3,2,1,0:T(8,128)S(1)}, f32[5,1,128,512]{3,2,1,0:T(8,128)}, u32[]{:S(2)}) %copy-start.2) | copy-done | bytes 1310744
  3.3 0.9 %copy-done.4 = f32[1,128,512]{2,1,0:T(8,128)S(1)} copy-done((f32[1,128,512]{2,1,0:T(8,128)S(1)}, f32[1,128,512]{2,1,0:T(8,128)}, u32[]{:S(2)}) %copy-start.4) | copy-done | bytes 262168
  4.2 0.7 %copy-done.7 = s32[4,1,1024]{2,1,0:T(1,128)S(1)} copy-done((s32[4,1,1024]{2,1,0:T(1,128)S(1)}, s32[4,1,1024]{2,1,0:T(1,128)}, u32[]{:S(2)}) %copy-start.7) | copy-done | bytes 16408
  4.9 0.7 %copy-done.8 = f32[4,1,1024]{2,1,0:T(1,128)S(1)} copy-done((f32[4,1,1024]{2,1,0:T(1,128)S(1)}, f32[4,1,1024]{2,1,0:T(1,128)}, u32[]{:S(2)}) %copy-start.8) | copy-done | bytes 16408
  5.7 0.9 %pack.1 = (f32[64,128]{1,0:T(8,128)S(1)}, f32[56,128]{1,0:T(8,128)S(1)}, f32[72,512]{1,0:T(8,128)S(1)}, f32[72,512]{1,0:T(8,128)S(1)}) custom-call(f32[5,1,128,512]{3,2,1,0:T(8,128)S(1)} %copy-done, f32[5,1,128,512]{3,2,1,0:T(8,128)S(1)} %copy-done.2, f32[1,128,512]{2,1,0:T(8,128)S(1)} %copy-done.4, s32[4,1,1024]{2,1,0:T(1,128)S(1)} %copy-done.7, ...), custom_call_target="tpu_custom_call" | custom-call | tf_op jit(solution)/shard_map/pack/pallas_call | solution.py:96
  6.6 0.0 copy-start.1
  6.6 0.0 copy-start.5
  6.7 3.0 %collective-permute-start.2 = (f32[64,128]{1,0:T(8,128)S(1)}, f32[64,128]{1,0:T(8,128)S(1)}, u32[]{:S(2)}, u32[]{:S(2)}) collective-permute-start(f32[64,128]{1,0:T(8,128)S(1)} %get-tuple-element.8), channel_id=1, source_target_pairs={{0,8},{8,0},{16,24},{24,16},{1,9},{9,1},{17,25},{25,17},{2,10},{10... | collective-permute-start | bytes 98312 | tf_op jit(solution)/shard_map/ppermute | solution.py:615
  9.7 3.5 %collective-permute-start.1 = (f32[72,512]{1,0:T(8,128)S(1)}, f32[72,512]{1,0:T(8,128)S(1)}, u32[]{:S(2)}, u32[]{:S(2)}) collective-permute-start(f32[72,512]{1,0:T(8,128)S(1)} %get-tuple-element.7), channel_id=1, source_target_pairs={{0,7},{1,0},{2,1},{3,2},{4,3},{5,4},{6,5},{7,6},{8,15},{9,8},{10,9... | collective-permute-start | bytes 442376 | tf_op jit(solution)/shard_map/ppermute | solution.py:607
  13.2 0.6 %constant_dynamic-update-slice_fusion.4 = f32[8,64,128]{2,1,0:T(8,128)} fusion(f32[64,128]{1,0:T(8,128)S(1)} %get-tuple-element.8), kind=kLoop, calls=%fused_computation.5 | loop fusion | bytes 65536
  13.8 1.9 %collective-permute-start.5 = (f32[2,64,128]{2,1,0:T(8,128)S(1)}, f32[2,64,128]{2,1,0:T(8,128)S(1)}, u32[]{:S(2)}, u32[]{:S(2)}) collective-permute-start(f32[2,64,128]{2,1,0:T(8,128)S(1)} %pad_maximum_fusion), channel_id=1, source_target_pairs={{0,6},{1,7},{2,4},{3,5},{4,2},{5,3},{6,0},{7,1},{8,14},{9,15},{10,... | collective-permute-start | bytes 196616 | tf_op jit(solution)/shard_map/ppermute | solution.py:611
  15.7 2.6 %collective-permute-start.3 = (f32[2,64,128]{2,1,0:T(8,128)S(1)}, f32[2,64,128]{2,1,0:T(8,128)S(1)}, u32[]{:S(2)}, u32[]{:S(2)}) collective-permute-start(f32[2,64,128]{2,1,0:T(8,128)S(1)} %pad_maximum_fusion), channel_id=1, source_target_pairs={{0,2},{1,3},{2,0},{3,1},{4,6},{5,7},{6,4},{7,5},{8,10},{9,11},{10,... | collective-permute-start | bytes 196616 | tf_op jit(solution)/shard_map/ppermute | solution.py:611
  18.3 0.6 %constant_dynamic-update-slice_fusion.3 = f32[8,64,128]{2,1,0:T(8,128)} fusion(f32[8,64,128]{2,1,0:T(8,128)} %constant_dynamic-update-slice_fusion.4, f32[64,128]{1,0:T(8,128)S(1)} %collective-permute-done.2), kind=kLoop, calls=%fused_computation.4 | loop fusion | bytes 65536
  18.9 2.4 %collective-permute-done.3 = f32[2,64,128]{2,1,0:T(8,128)S(1)} collective-permute-done((f32[2,64,128]{2,1,0:T(8,128)S(1)}, f32[2,64,128]{2,1,0:T(8,128)S(1)}, u32[]{:S(2)}, u32[]{:S(2)}) %collective-permute-start.3) | collective-permute-done | bytes 65568 | tf_op jit(solution)/shard_map/ppermute | solution.py:611
  21.3 0.6 %constant_dynamic-update-slice_fusion.2 = f32[8,64,128]{2,1,0:T(8,128)} fusion(f32[8,64,128]{2,1,0:T(8,128)} %constant_dynamic-update-slice_fusion.3, f32[2,64,128]{2,1,0:T(8,128)S(1)} %collective-permute-done.3), kind=kLoop, calls=%fused_computation.3 | loop fusion | bytes 131072
  22.0 1.3 %collective-permute-done.4 = f32[2,64,128]{2,1,0:T(8,128)S(1)} collective-permute-done((f32[2,64,128]{2,1,0:T(8,128)S(1)}, f32[2,64,128]{2,1,0:T(8,128)S(1)}, u32[]{:S(2)}, u32[]{:S(2)}) %collective-permute-start.4) | collective-permute-done | bytes 65568 | tf_op jit(solution)/shard_map/ppermute | solution.py:611
  23.2 0.6 %constant_dynamic-update-slice_fusion.1 = f32[8,64,128]{2,1,0:T(8,128)} fusion(f32[8,64,128]{2,1,0:T(8,128)} %constant_dynamic-update-slice_fusion.2, f32[2,64,128]{2,1,0:T(8,128)S(1)} %collective-permute-done.4), kind=kLoop, calls=%fused_computation.2 | loop fusion | bytes 131072
  23.9 0.6 %constant_dynamic-update-slice_fusion.same = f32[8,64,128]{2,1,0:T(8,128)} fusion(f32[8,64,128]{2,1,0:T(8,128)} %constant_dynamic-update-slice_fusion.1, f32[2,64,128]{2,1,0:T(8,128)S(1)} %collective-permute-done.5), kind=kLoop, calls=%fused_computation.1 | loop fusion | bytes 131072 | tf_op jit(solution)/shard_map/concatenate | solution.py:623
  24.6 3.3 %wall_gradient.1 = f32[32,8,128]{2,1,0:T(8,128)} custom-call(f32[56,128]{1,0:T(8,128)S(1)} %get-tuple-element.9.own, f32[72,512]{1,0:T(8,128)S(1)} %collective-permute-done.before, f32[72,512]{1,0:T(8,128)S(1)} %collective-permute-done.1.after, f32[5,5]{1,0:T(8,128)S(1)} %copy-done.6, f32[3,5]{1,0:T(4,128)S(1)} %copy-done.11, f32[1,384]{1,0:T(1,128)S(1)} %copy-done.12, ...), custom_call_target="tpu_custom_call" | custom-call | tf_op jit(solution)/shard_map/wall_gradient/pallas_call | solution.py:217
  27.9 3.5 %all-to-all-start = ((f32[32,8,128]{2,1,0:T(8,128)}), f32[32,8,128]{2,1,0:T(8,128)S(1)}, u32[]{:S(2)}, u32[]{:S(2)}) async-start(f32[32,8,128]{2,1,0:T(8,128)} %wall_gradient.1), calls=%async_computation | async-start | bytes 262144 | tf_op jit(solution)/shard_map/all_to_all | solution.py:650
  31.4 3.2 %face_terms.1.terms = f32[256,128]{1,0:T(8,128)S(1)} custom-call(f32[8,64,128]{2,1,0:T(8,128)} %constant_dynamic-update-slice_fusion.same, f32[8,64,128]{2,1,0:T(8,128)} %collective-permute-done.6.other, f32[5,5]{1,0:T(8,128)S(1)} %copy-done.6), custom_call_target="tpu_custom_call" | custom-call | tf_op jit(solution)/shard_map/face_terms/pallas_call | solution.py:417
  34.7 11.3 %field.1 = f32[5,1,128,512]{3,2,1,0:T(8,128)} custom-call(f32[5,1,128,512]{3,2,1,0:T(8,128)S(1)} %copy-done.1, f32[5,1,128,512]{3,2,1,0:T(8,128)S(1)} %copy-done.3, f32[1,128,512]{2,1,0:T(8,128)S(1)} %copy-done.5, f32[72,512]{1,0:T(8,128)S(1)} %collective-permute-done.before, f32[72,512]{1,0:T(8,128)S(1)} %collective-permute-done.1.after, ...), custom_call_target="tpu_custom_call" | custom-call | tf_op jit(solution)/shard_map/field/pallas_call | solution.py:584
  46.0 0.6 %sum_points.1 = f32[3,256]{1,0:T(4,128)} custom-call(f32[32,8,128]{2,1,0:T(8,128)S(1)} %all-to-all-done.parts), custom_call_target="tpu_custom_call" | custom-call | tf_op jit(solution)/shard_map/sum_points/pallas_call | solution.py:238
  (29 shorter events, 0.1 us)
Async XLA Ops:
  0.6 1.3 %copy-start = (f32[5,1,128,512]{3,2,1,0:T(8,128)S(1)}, f32[5,1,128,512]{3,2,1,0:T(8,128)}, u32[]{:S(2)}) copy-start(f32[5,1,128,512]{3,2,1,0:T(8,128)} %u_hbm.3) | copy-start | bytes 3932164
  2.0 1.3 %copy-start.2 = (f32[5,1,128,512]{3,2,1,0:T(8,128)S(1)}, f32[5,1,128,512]{3,2,1,0:T(8,128)}, u32[]{:S(2)}) copy-start(f32[5,1,128,512]{3,2,1,0:T(8,128)} %l_hbm.3) | copy-start | bytes 3932164
  3.3 0.9 %copy-start.4 = (f32[1,128,512]{2,1,0:T(8,128)S(1)}, f32[1,128,512]{2,1,0:T(8,128)}, u32[]{:S(2)}) copy-start(f32[1,128,512]{2,1,0:T(8,128)} %k_hbm.3) | copy-start | bytes 786436
  4.2 0.7 %copy-start.7 = (s32[4,1,1024]{2,1,0:T(1,128)S(1)}, s32[4,1,1024]{2,1,0:T(1,128)}, u32[]{:S(2)}) copy-start(s32[4,1,1024]{2,1,0:T(1,128)} %map_hbm.1) | copy-start | bytes 49156
  4.9 0.7 %copy-start.8 = (f32[4,1,1024]{2,1,0:T(1,128)S(1)}, f32[4,1,1024]{2,1,0:T(1,128)}, u32[]{:S(2)}) copy-start(f32[4,1,1024]{2,1,0:T(1,128)} %weight_hbm.1) | copy-start | bytes 49156
  5.7 18.9 %copy-start.6 = (f32[5,5]{1,0:T(8,128)S(1)}, f32[5,5]{1,0:T(8,128)}, u32[]{:S(2)}) copy-start(f32[5,5]{1,0:T(8,128)} %c.5) | copy-start | bytes 304
  5.7 18.9 %copy-start.9 = (s32[1,8,384]{2,1,0:T(8,128)S(1)}, s32[1,8,384]{2,1,0:T(8,128)}, u32[]{:S(2)}) copy-start(s32[1,8,384]{2,1,0:T(8,128)} %ids.1) | copy-start | bytes 36868
  5.7 18.9 %copy-start.10 = (f32[1,8,384]{2,1,0:T(8,128)S(1)}, f32[1,8,384]{2,1,0:T(8,128)}, u32[]{:S(2)}) copy-start(f32[1,8,384]{2,1,0:T(8,128)} %dist.1) | copy-start | bytes 36868
  5.7 18.9 %copy-start.11 = (f32[3,5]{1,0:T(4,128)S(1)}, f32[3,5]{1,0:T(4,128)}, u32[]{:S(2)}) copy-start(f32[3,5]{1,0:T(4,128)} %proj.1) | copy-start | bytes 184
  5.7 18.9 %copy-start.12 = (f32[1,384]{1,0:T(1,128)S(1)}, f32[1,384]{1,0:T(1,128)}, u32[]{:S(2)}) copy-start(f32[1,384]{1,0:T(1,128)} %area.1) | copy-start | bytes 4612
  5.7 29.0 %copy-start.3 = (f32[5,1,128,512]{3,2,1,0:T(8,128)S(1)}, f32[5,1,128,512]{3,2,1,0:T(8,128)}, u32[]{:S(2)}) copy-start(f32[5,1,128,512]{3,2,1,0:T(8,128)} %l_hbm.3) | copy-start | bytes 3932164
  6.6 28.0 %copy-start.1 = (f32[5,1,128,512]{3,2,1,0:T(8,128)S(1)}, f32[5,1,128,512]{3,2,1,0:T(8,128)}, u32[]{:S(2)}) copy-start(f32[5,1,128,512]{3,2,1,0:T(8,128)} %u_hbm.3) | copy-start | bytes 3932164
  6.6 28.0 %copy-start.5 = (f32[1,128,512]{2,1,0:T(8,128)S(1)}, f32[1,128,512]{2,1,0:T(8,128)}, u32[]{:S(2)}) copy-start(f32[1,128,512]{2,1,0:T(8,128)} %k_hbm.3) | copy-start | bytes 786436
  6.7 7.2 %collective-permute-start.2 = (f32[64,128]{1,0:T(8,128)S(1)}, f32[64,128]{1,0:T(8,128)S(1)}, u32[]{:S(2)}, u32[]{:S(2)}) collective-permute-start(f32[64,128]{1,0:T(8,128)S(1)} %get-tuple-element.8), channel_id=1, source_target_pairs={{0,8},{8,0},{16,24},{24,16},{1,9},{9,1},{17,25},{25,17},{2,10},{10... | collective-permute-start | bytes 98312 | tf_op jit(solution)/shard_map/ppermute | solution.py:615
  9.7 14.8 %collective-permute-start = (f32[72,512]{1,0:T(8,128)S(1)}, f32[72,512]{1,0:T(8,128)S(1)}, u32[]{:S(2)}, u32[]{:S(2)}) collective-permute-start(f32[72,512]{1,0:T(8,128)S(1)} %get-tuple-element.6), channel_id=1, source_target_pairs={{0,1},{1,2},{2,3},{3,4},{4,5},{5,6},{6,7},{7,0},{8,9},{9,10},{10,1... | collective-permute-start | bytes 442376 | tf_op jit(solution)/shard_map/ppermute | solution.py:607
  9.7 14.8 %collective-permute-start.1 = (f32[72,512]{1,0:T(8,128)S(1)}, f32[72,512]{1,0:T(8,128)S(1)}, u32[]{:S(2)}, u32[]{:S(2)}) collective-permute-start(f32[72,512]{1,0:T(8,128)S(1)} %get-tuple-element.7), channel_id=1, source_target_pairs={{0,7},{1,0},{2,1},{3,2},{4,3},{5,4},{6,5},{7,6},{8,15},{9,8},{10,9... | collective-permute-start | bytes 442376 | tf_op jit(solution)/shard_map/ppermute | solution.py:607
  13.8 10.0 %collective-permute-start.5 = (f32[2,64,128]{2,1,0:T(8,128)S(1)}, f32[2,64,128]{2,1,0:T(8,128)S(1)}, u32[]{:S(2)}, u32[]{:S(2)}) collective-permute-start(f32[2,64,128]{2,1,0:T(8,128)S(1)} %pad_maximum_fusion), channel_id=1, source_target_pairs={{0,6},{1,7},{2,4},{3,5},{4,2},{5,3},{6,0},{7,1},{8,14},{9,15},{10,... | collective-permute-start | bytes 196616 | tf_op jit(solution)/shard_map/ppermute | solution.py:611
  15.7 7.5 %collective-permute-start.4 = (f32[2,64,128]{2,1,0:T(8,128)S(1)}, f32[2,64,128]{2,1,0:T(8,128)S(1)}, u32[]{:S(2)}, u32[]{:S(2)}) collective-permute-start(f32[2,64,128]{2,1,0:T(8,128)S(1)} %pad_maximum_fusion), channel_id=1, source_target_pairs={{0,4},{1,5},{2,6},{3,7},{4,0},{5,1},{6,2},{7,3},{8,12},{9,13},{10,... | collective-permute-start | bytes 196616 | tf_op jit(solution)/shard_map/ppermute | solution.py:611
  15.7 5.6 %collective-permute-start.3 = (f32[2,64,128]{2,1,0:T(8,128)S(1)}, f32[2,64,128]{2,1,0:T(8,128)S(1)}, u32[]{:S(2)}, u32[]{:S(2)}) collective-permute-start(f32[2,64,128]{2,1,0:T(8,128)S(1)} %pad_maximum_fusion), channel_id=1, source_target_pairs={{0,2},{1,3},{2,0},{3,1},{4,6},{5,7},{6,4},{7,5},{8,10},{9,11},{10,... | collective-permute-start | bytes 196616 | tf_op jit(solution)/shard_map/ppermute | solution.py:611
  24.5 6.9 %collective-permute-start.6 = (f32[8,64,128]{2,1,0:T(8,128)}, f32[8,64,128]{2,1,0:T(8,128)}, u32[]{:S(2)}, u32[]{:S(2)}) collective-permute-start(f32[8,64,128]{2,1,0:T(8,128)} %constant_dynamic-update-slice_fusion.same), channel_id=1, source_target_pairs={{0,1},{1,0},{2,3},{3,2},{4,5},{5,4},{6,7},{7,6},{8,9},{9,8},{10,11... | collective-permute-start | bytes 786440 | tf_op jit(solution)/shard_map/ppermute | solution.py:611
  27.9 18.1 %all-to-all-start = ((f32[32,8,128]{2,1,0:T(8,128)}), f32[32,8,128]{2,1,0:T(8,128)S(1)}, u32[]{:S(2)}, u32[]{:S(2)}) async-start(f32[32,8,128]{2,1,0:T(8,128)} %wall_gradient.1), calls=%async_computation | async-start | bytes 262144 | tf_op jit(solution)/shard_map/all_to_all | solution.py:650

commit v3 on v2

--- a/solution.py
+++ b/solution.py
@@ -19,41 +19,39 @@
 ROW_U = ROW_K + UCOLS
 ROW_L = ROW_U + NV * UCOLS
 STRIP = ROW_L + NV * LCOLS
-WALL = STRIP - ROW_K
 EDGE_L = NV * UCOLS
 EDGE_K = EDGE_L + NV * LCOLS
-EDGE_W = EDGE_K + UCOLS
-WALL_ROWS = 2 * SUB
-EDGE = EDGE_W + WALL_ROWS
+EDGE = EDGE_K + UCOLS
 TAPS = 6
+UNROLL = 18
 VMEM_LIMIT = 48 * 1024 * 1024
 
 
-def params(**kw):
-    return pltpu.CompilerParams(vmem_limit_bytes=VMEM_LIMIT, **kw)
+def params(limit=VMEM_LIMIT):
+    return pltpu.CompilerParams(vmem_limit_bytes=limit)
 
 
 def pack_kernel(
-    u_hbm, l_hbm, k_hbm, map_hbm, weight_hbm, strip, wall, low, high,
+    u_hbm, l_hbm, k_hbm, map_hbm, weight_hbm, strip, near, far,
     u_side, l_side, k_side, u_edge, l_edge, k_edge, dmap, dweight, sems,
 ):
     rows, radial = u_hbm.shape[2], u_hbm.shape[3]
-    tiles = radial // LANES
     block = lax.axis_index("block")
     own = pl.ds(pl.multiple_of(block * rows, LANES), rows)
     copies = [
         pltpu.make_async_copy(map_hbm.at[:, 0, own], dmap, sems.at[0, 0]),
         pltpu.make_async_copy(weight_hbm.at[:, 0, own], dweight, sems.at[0, 1]),
     ]
-    for i, start in enumerate((0, radial - LANES)):
-        lanes = pl.ds(start, LANES)
-        copies += [
-            pltpu.make_async_copy(u_hbm.at[:, 0, :, lanes], u_side.at[i], sems.at[1, i]),
-            pltpu.make_async_copy(l_hbm.at[:, 0, :, lanes], l_side.at[i], sems.at[2, i]),
-            pltpu.make_async_copy(k_hbm.at[0, :, lanes], k_side.at[i], sems.at[3, i]),
-        ]
-    for i, start in enumerate((0, rows - SUB)):
-        some = pl.ds(start, SUB)
+    lanes = pl.ds(radial - LANES, LANES)
+    copies += [
+        pltpu.make_async_copy(u_hbm.at[:, 0, :, lanes], u_side, sems.at[1, 0]),
+        pltpu.make_async_copy(l_hbm.at[:, 0, :, lanes], l_side, sems.at[2, 0]),
+        pltpu.make_async_copy(k_hbm.at[0, :, lanes], k_side, sems.at[3, 0]),
+    ]
+    lower = block % 2 == 0
+    top = jnp.where(lower, rows - SUB, 0)
+    for i, start in enumerate((top, rows - SUB - top)):
+        some = pl.ds(pl.multiple_of(start, SUB), SUB)
         copies += [
             pltpu.make_async_copy(u_hbm.at[:, 0, some], u_edge.at[i], sems.at[4, i]),
             pltpu.make_async_copy(l_hbm.at[:, 0, some], l_edge.at[i], sems.at[5, i]),
@@ -65,43 +63,36 @@
         copy.wait()
     strip[0:STEPS, :] = dmap[...].astype(jnp.float32)
     strip[STEPS : 2 * STEPS, :] = dweight[...]
-    strip[ROW_K : ROW_K + UCOLS, :] = k_side[1].T[LANES - UCOLS :]
-    wall[0:UCOLS, :] = k_side[0].T[:UCOLS]
+    strip[ROW_K : ROW_K + UCOLS, :] = k_side[...].T[LANES - UCOLS :]
     for v in range(NV):
         a, b = ROW_U + v * UCOLS, ROW_L + v * LCOLS
-        strip[a : a + UCOLS, :] = u_side[1, v].T[LANES - UCOLS :]
-        strip[b : b + LCOLS, :] = l_side[1, v].T[LANES - LCOLS :]
-        a, b = a - ROW_K, b - ROW_K
-        wall[a : a + UCOLS, :] = u_side[0, v].T[:UCOLS]
-        wall[b : b + LCOLS, :] = l_side[0, v].T[:LCOLS]
-    for i, ref in enumerate((low, high)):
-        few = slice(0, UCOLS) if i == 0 else slice(SUB - UCOLS, SUB)
-        fewer = slice(0, LCOLS) if i == 0 else slice(SUB - LCOLS, SUB)
+        strip[a : a + UCOLS, :] = u_side[v].T[LANES - UCOLS :]
+        strip[b : b + LCOLS, :] = l_side[v].T[LANES - LCOLS :]
+    for i, ref in enumerate((near, far)):
+        last = lower if i == 0 else jnp.logical_not(lower)
+
+        def ends(x, count):
+            return jnp.where(last, x[SUB - count :], x[:count])
+
         for v in range(NV):
-            ref[v * UCOLS : (v + 1) * UCOLS, :] = u_edge[i, v, few, :]
-            ref[EDGE_L + v * LCOLS : EDGE_L + (v + 1) * LCOLS, :] = l_edge[i, v, fewer, :]
-        ref[EDGE_K:EDGE_W, :] = k_edge[i, few, :]
-        for j in range(tiles):
-            some = wall[min(j * WALL_ROWS, WALL) : min((j + 1) * WALL_ROWS, WALL), :]
-            if some.shape[0] < WALL_ROWS:
-                gap = jnp.zeros((WALL_ROWS - some.shape[0], rows), jnp.float32)
-                some = jnp.concatenate([some, gap], axis=0) if some.shape[0] else gap
-            ref[EDGE_W:EDGE, j * LANES : (j + 1) * LANES] = some
+            ref[v * UCOLS : (v + 1) * UCOLS, :] = ends(u_edge[i, v], UCOLS)
+            ref[EDGE_L + v * LCOLS : EDGE_L + (v + 1) * LCOLS, :] = ends(l_edge[i, v], LCOLS)
+        ref[EDGE_K:EDGE, :] = ends(k_edge[i], UCOLS)
 
 
 def pack(start_state, final_cotangent, diffusivity, donor_map, donor_weight):
     _, _, rows, radial = start_state.shape
     f32 = jnp.float32
-    outs = ((STRIP, rows), (WALL, rows), (EDGE, radial), (EDGE, radial))
+    outs = ((STRIP, rows), (EDGE, radial), (EDGE, radial))
     return pl.pallas_call(
         pack_kernel,
         in_specs=[pl.BlockSpec(memory_space=pltpu.HBM)] * 5,
-        out_specs=[pl.BlockSpec(memory_space=pltpu.VMEM)] * 4,
+        out_specs=[pl.BlockSpec(memory_space=pltpu.VMEM)] * 3,
         out_shape=[jax.ShapeDtypeStruct(s, f32) for s in outs],
         scratch_shapes=[
-            pltpu.VMEM((2, NV, rows, LANES), f32),
-            pltpu.VMEM((2, NV, rows, LANES), f32),
-            pltpu.VMEM((2, rows, LANES), f32),
+            pltpu.VMEM((NV, rows, LANES), f32),
+            pltpu.VMEM((NV, rows, LANES), f32),
+            pltpu.VMEM((rows, LANES), f32),
             pltpu.VMEM((2, NV, SUB, radial), f32),
             pltpu.VMEM((2, NV, SUB, radial), f32),
             pltpu.VMEM((2, SUB, radial), f32),
@@ -111,7 +102,12 @@
         ],
         compiler_params=params(),
         name="pack",
-    )(start_state, final_cotangent, diffusivity, donor_map, donor_weight)
+    )(
+        *(
+            pltpu.with_memory_space_constraint(x, pltpu.HBM)
+            for x in (start_state, final_cotangent, diffusivity, donor_map, donor_weight)
+        )
+    )
 
 
 def iota(shape, axis):
@@ -147,24 +143,28 @@
     return new
 
 
-def wall_kernel(own, before, after, c, proj, area, ids, dist, out, sides, *, devices):
-    rows, nodes = own.shape[1], area.shape[1]
-    for i, ref in enumerate((before, after)):
-        for j in range(-(-WALL // WALL_ROWS)):
-            a, b = j * WALL_ROWS, min((j + 1) * WALL_ROWS, WALL)
-            sides[i, a:b, :] = ref[EDGE_W : EDGE_W + b - a, j * LANES : (j + 1) * LANES]
-
-    def first(start, cols):
-        start = start - ROW_K
-        piece = jnp.concatenate(
-            [ref[start : start + cols, :] for ref in (sides.at[0], own, sides.at[1])], axis=1
-        )
-        pad = jnp.zeros((SUB - cols, piece.shape[1]), jnp.float32)
-        return jnp.concatenate([piece, pad], axis=0)
-
-    kappa = first(ROW_K, UCOLS)
-    u = [first(ROW_U + v * UCOLS, UCOLS) for v in range(NV)]
-    lam = [first(ROW_L + v * LCOLS, LCOLS) for v in range(NV)]
+def wall_kernel(
+    u_own, l_own, k_own, near, far, c_hbm, proj, area, ids, dist, out, c, sem, *, devices
+):
+    rows, nodes = u_own.shape[2], area.shape[1]
+    copy = pltpu.make_async_copy(c_hbm, c, sem)
+    copy.start()
+    lower = lax.axis_index("block") % 2 == 0
+    x, y = near[:, 0:LANES], far[:, 0:LANES]
+    gap = jnp.zeros((LANES - 2 * EDGE, LANES), jnp.float32)
+    halos = jnp.concatenate([jnp.where(lower, y, x), jnp.where(lower, x, y), gap], axis=0).T[:SUB]
+    lane = iota((SUB, LANES), 1)
+
+    def first(own, edge, cols):
+        after = pltpu.roll(halos, (LANES - EDGE - edge) % LANES, 1)
+        before = pltpu.roll(halos, (LANES - cols - edge) % LANES, 1)
+        beside = jnp.where(lane < cols, after, jnp.where(lane >= LANES - cols, before, 0.0))
+        return jnp.concatenate([own[:, :LANES].T[:SUB], beside], axis=1)
+
+    kappa = first(k_own.at[0], EDGE_K, UCOLS)
+    u = [first(u_own.at[v, 0], v * UCOLS, UCOLS) for v in range(NV)]
+    lam = [first(l_own.at[v, 0], EDGE_L + v * LCOLS, LCOLS) for v in range(NV)]
+    copy.wait()
     history = []
     for n in range(STEPS):
         t = [jnp.tanh(x) for x in u]
@@ -174,7 +174,7 @@
     h = [0.0] * NV
     for n in reversed(range(STEPS)):
         u, t = history[n]
-        h = [h[v] + (lam[v] * u[v])[0:1, rows : 2 * rows] for v in range(NV)]
+        h = [h[v] + (lam[v] * u[v])[0:1, :rows] for v in range(NV)]
         if n > 0:
             lam = strip_backward(lam, t, kappa, c)
     per_row = nodes // rows
@@ -201,7 +201,7 @@
         lo = (iota((LANES, nodes), 0) == minor[k : k + 1]).astype(bf)
         hit = target == major[k : k + 1][None]
         w = s * phi[k : k + 1]
-        for piece in range(3):
+        for piece in range(2):
             part = w.astype(bf).astype(jnp.float32)
             w = w - part
             a = jnp.where(hit, part[None], 0.0).reshape(devices * SUB, nodes).astype(bf)
@@ -211,18 +211,18 @@
     out[...] = total.reshape(devices, SUB, LANES)
 
 
-def wall_gradient(own, before, after, coupling, proj, area, ids, dist, devices):
+def wall_gradient(u, lam, kappa, near, far, coupling, proj, area, ids, dist, devices):
     vm = pl.BlockSpec(memory_space=pltpu.VMEM)
     sm = pl.BlockSpec(memory_space=pltpu.SMEM)
     return pl.pallas_call(
         functools.partial(wall_kernel, devices=devices),
-        in_specs=[vm, vm, vm, sm, sm, vm, vm, vm],
+        in_specs=[vm] * 5 + [pl.BlockSpec(memory_space=pltpu.HBM), sm, vm, vm, vm],
         out_specs=vm,
         out_shape=jax.ShapeDtypeStruct((devices, SUB, LANES), jnp.float32),
-        scratch_shapes=[pltpu.VMEM((2, WALL, own.shape[1]), jnp.float32)],
+        scratch_shapes=[pltpu.SMEM(coupling.shape, jnp.float32), pltpu.SemaphoreType.DMA],
         compiler_params=params(),
         name="wall_gradient",
-    )(own, before, after, coupling, proj, area, ids, dist)
+    )(u, lam, kappa, near, far, coupling, proj, area, ids, dist)
 
 
 def sum_kernel(parts, out):
@@ -245,16 +245,16 @@
     )(parts)
 
 
-def face_kernel(same, other, c, out, buf, turned, flip, *, rows):
+def face_terms(same, other, c, out, buf, turned, flip, rows, ready):
     block = lax.axis_index("block")
-    blocks = same.shape[0] // 2 * 2
+    blocks = 2 * same[0].shape[0]
     shape = (blocks, LANES)
     for m in range(blocks // 2):
         at = block ^ (2 * m)
         for q in range(2):
             start = q * STRIP * blocks
-            buf[pl.ds(start + at, STRIP, stride=blocks), :] = same[2 * m + q]
-            buf[pl.ds(start + (at ^ 1), STRIP, stride=blocks), :] = other[2 * m + q]
+            buf[pl.ds(start + at, STRIP, stride=blocks), :] = same[q][m]
+            buf[pl.ds(start + (at ^ 1), STRIP, stride=blocks), :] = other[q][m]
 
     def load(q, row):
         return buf[pl.ds((q * STRIP + row) * blocks, blocks), :]
@@ -270,16 +270,6 @@
     def earlier(x, by=1):
         y = jnp.where(lane < LANES - by, x, pltpu.roll(x, 1, 0))
         return pltpu.roll(y, by, 1)
-
-    def later_far(x, whole, rest):
-        near = pltpu.roll(x, (blocks - whole) % blocks, 0)
-        y = jnp.where(lane >= rest, near, pltpu.roll(near, blocks - 1, 0))
-        return pltpu.roll(y, (LANES - rest) % LANES, 1)
-
-    def earlier_far(x, whole, rest):
-        near = pltpu.roll(x, whole, 0)
-        y = jnp.where(lane < LANES - rest, near, pltpu.roll(near, 1, 0))
-        return pltpu.roll(y, rest, 1)
 
     far, taps = {}, {}
     for q in range(2):
@@ -303,28 +293,39 @@
                 for i in range(TAPS)
             ]
 
+    def shifts(q, n):
+        whole, rest = far[q, n]
+        return whole, [
+            (jnp.where(rest + i < LANES, rest + i, rest + i - LANES), lane >= rest + i,
+             lane >= rest + i - LANES)
+            for i in range(TAPS)
+        ]
+
     def ghost(q, n, faces):
+        whole, moves = shifts(q, n)
         result = []
         for f in faces:
-            f = later_far(f, *far[q, n])
-            after = pltpu.roll(f, blocks - 1, 0)
-            acc = taps[q, n][0] * f
-            for i in range(1, TAPS):
-                y = pltpu.roll(jnp.where(lane >= i, f, after), LANES - i, 1)
-                acc = acc + taps[q, n][i] * y
+            near = [pltpu.roll(f, (2 * blocks - whole - k) % blocks, 0) for k in range(3)]
+            acc = 0.0
+            for i, (by, here, next_one) in enumerate(moves):
+                y = jnp.where(here, near[0], jnp.where(next_one, near[1], near[2]))
+                acc = acc + taps[q, n][i] * pltpu.roll(y, (LANES - by) % LANES, 1)
             result.append(acc)
         return result
 
     def back(q, n, faces):
+        whole, moves = shifts(q, n)
         result = []
         for f in faces:
-            here = taps[q, n][0] * f
-            carried = jnp.zeros_like(here)
-            for i in range(1, TAPS):
-                y = pltpu.roll(taps[q, n][i] * f, i, 1)
-                here = here + jnp.where(lane >= i, y, 0.0)
-                carried = carried + jnp.where(lane < i, y, 0.0)
-            result.append(earlier_far(here + pltpu.roll(carried, 1, 0), *far[q, n]))
+            parts = [0.0, 0.0, 0.0]
+            for i, (by, here, next_one) in enumerate(moves):
+                y = pltpu.roll(taps[q, n][i] * f, by, 1)
+                parts[0] = parts[0] + jnp.where(here, y, 0.0)
+                parts[1] = parts[1] + jnp.where(here, 0.0, jnp.where(next_one, y, 0.0))
+                parts[2] = parts[2] + jnp.where(next_one, 0.0, y)
+            result.append(
+                sum(pltpu.roll(parts[k], (whole + k) % blocks, 0) for k in range(3))
+            )
         return result
 
     def emit(index, g):
@@ -343,6 +344,7 @@
         for q in range(2)
     ]
     history = {}
+    ready()
     for n in range(STEPS):
         first = n + 1 if n < STEPS - 1 else STEPS - 1
         for q in range(2):
@@ -409,29 +411,9 @@
         out[j * LANES : (j + 1) * LANES, :] = flip[:, j * LANES : (j + 1) * LANES].T
 
 
-def face_terms(same, other, coupling, rows):
-    vm = pl.BlockSpec(memory_space=pltpu.VMEM)
-    sm = pl.BlockSpec(memory_space=pltpu.SMEM)
-    blocks = same.shape[0]
-    f32 = jnp.float32
-    return pl.pallas_call(
-        functools.partial(face_kernel, rows=rows),
-        in_specs=[vm, vm, sm],
-        out_specs=vm,
-        out_shape=jax.ShapeDtypeStruct((2 * LANES, LANES), f32),
-        scratch_shapes=[
-            pltpu.VMEM((2 * STRIP * blocks, LANES), f32),
-            pltpu.VMEM(((2 * STEPS - 1) * SUB * blocks, LANES), f32),
-            pltpu.VMEM((LANES, 2 * LANES), f32),
-        ],
-        compiler_params=params(),
-        name="face_terms",
-    )(same, other, coupling)
-
-
 def field_kernel(
-    u_hbm, l_hbm, k_hbm, before, after, terms, c, out,
-    ext_u, ext_l, ext_k, kap, states, tanhs, lam, scaled, sems,
+    u_hbm, l_hbm, k_hbm, near, far, same_0, same_1, other_0, other_1, c_hbm, out,
+    c, ext_u, ext_l, ext_k, kap, rest, states, tanhs, lam, scaled, terms, buf, turned, flip, sems,
 ):
     rows, radial = u_hbm.shape[2], u_hbm.shape[3]
     chunks = kap.shape[0]
@@ -441,6 +423,8 @@
     def cut(j):
         return slice(j * LANES, (j + 1) * LANES)
 
+    c_copy = pltpu.make_async_copy(c_hbm, c, sems.at[4, 0])
+    c_copy.start()
     copies = []
     for j in range(tiles):
         lanes = pl.ds(j * LANES, LANES)
@@ -451,20 +435,26 @@
         ]
     for copy in copies:
         copy.start()
-    for ref, lower in ((before, True), (after, False)):
-        start = 0 if lower else HALO + rows
-        at = start + HALO - UCOLS if lower else start
-        below = start + HALO - LCOLS if lower else start
-        for j in range(tiles):
-            for v in range(NV):
-                ext_u[v, j, start : start + HALO] = jnp.zeros((HALO, LANES), jnp.float32)
-                ext_l[v, j, start : start + HALO] = jnp.zeros((HALO, LANES), jnp.float32)
-                ext_u[v, j, at : at + UCOLS] = ref[v * UCOLS : (v + 1) * UCOLS, cut(j)]
-                ext_l[v, j, below : below + LCOLS] = ref[
-                    EDGE_L + v * LCOLS : EDGE_L + (v + 1) * LCOLS, cut(j)
-                ]
-            ext_k[j, start : start + HALO] = jnp.zeros((HALO, LANES), jnp.float32)
-            ext_k[j, at : at + UCOLS] = ref[EDGE_K:EDGE_W, cut(j)]
+    face_terms(
+        (same_0, same_1), (other_0, other_1), c, terms, buf, turned, flip, rows, c_copy.wait
+    )
+    lower = lax.axis_index("block") % 2 == 0
+
+    def halo(a, b, cols):
+        x, y = near[a:b, cols], far[a:b, cols]
+        return jnp.where(lower, y, x), jnp.where(lower, x, y)
+
+    def put(ref, where, pair, count):
+        gap = jnp.zeros((HALO - count, LANES), jnp.float32)
+        ref[(*where, pl.ds(0, HALO))] = jnp.concatenate([gap, pair[0]], axis=0)
+        ref[(*where, pl.ds(HALO + rows, HALO))] = jnp.concatenate([pair[1], gap], axis=0)
+
+    for j in range(tiles):
+        put(ext_k, (j,), halo(EDGE_K, EDGE, cut(j)), UCOLS)
+        for v in range(NV):
+            put(ext_u, (v, j), halo(v * UCOLS, (v + 1) * UCOLS, cut(j)), UCOLS)
+            at = EDGE_L + v * LCOLS
+            put(ext_l, (v, j), halo(at, at + LCOLS, cut(j)), LCOLS)
     for copy in copies:
         copy.wait()
 
@@ -473,6 +463,7 @@
         for j in range(tiles):
             kappa = ext_k[j, at, :]
             kap[i, :, cut(j)] = kappa
+            rest[i, :, cut(j)] = 1.0 - 4.0 * kappa
             for v in range(NV):
                 states[0, v, i + 1, :, cut(j)] = ext_u[v, j, at, :]
                 x = ext_l[v, j, at, :]
@@ -521,30 +512,29 @@
                     tanhs[n, v, i, :, cut(j)] = t[v]
                     reaction = sum(c[v, w] * t[w] for w in range(NV))
                     states[n + 1, v, i + 1, :, cut(j)] = (
-                        x + kappa * (around - 4.0 * x) - reaction
+                        rest[i, :, cut(j)] * x + kappa * around - reaction
                     )
             return carry
 
-        lax.fori_loop(0, chunks, body, 0, unroll=6)
+        lax.fori_loop(0, chunks, body, 0, unroll=UNROLL)
         if n + 1 < STEPS - 1:
             wrap(states.at[n + 1])
 
-    def backward(n, source, target):
+    def backward(n, source, target, chosen):
         def body(i, carry):
             edge = edges(i, STEPS - 1 + n)
             cache = {}
             for j in range(tiles):
                 kappa = kap[i, :, cut(j)]
-                pairs = [neighbours(scaled.at[source], v, i, j, edge[v], cache) for v in range(NV)]
                 x = [lam[v, i, :, cut(j)] for v in range(NV)]
-                for v in range(NV):
+                for v in chosen:
+                    around, _ = neighbours(scaled.at[source], v, i, j, edge[v], cache)
                     if n < STEPS - 1:
                         t = tanhs[n, v, i, :, cut(j)]
                     else:
                         t = jnp.tanh(states[n, v, i + 1, :, cut(j)])
-                    around, s = pairs[v]
                     pulled = sum(c[w, v] * x[w] for w in range(NV))
-                    new = x[v] + (around - 4.0 * s) - (1.0 - t * t) * pulled
+                    new = rest[i, :, cut(j)] * x[v] + around - (1.0 - t * t) * pulled
                     if n > 0:
                         lam[v, i, :, cut(j)] = new
                         scaled[target, v, i + 1, :, cut(j)] = kappa * new
@@ -552,59 +542,68 @@
                         ext_l[v, j, pl.ds(i, SUB, stride=chunks), :] = new
             return carry
 
-        lax.fori_loop(0, chunks, body, 0, unroll=6)
+        lax.fori_loop(0, chunks, body, 0, unroll=UNROLL)
         if n > 0:
             wrap(scaled.at[target])
 
     for n in range(STEPS - 1):
         forward(n)
     source = 0
-    for n in reversed(range(STEPS)):
-        backward(n, source, 1 - source)
+    for n in reversed(range(1, STEPS)):
+        backward(n, source, 1 - source, range(NV))
         source = 1 - source
-    copies = [
-        pltpu.make_async_copy(
-            ext_l.at[:, j, own], out.at[:, 0, :, pl.ds(j * LANES, LANES)], sems.at[3, j]
-        )
-        for j in range(tiles)
-    ]
-    for copy in copies:
-        copy.start()
+    copies = []
+    for v in range(NV):
+        backward(0, source, 1 - source, (v,))
+        for j in range(tiles):
+            lanes = pl.ds(j * LANES, LANES)
+            copies.append(
+                pltpu.make_async_copy(
+                    ext_l.at[v, j, own], out.at[v, 0, :, lanes], sems.at[5 + v, j]
+                )
+            )
+            copies[-1].start()
     for copy in copies:
         copy.wait()
 
 
-def field(start_state, final_cotangent, diffusivity, before, after, terms, coupling):
+def field(start_state, final_cotangent, diffusivity, near, far, strips, coupling):
     _, _, rows, radial = start_state.shape
     ext = rows + 2 * HALO
-    chunks, tiles = ext // SUB, radial // LANES
+    chunks, tiles, blocks = ext // SUB, radial // LANES, 2 * strips[0].shape[0]
     vm = pl.BlockSpec(memory_space=pltpu.VMEM)
-    hbm = pl.BlockSpec(memory_space=pl.ANY)
+    hbm = pl.BlockSpec(memory_space=pltpu.HBM)
     f32 = jnp.float32
     return pl.pallas_call(
         field_kernel,
-        in_specs=[hbm, hbm, hbm, vm, vm, vm, pl.BlockSpec(memory_space=pltpu.SMEM)],
+        in_specs=[vm] * 9 + [hbm],
         out_specs=hbm,
         out_shape=jax.ShapeDtypeStruct(start_state.shape, f32),
         scratch_shapes=[
+            pltpu.SMEM(coupling.shape, f32),
             pltpu.VMEM((NV, tiles, ext, LANES), f32),
             pltpu.VMEM((NV, tiles, ext, LANES), f32),
             pltpu.VMEM((tiles, ext, LANES), f32),
+            pltpu.VMEM((chunks, SUB, radial), f32),
             pltpu.VMEM((chunks, SUB, radial), f32),
             pltpu.VMEM((STEPS, NV, chunks + 2, SUB, radial), f32),
             pltpu.VMEM((STEPS - 1, NV, chunks, SUB, radial), f32),
             pltpu.VMEM((NV, chunks, SUB, radial), f32),
             pltpu.VMEM((2, NV, chunks + 2, SUB, radial), f32),
-            pltpu.SemaphoreType.DMA((4, tiles)),
+            pltpu.VMEM((2 * LANES, LANES), f32),
+            pltpu.VMEM((2 * STRIP * blocks, LANES), f32),
+            pltpu.VMEM(((2 * STEPS - 1) * SUB * blocks, LANES), f32),
+            pltpu.VMEM((LANES, 2 * LANES), f32),
+            pltpu.SemaphoreType.DMA((5 + NV, tiles)),
         ],
         compiler_params=params(),
         name="field",
-    )(start_state, final_cotangent, diffusivity, before, after, terms, coupling)
-
-
-def ring(x, step):
+    )(start_state, final_cotangent, diffusivity, near, far, *strips, coupling)
+
+
+def beyond(x):
     size = lax.axis_size("block")
-    return lax.ppermute(x, "block", [(i, (i + step) % size) for i in range(size)])
+    return lax.ppermute(x, "block", [(i, (i + (1 if i % 2 else -1)) % size) for i in range(size)])
 
 
 def crossed(x, mask):
@@ -615,14 +614,17 @@
     return lax.ppermute(x, "zone", [(i, i ^ 1) for i in range(lax.axis_size("zone"))])
 
 
-def gather_pair(strip):
-    x = jnp.stack([strip, swapped(strip)])
+def gather_pair(strip, first):
+    x = strip[None]
     bit, size = 1, lax.axis_size("block")
     while 2**bit < size:
         wide = 4 if 2 ** (bit + 1) < size else 2
-        x = jnp.concatenate([x] + [crossed(x, k << bit) for k in range(1, wide)], axis=0)
+        pieces = [x] + [crossed(x, k << bit) for k in range(1, wide)]
+        *pieces, _ = lax.optimization_barrier((*pieces, first))
+        x = jnp.concatenate(pieces, axis=0)
         bit += 2 if wide == 4 else 1
-    return x, crossed(x, 1)
+    y = swapped(x)
+    return x, y, crossed(x, 1), crossed(y, 1)
 
 
 def local(
@@ -637,21 +639,21 @@
     center_ids,
     center_dist,
 ):
-    rows = start_state.shape[2]
     devices = lax.axis_size("zone") * lax.axis_size("block")
-    strip, wall, low, high = pack(
+    strip, near, far = pack(
         start_state, final_cotangent, diffusivity, donor_map, donor_weight
     )
-    before, after = ring(high, 1), ring(low, -1)
-    same, other = gather_pair(strip)
+    near, far = crossed(near, 1), beyond(far)
     points = wall_gradient(
-        wall, before, after, coupling, wall_projection, wall_area, center_ids, center_dist, devices
+        start_state, final_cotangent, diffusivity, near, far, coupling, wall_projection,
+        wall_area, center_ids, center_dist, devices,
     )
+    strips = gather_pair(strip, points)
     points = lax.all_to_all(points, ("zone", "block"), 0, 0, tiled=True)
-    gradient = sum_points(points)
-    terms = face_terms(same, other, coupling, rows)
-    adjoint = field(start_state, final_cotangent, diffusivity, before, after, terms, coupling)
-    return adjoint, gradient
+
+    adjoint = field(start_state, final_cotangent, diffusivity, near, far, strips, coupling)
+    adjoint, points = lax.optimization_barrier((adjoint, points))
+    return adjoint, sum_points(points)
 
 
 def solution(mesh):

time: 47 us -> 35.4 us (0.75)
  local copies, waits for them, and re-layouts: 8.18 us -> 0.05 us
  waiting for transfers between devices: 3.7 us -> 1.04 us
  Pallas kernels: 19.4 us -> 18 us
  starting transfers between devices: 14.5 us -> 15.2 us
    unnamed x30 -> x19, local copies, waits for them, and re-layouts: 7.55 us -> 0.05 us
    ppermute x4 -> x6, waiting for transfers between devices: 3.69 us -> 1.03 us  [crossed(): lax.ppermute(x, 'block', [(i, i ^ mask) for i in range(lax.axis_size('blo...]
    pallas_call x2 -> x1, Pallas kernels: 14.5 us -> 12 us  [field(): pl.pallas_call(field_kernel, in_specs=[vm] * 9 + [hbm], out_specs=hbm, ou...]
    ppermute x1, starting transfers between devices: 3 us -> 1.56 us  [swapped(): lax.ppermute(x, 'zone', [(i, i ^ 1) for i in range(lax.axis_size('zone'))])]
    ppermute x2 -> x1, starting transfers between devices: 3.54 us -> 4.71 us  [beyond(): lax.ppermute(x, 'block', [(i, (i + (1 if i % 2 else -1)) % size) for i in...]
    ppermute x4 -> x6, starting transfers between devices: 4.46 us -> 5.48 us  [crossed(): lax.ppermute(x, 'block', [(i, i ^ mask) for i in range(lax.axis_size('blo...]
    pallas_call x1, Pallas kernels: 0.94 us -> 1.78 us  [pack(): pl.pallas_call(pack_kernel, in_specs=[pl.BlockSpec(memory_space=pltpu.HBM...]
    concatenate x1, local copies, waits for them, and re-layouts: 0.63 us -> 0.01 us  [gather_pair(): x = jnp.concatenate(pieces, axis=0)]
  transfers between devices with their start and end apart: 8 -> 9, of which waited for: 2 -> 2; matrix products, arithmetic and copies ran while one was open for 7% -> 0% of each run, Pallas kernels for 38% -> 44%
where the time goes in v3:
time: 35.4 us; the launch traced here: 35.1 us
  Pallas kernels  18 us (51%)
  starting transfers between devices  15.2 us (43%)
  waiting for transfers between devices  1.04 us (3%)
  between operations  0.86 us (2%)
    pallas_call x1, Pallas kernels, field(): pl.pallas_call(field_kernel, in_specs=[vm] * 9 + [hbm], out_specs=hbm, ou...  12 us
    ppermute x6, starting transfers between devices, crossed(): lax.ppermute(x, 'block', [(i, i ^ mask) for i in range(lax.axis_size('blo...  5.48 us
    ppermute x1, starting transfers between devices, beyond(): lax.ppermute(x, 'block', [(i, (i + (1 if i % 2 else -1)) % size) for i in...  4.71 us
    pallas_call x1, Pallas kernels, wall_gradient(): pl.pallas_call(functools.partial(wall_kernel, devices=devices), in_specs=...  3.57 us
    all_to_all x1, starting transfers between devices, local(): points = lax.all_to_all(points, ('zone', 'block'), 0, 0, tiled=True)  3.42 us
    pallas_call x1, Pallas kernels, pack(): pl.pallas_call(pack_kernel, in_specs=[pl.BlockSpec(memory_space=pltpu.HBM...  1.78 us
    ppermute x1, starting transfers between devices, swapped(): lax.ppermute(x, 'zone', [(i, i ^ 1) for i in range(lax.axis_size('zone'))])  1.56 us
    ppermute x6, waiting for transfers between devices, crossed(): lax.ppermute(x, 'block', [(i, i ^ mask) for i in range(lax.axis_size('blo...  1.03 us
  transfers between devices with their start and end apart: 9, of which 2 were waited for; matrix products, arithmetic and copies ran while one was open for 0% of the time, Pallas kernels for 44%

profile of v3, /device:TPU:0, one launch (start us, length us, event | category | flops | bytes accessed | tf_op | source)
XLA Modules:
  0.0 35.1 jit_solution(13087438464199623933)
XLA Ops:
  0.6 0.0 copy-start.1
  0.6 0.0 copy-start.2
  0.7 1.8 %pack.1 = (f32[64,128]{1,0:T(8,128)S(1)}, f32[56,512]{1,0:T(8,128)S(1)}, f32[56,512]{1,0:T(8,128)S(1)}) custom-call(f32[5,1,128,512]{3,2,1,0:T(8,128)} %u_hbm.3, f32[5,1,128,512]{3,2,1,0:T(8,128)} %l_hbm.3, f32[1,128,512]{2,1,0:T(8,128)} %k_hbm.3, s32[4,1,1024]{2,1,0:T(1,128)} %map_hbm.1, f32[4,1,1024]{2,1,0:T(1,128)} %weight_hbm.1), custom_call_target="tpu_custom_call" | custom-call | tf_op jit(solution)/shard_map/pack/pallas_call | solution.py:87
  2.5 0.5 %collective-permute-start = (f32[56,512]{1,0:T(8,128)S(1)}, f32[56,512]{1,0:T(8,128)S(1)}, u32[]{:S(2)}, u32[]{:S(2)}) collective-permute-start(f32[56,512]{1,0:T(8,128)S(1)} %get-tuple-element.11), channel_id=1, source_target_pairs={{0,1},{1,0},{2,3},{3,2},{4,5},{5,4},{6,7},{7,6},{8,9},{9,8},{10,11... | collective-permute-start | bytes 344072 | tf_op jit(solution)/shard_map/ppermute | solution.py:610
  3.0 4.7 %collective-permute-start.1 = (f32[56,512]{1,0:T(8,128)S(1)}, f32[56,512]{1,0:T(8,128)S(1)}, u32[]{:S(2)}, u32[]{:S(2)}) collective-permute-start(f32[56,512]{1,0:T(8,128)S(1)} %get-tuple-element.12), channel_id=1, source_target_pairs={{0,7},{1,2},{2,1},{3,4},{4,3},{5,6},{6,5},{7,0},{8,15},{9,10},{10,... | collective-permute-start | bytes 344072 | tf_op jit(solution)/shard_map/ppermute | solution.py:606
  7.7 0.4 %collective-permute-start.4 = (f32[1,64,128]{2,1,0:T(8,128)S(1)}, f32[1,64,128]{2,1,0:T(8,128)S(1)}, u32[]{:S(2)}, u32[]{:S(2)}) collective-permute-start(f32[1,64,128]{2,1,0:T(8,128)S(1)} %bitcast.1), channel_id=1, source_target_pairs={{0,6},{1,7},{2,4},{3,5},{4,2},{5,3},{6,0},{7,1},{8,14},{9,15},{10,... | collective-permute-start | bytes 98312 | tf_op jit(solution)/shard_map/ppermute | solution.py:610
  8.2 0.0 collective-permute-start.3
  8.2 3.9 %collective-permute-start.2 = (f32[1,64,128]{2,1,0:T(8,128)S(1)}, f32[1,64,128]{2,1,0:T(8,128)S(1)}, u32[]{:S(2)}, u32[]{:S(2)}) collective-permute-start(f32[1,64,128]{2,1,0:T(8,128)S(1)} %bitcast.3), channel_id=1, source_target_pairs={{0,2},{1,3},{2,0},{3,1},{4,6},{5,7},{6,4},{7,5},{8,10},{9,11},{10,... | collective-permute-start | bytes 98312 | tf_op jit(solution)/shard_map/ppermute | solution.py:610
  12.1 0.0 collective-permute-done.near
  12.1 0.0 collective-permute-done.1.far
  12.2 3.6 %wall_gradient.1 = f32[32,8,128]{2,1,0:T(8,128)} custom-call(f32[5,1,128,512]{3,2,1,0:T(8,128)S(1)} %copy-done, f32[5,1,128,512]{3,2,1,0:T(8,128)S(1)} %copy-done.1, f32[1,128,512]{2,1,0:T(8,128)S(1)} %copy-done.2, f32[56,512]{1,0:T(8,128)S(1)} %collective-permute-done.near, f32[56,512]{1,0:T(8,128)S(1)} %collective-permute-done.1.far, ...), custom_call_target="tpu_custom_call" | custom-call | tf_op jit(solution)/shard_map/wall_gradient/pallas_call | solution.py:217
  15.8 0.0 collective-permute-done.4
  15.8 0.0 collective-permute-done.3
  15.8 0.0 collective-permute-done.2
  15.9 1.6 %collective-permute-start.5 = (f32[4,64,128]{2,1,0:T(8,128)S(1)}, f32[4,64,128]{2,1,0:T(8,128)S(1)}, u32[]{:S(2)}, u32[]{:S(2)}) collective-permute-start(f32[4,64,128]{2,1,0:T(8,128)S(1)} %constant_dynamic-update-slice_fusion.same_0), channel_id=1, source_target_pairs={{0,8},{8,0},{16,24},{24,16},{1,9},{9,1},{17,25},{25,17},{2,10},{10... | collective-permute-start | bytes 393224 | tf_op jit(solution)/shard_map/ppermute | solution.py:614
  17.4 3.4 %all-to-all-start = ((f32[32,8,128]{2,1,0:T(8,128)}), f32[32,8,128]{2,1,0:T(8,128)S(1)}, u32[]{:S(2)}, u32[]{:S(2)}) async-start(f32[32,8,128]{2,1,0:T(8,128)} %wall_gradient.1), calls=%async_computation | async-start | bytes 262144 | tf_op jit(solution)/shard_map/all_to_all | solution.py:652
  20.9 0.1 collective-permute-start.6
  21.0 0.0 collective-permute-done.5.same_1
  21.0 0.4 %collective-permute-start.7 = (f32[4,64,128]{2,1,0:T(8,128)S(1)}, f32[4,64,128]{2,1,0:T(8,128)S(1)}, u32[]{:S(2)}, u32[]{:S(2)}) collective-permute-start(f32[4,64,128]{2,1,0:T(8,128)S(1)} %collective-permute-done.5.same_1), channel_id=1, source_target_pairs={{0,1},{1,0},{2,3},{3,2},{4,5},{5,4},{6,7},{7,6},{8,9},{9,8},{10,11... | collective-permute-start | bytes 393224 | tf_op jit(solution)/shard_map/ppermute | solution.py:610
  21.4 0.8 %collective-permute-done.6.other_0 = f32[4,64,128]{2,1,0:T(8,128)S(1)} collective-permute-done((f32[4,64,128]{2,1,0:T(8,128)S(1)}, f32[4,64,128]{2,1,0:T(8,128)S(1)}, u32[]{:S(2)}, u32[]{:S(2)}) %collective-permute-start.6) | collective-permute-done | bytes 131104 | tf_op jit(solution)/shard_map/ppermute | solution.py:610
  22.3 0.2 collective-permute-done.7.other_1
  22.5 12.0 %field.1 = f32[5,1,128,512]{3,2,1,0:T(8,128)} custom-call(f32[5,1,128,512]{3,2,1,0:T(8,128)S(1)} %copy-done, f32[5,1,128,512]{3,2,1,0:T(8,128)S(1)} %copy-done.1, f32[1,128,512]{2,1,0:T(8,128)S(1)} %copy-done.2, f32[56,512]{1,0:T(8,128)S(1)} %collective-permute-done.near, f32[56,512]{1,0:T(8,128)S(1)} %collective-permute-done.1.far, ...), custom_call_target="tpu_custom_call" | custom-call | tf_op jit(solution)/shard_map/field/pallas_call | solution.py:577
  34.5 0.0 all-to-all-done.parts
  34.5 0.6 %sum_points.1 = f32[3,256]{1,0:T(4,128)} custom-call(f32[32,8,128]{2,1,0:T(8,128)S(1)} %all-to-all-done.parts), custom_call_target="tpu_custom_call" | custom-call | tf_op jit(solution)/shard_map/sum_points/pallas_call | solution.py:238
  (18 shorter events, 0.0 us)
Async XLA Ops:
  0.6 11.5 %copy-start.1 = (f32[5,1,128,512]{3,2,1,0:T(8,128)S(1)}, f32[5,1,128,512]{3,2,1,0:T(8,128)}, u32[]{:S(2)}) copy-start(f32[5,1,128,512]{3,2,1,0:T(8,128)} %l_hbm.3) | copy-start | bytes 3932164
  0.6 11.5 %copy-start.2 = (f32[1,128,512]{2,1,0:T(8,128)S(1)}, f32[1,128,512]{2,1,0:T(8,128)}, u32[]{:S(2)}) copy-start(f32[1,128,512]{2,1,0:T(8,128)} %k_hbm.3) | copy-start | bytes 786436
  0.7 11.5 %copy-start = (f32[5,1,128,512]{3,2,1,0:T(8,128)S(1)}, f32[5,1,128,512]{3,2,1,0:T(8,128)}, u32[]{:S(2)}) copy-start(f32[5,1,128,512]{3,2,1,0:T(8,128)} %u_hbm.3) | copy-start | bytes 3932164
  0.7 11.5 %copy-start.3 = (f32[5,5]{1,0:T(8,128)S(1)}, f32[5,5]{1,0:T(8,128)}, u32[]{:S(2)}) copy-start(f32[5,5]{1,0:T(8,128)} %c_hbm.3) | copy-start | bytes 304
  0.7 11.5 %copy-start.5 = (f32[1,8,384]{2,1,0:T(8,128)S(1)}, f32[1,8,384]{2,1,0:T(8,128)}, u32[]{:S(2)}) copy-start(f32[1,8,384]{2,1,0:T(8,128)} %dist.1) | copy-start | bytes 36868
  0.7 11.5 %copy-start.4 = (s32[1,8,384]{2,1,0:T(8,128)S(1)}, s32[1,8,384]{2,1,0:T(8,128)}, u32[]{:S(2)}) copy-start(s32[1,8,384]{2,1,0:T(8,128)} %ids.1) | copy-start | bytes 36868
  0.7 11.5 %copy-start.6 = (f32[3,5]{1,0:T(4,128)S(1)}, f32[3,5]{1,0:T(4,128)}, u32[]{:S(2)}) copy-start(f32[3,5]{1,0:T(4,128)} %proj.1) | copy-start | bytes 184
  0.7 11.5 %copy-start.7 = (f32[1,384]{1,0:T(1,128)S(1)}, f32[1,384]{1,0:T(1,128)}, u32[]{:S(2)}) copy-start(f32[1,384]{1,0:T(1,128)} %area.1) | copy-start | bytes 4612
  2.5 9.6 %collective-permute-start = (f32[56,512]{1,0:T(8,128)S(1)}, f32[56,512]{1,0:T(8,128)S(1)}, u32[]{:S(2)}, u32[]{:S(2)}) collective-permute-start(f32[56,512]{1,0:T(8,128)S(1)} %get-tuple-element.11), channel_id=1, source_target_pairs={{0,1},{1,0},{2,3},{3,2},{4,5},{5,4},{6,7},{7,6},{8,9},{9,8},{10,11... | collective-permute-start | bytes 344072 | tf_op jit(solution)/shard_map/ppermute | solution.py:610
  3.0 9.1 %collective-permute-start.1 = (f32[56,512]{1,0:T(8,128)S(1)}, f32[56,512]{1,0:T(8,128)S(1)}, u32[]{:S(2)}, u32[]{:S(2)}) collective-permute-start(f32[56,512]{1,0:T(8,128)S(1)} %get-tuple-element.12), channel_id=1, source_target_pairs={{0,7},{1,2},{2,1},{3,4},{4,3},{5,6},{6,5},{7,0},{8,15},{9,10},{10,... | collective-permute-start | bytes 344072 | tf_op jit(solution)/shard_map/ppermute | solution.py:606
  7.7 8.1 %collective-permute-start.4 = (f32[1,64,128]{2,1,0:T(8,128)S(1)}, f32[1,64,128]{2,1,0:T(8,128)S(1)}, u32[]{:S(2)}, u32[]{:S(2)}) collective-permute-start(f32[1,64,128]{2,1,0:T(8,128)S(1)} %bitcast.1), channel_id=1, source_target_pairs={{0,6},{1,7},{2,4},{3,5},{4,2},{5,3},{6,0},{7,1},{8,14},{9,15},{10,... | collective-permute-start | bytes 98312 | tf_op jit(solution)/shard_map/ppermute | solution.py:610
  8.2 7.6 %collective-permute-start.3 = (f32[1,64,128]{2,1,0:T(8,128)S(1)}, f32[1,64,128]{2,1,0:T(8,128)S(1)}, u32[]{:S(2)}, u32[]{:S(2)}) collective-permute-start(f32[1,64,128]{2,1,0:T(8,128)S(1)} %bitcast.2), channel_id=1, source_target_pairs={{0,4},{1,5},{2,6},{3,7},{4,0},{5,1},{6,2},{7,3},{8,12},{9,13},{10,... | collective-permute-start | bytes 98312 | tf_op jit(solution)/shard_map/ppermute | solution.py:610
  8.2 7.6 %collective-permute-start.2 = (f32[1,64,128]{2,1,0:T(8,128)S(1)}, f32[1,64,128]{2,1,0:T(8,128)S(1)}, u32[]{:S(2)}, u32[]{:S(2)}) collective-permute-start(f32[1,64,128]{2,1,0:T(8,128)S(1)} %bitcast.3), channel_id=1, source_target_pairs={{0,2},{1,3},{2,0},{3,1},{4,6},{5,7},{6,4},{7,5},{8,10},{9,11},{10,... | collective-permute-start | bytes 98312 | tf_op jit(solution)/shard_map/ppermute | solution.py:610
  15.9 5.1 %collective-permute-start.5 = (f32[4,64,128]{2,1,0:T(8,128)S(1)}, f32[4,64,128]{2,1,0:T(8,128)S(1)}, u32[]{:S(2)}, u32[]{:S(2)}) collective-permute-start(f32[4,64,128]{2,1,0:T(8,128)S(1)} %constant_dynamic-update-slice_fusion.same_0), channel_id=1, source_target_pairs={{0,8},{8,0},{16,24},{24,16},{1,9},{9,1},{17,25},{25,17},{2,10},{10... | collective-permute-start | bytes 393224 | tf_op jit(solution)/shard_map/ppermute | solution.py:614
  17.4 17.1 %all-to-all-start = ((f32[32,8,128]{2,1,0:T(8,128)}), f32[32,8,128]{2,1,0:T(8,128)S(1)}, u32[]{:S(2)}, u32[]{:S(2)}) async-start(f32[32,8,128]{2,1,0:T(8,128)} %wall_gradient.1), calls=%async_computation | async-start | bytes 262144 | tf_op jit(solution)/shard_map/all_to_all | solution.py:652
  20.9 1.4 %collective-permute-start.6 = (f32[4,64,128]{2,1,0:T(8,128)S(1)}, f32[4,64,128]{2,1,0:T(8,128)S(1)}, u32[]{:S(2)}, u32[]{:S(2)}) collective-permute-start(f32[4,64,128]{2,1,0:T(8,128)S(1)} %constant_dynamic-update-slice_fusion.same_0), channel_id=1, source_target_pairs={{0,1},{1,0},{2,3},{3,2},{4,5},{5,4},{6,7},{7,6},{8,9},{9,8},{10,11... | collective-permute-start | bytes 393224 | tf_op jit(solution)/shard_map/ppermute | solution.py:610
  21.0 1.5 %collective-permute-start.7 = (f32[4,64,128]{2,1,0:T(8,128)S(1)}, f32[4,64,128]{2,1,0:T(8,128)S(1)}, u32[]{:S(2)}, u32[]{:S(2)}) collective-permute-start(f32[4,64,128]{2,1,0:T(8,128)S(1)} %collective-permute-done.5.same_1), channel_id=1, source_target_pairs={{0,1},{1,0},{2,3},{3,2},{4,5},{5,4},{6,7},{7,6},{8,9},{9,8},{10,11... | collective-permute-start | bytes 393224 | tf_op jit(solution)/shard_map/ppermute | solution.py:610

commit v4 on v3

--- a/solution.py
+++ b/solution.py
@@ -23,7 +23,6 @@
 EDGE_K = EDGE_L + NV * LCOLS
 EDGE = EDGE_K + UCOLS
 TAPS = 6
-UNROLL = 18
 VMEM_LIMIT = 48 * 1024 * 1024
 
 
@@ -33,13 +32,13 @@
 
 def pack_kernel(
     u_hbm, l_hbm, k_hbm, map_hbm, weight_hbm, strip, near, far,
-    u_side, l_side, k_side, u_edge, l_edge, k_edge, dmap, dweight, sems,
+    u_side, l_side, k_side, u_edge, l_edge, k_edge, dmap, dweight, near_offset, sems,
 ):
     rows, radial = u_hbm.shape[2], u_hbm.shape[3]
     block = lax.axis_index("block")
     own = pl.ds(pl.multiple_of(block * rows, LANES), rows)
     copies = [
-        pltpu.make_async_copy(map_hbm.at[:, 0, own], dmap, sems.at[0, 0]),
+        pltpu.make_async_copy(map_hbm.at[:, 0], dmap, sems.at[0, 0]),
         pltpu.make_async_copy(weight_hbm.at[:, 0, own], dweight, sems.at[0, 1]),
     ]
     lanes = pl.ds(radial - LANES, LANES)
@@ -61,9 +60,23 @@
         copy.start()
     for copy in copies:
         copy.wait()
-    strip[0:STEPS, :] = dmap[...].astype(jnp.float32)
+    size = dmap.shape[1]
+    delta = dmap[...] - iota(dmap.shape, 1)
+    delta = jnp.where(delta < 0, delta + size, delta)
+    ahead = delta - delta[:, 0:1] + STEPS
+    ahead = jnp.where(ahead < 0, ahead + size, ahead)
+    ahead = jnp.where(ahead >= size, ahead - size, ahead).astype(jnp.float32)
+    least = jnp.min(ahead, axis=1, keepdims=True)
+    offset = delta[:, 0:1].astype(jnp.float32) - float(STEPS) + least
+    offset = jnp.where(offset < 0.0, offset + float(size), offset)
+    offset = jnp.where(offset >= float(size), offset - float(size), offset)
+    near_offset[...] = ahead - least
+    strip[0:STEPS, :] = near_offset[:, own]
+    which = iota((STEPS, rows), 1) == iota((STEPS, rows), 0)
+    offsets = jnp.sum(jnp.where(which, offset, 0.0), axis=0, keepdims=True)
     strip[STEPS : 2 * STEPS, :] = dweight[...]
-    strip[ROW_K : ROW_K + UCOLS, :] = k_side[...].T[LANES - UCOLS :]
+    strip[ROW_K : ROW_K + 1, :] = offsets
+    strip[ROW_K + 1 : ROW_K + UCOLS, :] = k_side[...].T[LANES - UCOLS + 1 :]
     for v in range(NV):
         a, b = ROW_U + v * UCOLS, ROW_L + v * LCOLS
         strip[a : a + UCOLS, :] = u_side[v].T[LANES - UCOLS :]
@@ -96,8 +109,9 @@
             pltpu.VMEM((2, NV, SUB, radial), f32),
             pltpu.VMEM((2, NV, SUB, radial), f32),
             pltpu.VMEM((2, SUB, radial), f32),
-            pltpu.VMEM((STEPS, rows), jnp.int32),
+            pltpu.VMEM((STEPS, donor_map.shape[2]), jnp.int32),
             pltpu.VMEM((STEPS, rows), f32),
+            pltpu.VMEM((STEPS, donor_map.shape[2]), f32),
             pltpu.SemaphoreType.DMA((7, 2)),
         ],
         compiler_params=params(),
@@ -144,11 +158,11 @@
 
 
 def wall_kernel(
-    u_own, l_own, k_own, near, far, c_hbm, proj, area, ids, dist, out, c, sem, *, devices
+    u_own, l_own, k_own, near, far, c_ref, proj_ref, area, ids, dist, out, *, devices
 ):
     rows, nodes = u_own.shape[2], area.shape[1]
-    copy = pltpu.make_async_copy(c_hbm, c, sem)
-    copy.start()
+    c = {(v, w): c_ref[v : v + 1, w : w + 1] for v in range(NV) for w in range(NV)}
+    proj = {(i, v): proj_ref[i : i + 1, v : v + 1] for i in range(3) for v in range(NV)}
     lower = lax.axis_index("block") % 2 == 0
     x, y = near[:, 0:LANES], far[:, 0:LANES]
     gap = jnp.zeros((LANES - 2 * EDGE, LANES), jnp.float32)
@@ -164,7 +178,6 @@
     kappa = first(k_own.at[0], EDGE_K, UCOLS)
     u = [first(u_own.at[v, 0], v * UCOLS, UCOLS) for v in range(NV)]
     lam = [first(l_own.at[v, 0], EDGE_L + v * LCOLS, LCOLS) for v in range(NV)]
-    copy.wait()
     history = []
     for n in range(STEPS):
         t = [jnp.tanh(x) for x in u]
@@ -179,8 +192,9 @@
             lam = strip_backward(lam, t, kappa, c)
     per_row = nodes // rows
     groups = CP_DEV // LANES
-    s_rows = [sum(proj[i // groups, v] * h[v] for v in range(NV)) for i in range(3 * groups)]
-    s_rows += [jnp.zeros((SUB - 3 * groups, rows), jnp.float32)]
+    components = [sum(proj[i, v] * h[v] for v in range(NV)) for i in range(3)]
+    components += [jnp.zeros((SUB // groups - 3, rows), jnp.float32)]
+    s_rows = components * groups
     spread = (iota((rows, nodes), 1) // per_row == iota((rows, nodes), 0)).astype(jnp.float32)
     s = jnp.dot(
         jnp.concatenate(s_rows, axis=0), spread,
@@ -194,7 +208,7 @@
     key = ids[0]
     major, minor = key // LANES, key % LANES
     shape = (devices, SUB, nodes)
-    target = iota(shape, 0) * groups + iota(shape, 1) % groups
+    target = iota(shape, 0) * groups + iota(shape, 1) // (SUB // groups)
     total = jnp.zeros((devices * SUB, LANES), jnp.float32)
     bf = jnp.bfloat16
     for k in range(d.shape[0]):
@@ -208,41 +222,22 @@
             total += lax.dot_general(
                 a, lo, (((1,), (1,)), ((), ())), preferred_element_type=jnp.float32
             )
-    out[...] = total.reshape(devices, SUB, LANES)
+    total = total.reshape(devices, SUB, LANES)
+    for g in range(groups):
+        start = g * (SUB // groups)
+        out[:, :, g * LANES : (g + 1) * LANES] = total[:, start : start + 3]
 
 
 def wall_gradient(u, lam, kappa, near, far, coupling, proj, area, ids, dist, devices):
     vm = pl.BlockSpec(memory_space=pltpu.VMEM)
-    sm = pl.BlockSpec(memory_space=pltpu.SMEM)
     return pl.pallas_call(
         functools.partial(wall_kernel, devices=devices),
-        in_specs=[vm] * 5 + [pl.BlockSpec(memory_space=pltpu.HBM), sm, vm, vm, vm],
+        in_specs=[vm] * 10,
         out_specs=vm,
-        out_shape=jax.ShapeDtypeStruct((devices, SUB, LANES), jnp.float32),
-        scratch_shapes=[pltpu.SMEM(coupling.shape, jnp.float32), pltpu.SemaphoreType.DMA],
+        out_shape=jax.ShapeDtypeStruct((devices, 3, CP_DEV), jnp.float32),
         compiler_params=params(),
         name="wall_gradient",
     )(u, lam, kappa, near, far, coupling, proj, area, ids, dist)
-
-
-def sum_kernel(parts, out):
-    total = parts[...].sum(axis=0)
-    groups = CP_DEV // LANES
-    for i in range(3 * groups):
-        c, g = i // groups, i % groups
-        out[c : c + 1, g * LANES : (g + 1) * LANES] = total[i : i + 1]
-
-
-def sum_points(parts):
-    vm = pl.BlockSpec(memory_space=pltpu.VMEM)
-    return pl.pallas_call(
-        sum_kernel,
-        in_specs=[vm],
-        out_specs=vm,
-        out_shape=jax.ShapeDtypeStruct((3, CP_DEV), jnp.float32),
-        compiler_params=params(),
-        name="sum_points",
-    )(parts)
 
 
 def face_terms(same, other, c, out, buf, turned, flip, rows, ready):
@@ -260,8 +255,6 @@
         return buf[pl.ds((q * STRIP + row) * blocks, blocks), :]
 
     lane = iota(shape, 1)
-    place = (iota(shape, 0) * LANES + lane).astype(jnp.float32)
-    size = float(blocks * rows)
 
     def later(x, by=1):
         y = jnp.where(lane >= by, x, pltpu.roll(x, blocks - 1, 0))
@@ -274,18 +267,9 @@
     far, taps = {}, {}
     for q in range(2):
         for n in range(STEPS):
-            delta = load(q, n) - place
-            delta = jnp.where(delta < 0.0, delta + size, delta)
-            start = delta[0:1, 0:1]
-            rel = delta - start + float(STEPS)
-            rel = jnp.where(rel < 0.0, rel + size, rel)
-            rel = jnp.where(rel >= size, rel - size, rel)
-            least = jnp.min(jnp.min(rel, axis=0, keepdims=True), axis=1, keepdims=True)
-            e = rel - least
-            t = start - float(STEPS) + least
-            t = jnp.where(t < 0.0, t + size, t)
-            t = jnp.where(t >= size, t - size, t).astype(jnp.int32)[0, 0]
+            t = load(q, ROW_K)[0:1, n : n + 1].astype(jnp.int32)[0, 0]
             far[q, n] = (t // LANES, t % LANES)
+            e = load(q, n)
             share = load(q, STEPS + n)
             taps[q, n] = [
                 jnp.where(e == float(i), share, 0.0)
@@ -516,7 +500,7 @@
                     )
             return carry
 
-        lax.fori_loop(0, chunks, body, 0, unroll=UNROLL)
+        lax.fori_loop(0, chunks, body, 0, unroll=chunks)
         if n + 1 < STEPS - 1:
             wrap(states.at[n + 1])
 
@@ -542,7 +526,7 @@
                         ext_l[v, j, pl.ds(i, SUB, stride=chunks), :] = new
             return carry
 
-        lax.fori_loop(0, chunks, body, 0, unroll=UNROLL)
+        lax.fori_loop(0, chunks, body, 0, unroll=chunks)
         if n > 0:
             wrap(scaled.at[target])
 
@@ -653,7 +637,7 @@
 
     adjoint = field(start_state, final_cotangent, diffusivity, near, far, strips, coupling)
     adjoint, points = lax.optimization_barrier((adjoint, points))
-    return adjoint, sum_points(points)
+    return adjoint, points.sum(axis=0)
 
 
 def solution(mesh):

time: 35.4 us -> 33.5 us (0.946)
  Pallas kernels: 18 us -> 15.6 us
  other arithmetic: 0 us -> 0.64 us
    pallas_call x1, Pallas kernels: 12 us -> 11.1 us  [field(): pl.pallas_call(field_kernel, in_specs=[vm] * 9 + [hbm], out_specs=hbm, ou...]
    pallas_call x1, Pallas kernels: 3.57 us -> 2.67 us  [wall_gradient(): pl.pallas_call(functools.partial(wall_kernel, devices=devices), in_specs=...]
    reduce_sum x0 -> x1, other arithmetic: none -> 0.64 us  [local(): return (adjoint, points.sum(axis=0))]
    pallas_call x1 -> x0, Pallas kernels: 0.63 us -> none  [sum_points(): pl.pallas_call(sum_kernel, in_specs=[vm], out_specs=vm, out_shape=jax.Sha...]
  transfers between devices with their start and end apart: 9 -> 9, of which waited for: 2 -> 2; matrix products, arithmetic and copies ran while one was open for 0% -> 0% of each run, Pallas kernels for 44% -> 41%
where the time goes in v4:
time: 33.5 us; the launch traced here: 33.3 us
  Pallas kernels  15.6 us (47%)
  starting transfers between devices  15.2 us (45%)
  waiting for transfers between devices  1.04 us (3%)
  between operations  0.83 us (2%)
  other arithmetic  0.64 us (2%)
    pallas_call x1, Pallas kernels, field(): pl.pallas_call(field_kernel, in_specs=[vm] * 9 + [hbm], out_specs=hbm, ou...  11.1 us
    ppermute x6, starting transfers between devices, crossed(): lax.ppermute(x, 'block', [(i, i ^ mask) for i in range(lax.axis_size('blo...  5.48 us
    ppermute x1, starting transfers between devices, beyond(): lax.ppermute(x, 'block', [(i, (i + (1 if i % 2 else -1)) % size) for i in...  4.71 us
    all_to_all x1, starting transfers between devices, local(): points = lax.all_to_all(points, ('zone', 'block'), 0, 0, tiled=True)  3.42 us
    pallas_call x1, Pallas kernels, wall_gradient(): pl.pallas_call(functools.partial(wall_kernel, devices=devices), in_specs=...  2.67 us
    pallas_call x1, Pallas kernels, pack(): pl.pallas_call(pack_kernel, in_specs=[pl.BlockSpec(memory_space=pltpu.HBM...  1.85 us
    ppermute x1, starting transfers between devices, swapped(): lax.ppermute(x, 'zone', [(i, i ^ 1) for i in range(lax.axis_size('zone'))])  1.56 us
    ppermute x6, waiting for transfers between devices, crossed(): lax.ppermute(x, 'block', [(i, i ^ mask) for i in range(lax.axis_size('blo...  1.03 us
  transfers between devices with their start and end apart: 9, of which 2 were waited for; matrix products, arithmetic and copies ran while one was open for 0% of the time, Pallas kernels for 41%

profile of v4, /device:TPU:0, one launch (start us, length us, event | category | flops | bytes accessed | tf_op | source)
XLA Modules:
  0.0 33.3 jit_solution(12314883906840862637)
XLA Ops:
  0.6 0.0 copy-start.1
  0.6 0.0 copy-start.2
  0.7 1.8 %pack.1 = (f32[64,128]{1,0:T(8,128)S(1)}, f32[56,512]{1,0:T(8,128)S(1)}, f32[56,512]{1,0:T(8,128)S(1)}) custom-call(f32[5,1,128,512]{3,2,1,0:T(8,128)} %u_hbm.3, f32[5,1,128,512]{3,2,1,0:T(8,128)} %l_hbm.3, f32[1,128,512]{2,1,0:T(8,128)} %k_hbm.3, s32[4,1,1024]{2,1,0:T(1,128)} %map_hbm.1, f32[4,1,1024]{2,1,0:T(1,128)} %weight_hbm.1), custom_call_target="tpu_custom_call" | custom-call | tf_op jit(solution)/shard_map/pack/pallas_call | solution.py:100
  2.6 0.5 %collective-permute-start = (f32[56,512]{1,0:T(8,128)S(1)}, f32[56,512]{1,0:T(8,128)S(1)}, u32[]{:S(2)}, u32[]{:S(2)}) collective-permute-start(f32[56,512]{1,0:T(8,128)S(1)} %get-tuple-element.11), channel_id=1, source_target_pairs={{0,1},{1,0},{2,3},{3,2},{4,5},{5,4},{6,7},{7,6},{8,9},{9,8},{10,11... | collective-permute-start | bytes 344072 | tf_op jit(solution)/shard_map/ppermute | solution.py:594
  3.1 4.7 %collective-permute-start.1 = (f32[56,512]{1,0:T(8,128)S(1)}, f32[56,512]{1,0:T(8,128)S(1)}, u32[]{:S(2)}, u32[]{:S(2)}) collective-permute-start(f32[56,512]{1,0:T(8,128)S(1)} %get-tuple-element.12), channel_id=1, source_target_pairs={{0,7},{1,2},{2,1},{3,4},{4,3},{5,6},{6,5},{7,0},{8,15},{9,10},{10,... | collective-permute-start | bytes 344072 | tf_op jit(solution)/shard_map/ppermute | solution.py:590
  7.8 0.4 %collective-permute-start.4 = (f32[1,64,128]{2,1,0:T(8,128)S(1)}, f32[1,64,128]{2,1,0:T(8,128)S(1)}, u32[]{:S(2)}, u32[]{:S(2)}) collective-permute-start(f32[1,64,128]{2,1,0:T(8,128)S(1)} %bitcast.1), channel_id=1, source_target_pairs={{0,6},{1,7},{2,4},{3,5},{4,2},{5,3},{6,0},{7,1},{8,14},{9,15},{10,... | collective-permute-start | bytes 98312 | tf_op jit(solution)/shard_map/ppermute | solution.py:594
  8.2 0.0 collective-permute-start.3
  8.2 3.9 %collective-permute-start.2 = (f32[1,64,128]{2,1,0:T(8,128)S(1)}, f32[1,64,128]{2,1,0:T(8,128)S(1)}, u32[]{:S(2)}, u32[]{:S(2)}) collective-permute-start(f32[1,64,128]{2,1,0:T(8,128)S(1)} %bitcast.3), channel_id=1, source_target_pairs={{0,2},{1,3},{2,0},{3,1},{4,6},{5,7},{6,4},{7,5},{8,10},{9,11},{10,... | collective-permute-start | bytes 98312 | tf_op jit(solution)/shard_map/ppermute | solution.py:594
  12.2 0.0 collective-permute-done.near
  12.2 0.0 collective-permute-done.1.far
  12.3 2.7 %wall_gradient.1 = f32[32,3,256]{2,1,0:T(4,128)} custom-call(f32[5,1,128,512]{3,2,1,0:T(8,128)S(1)} %copy-done, f32[5,1,128,512]{3,2,1,0:T(8,128)S(1)} %copy-done.1, f32[1,128,512]{2,1,0:T(8,128)S(1)} %copy-done.2, f32[56,512]{1,0:T(8,128)S(1)} %collective-permute-done.near, f32[56,512]{1,0:T(8,128)S(1)} %collective-permute-done.1.far, ...), custom_call_target="tpu_custom_call" | custom-call | tf_op jit(solution)/shard_map/wall_gradient/pallas_call | solution.py:233
  14.9 0.0 collective-permute-done.4
  14.9 0.0 collective-permute-done.3
  14.9 0.0 collective-permute-done.2
  15.0 1.6 %collective-permute-start.5 = (f32[4,64,128]{2,1,0:T(8,128)S(1)}, f32[4,64,128]{2,1,0:T(8,128)S(1)}, u32[]{:S(2)}, u32[]{:S(2)}) collective-permute-start(f32[4,64,128]{2,1,0:T(8,128)S(1)} %constant_dynamic-update-slice_fusion.same_0), channel_id=1, source_target_pairs={{0,8},{8,0},{16,24},{24,16},{1,9},{9,1},{17,25},{25,17},{2,10},{10... | collective-permute-start | bytes 393224 | tf_op jit(solution)/shard_map/ppermute | solution.py:598
  16.6 3.4 %all-to-all-start = ((f32[32,3,256]{2,1,0:T(4,128)}), f32[32,3,256]{2,1,0:T(4,128)S(1)}, u32[]{:S(2)}, u32[]{:S(2)}) async-start(f32[32,3,256]{2,1,0:T(4,128)} %wall_gradient.1), calls=%async_computation | async-start | bytes 262144 | tf_op jit(solution)/shard_map/all_to_all | solution.py:636
  20.0 0.1 collective-permute-start.6
  20.1 0.0 collective-permute-done.5.same_1
  20.1 0.4 %collective-permute-start.7 = (f32[4,64,128]{2,1,0:T(8,128)S(1)}, f32[4,64,128]{2,1,0:T(8,128)S(1)}, u32[]{:S(2)}, u32[]{:S(2)}) collective-permute-start(f32[4,64,128]{2,1,0:T(8,128)S(1)} %collective-permute-done.5.same_1), channel_id=1, source_target_pairs={{0,1},{1,0},{2,3},{3,2},{4,5},{5,4},{6,7},{7,6},{8,9},{9,8},{10,11... | collective-permute-start | bytes 393224 | tf_op jit(solution)/shard_map/ppermute | solution.py:594
  20.6 0.8 %collective-permute-done.6.other_0 = f32[4,64,128]{2,1,0:T(8,128)S(1)} collective-permute-done((f32[4,64,128]{2,1,0:T(8,128)S(1)}, f32[4,64,128]{2,1,0:T(8,128)S(1)}, u32[]{:S(2)}, u32[]{:S(2)}) %collective-permute-start.6) | collective-permute-done | bytes 131104 | tf_op jit(solution)/shard_map/ppermute | solution.py:594
  21.4 0.2 collective-permute-done.7.other_1
  21.6 11.1 %field.1 = f32[5,1,128,512]{3,2,1,0:T(8,128)} custom-call(f32[5,1,128,512]{3,2,1,0:T(8,128)S(1)} %copy-done, f32[5,1,128,512]{3,2,1,0:T(8,128)S(1)} %copy-done.1, f32[1,128,512]{2,1,0:T(8,128)S(1)} %copy-done.2, f32[56,512]{1,0:T(8,128)S(1)} %collective-permute-done.near, f32[56,512]{1,0:T(8,128)S(1)} %collective-permute-done.1.far, ...), custom_call_target="tpu_custom_call" | custom-call | tf_op jit(solution)/shard_map/field/pallas_call | solution.py:561
  32.7 0.0 all-to-all-done
  32.7 0.6 %reduce_sum.9 = f32[3,256]{1,0:T(4,128)} reduce(f32[32,3,256]{2,1,0:T(4,128)S(1)} %all-to-all-done, f32[]{:T(128)} %constant.0.clone.1), dimensions={0}, to_apply=%region_0.0 | reduce | flops 23808 | bytes 101380 | tf_op jit(solution)/shard_map/reduce_sum | solution.py:640
  (18 shorter events, 0.0 us)
Async XLA Ops:
  0.6 11.6 %copy-start.1 = (f32[5,1,128,512]{3,2,1,0:T(8,128)S(1)}, f32[5,1,128,512]{3,2,1,0:T(8,128)}, u32[]{:S(2)}) copy-start(f32[5,1,128,512]{3,2,1,0:T(8,128)} %l_hbm.3) | copy-start | bytes 3932164
  0.6 11.6 %copy-start.2 = (f32[1,128,512]{2,1,0:T(8,128)S(1)}, f32[1,128,512]{2,1,0:T(8,128)}, u32[]{:S(2)}) copy-start(f32[1,128,512]{2,1,0:T(8,128)} %k_hbm.3) | copy-start | bytes 786436
  0.7 11.6 %copy-start = (f32[5,1,128,512]{3,2,1,0:T(8,128)S(1)}, f32[5,1,128,512]{3,2,1,0:T(8,128)}, u32[]{:S(2)}) copy-start(f32[5,1,128,512]{3,2,1,0:T(8,128)} %u_hbm.3) | copy-start | bytes 3932164
  0.7 11.6 %copy-start.3 = (f32[5,5]{1,0:T(8,128)S(1)}, f32[5,5]{1,0:T(8,128)}, u32[]{:S(2)}) copy-start(f32[5,5]{1,0:T(8,128)} %c_hbm.1) | copy-start | bytes 304
  0.7 11.6 %copy-start.5 = (f32[1,8,384]{2,1,0:T(8,128)S(1)}, f32[1,8,384]{2,1,0:T(8,128)}, u32[]{:S(2)}) copy-start(f32[1,8,384]{2,1,0:T(8,128)} %dist.1) | copy-start | bytes 36868
  0.7 11.6 %copy-start.4 = (s32[1,8,384]{2,1,0:T(8,128)S(1)}, s32[1,8,384]{2,1,0:T(8,128)}, u32[]{:S(2)}) copy-start(s32[1,8,384]{2,1,0:T(8,128)} %ids.1) | copy-start | bytes 36868
  0.7 11.6 %copy-start.6 = (f32[3,5]{1,0:T(4,128)S(1)}, f32[3,5]{1,0:T(4,128)}, u32[]{:S(2)}) copy-start(f32[3,5]{1,0:T(4,128)} %proj_ref.1) | copy-start | bytes 184
  0.7 11.6 %copy-start.7 = (f32[1,384]{1,0:T(1,128)S(1)}, f32[1,384]{1,0:T(1,128)}, u32[]{:S(2)}) copy-start(f32[1,384]{1,0:T(1,128)} %area.1) | copy-start | bytes 4612
  2.6 9.6 %collective-permute-start = (f32[56,512]{1,0:T(8,128)S(1)}, f32[56,512]{1,0:T(8,128)S(1)}, u32[]{:S(2)}, u32[]{:S(2)}) collective-permute-start(f32[56,512]{1,0:T(8,128)S(1)} %get-tuple-element.11), channel_id=1, source_target_pairs={{0,1},{1,0},{2,3},{3,2},{4,5},{5,4},{6,7},{7,6},{8,9},{9,8},{10,11... | collective-permute-start | bytes 344072 | tf_op jit(solution)/shard_map/ppermute | solution.py:594
  3.1 9.1 %collective-permute-start.1 = (f32[56,512]{1,0:T(8,128)S(1)}, f32[56,512]{1,0:T(8,128)S(1)}, u32[]{:S(2)}, u32[]{:S(2)}) collective-permute-start(f32[56,512]{1,0:T(8,128)S(1)} %get-tuple-element.12), channel_id=1, source_target_pairs={{0,7},{1,2},{2,1},{3,4},{4,3},{5,6},{6,5},{7,0},{8,15},{9,10},{10,... | collective-permute-start | bytes 344072 | tf_op jit(solution)/shard_map/ppermute | solution.py:590
  7.8 7.1 %collective-permute-start.4 = (f32[1,64,128]{2,1,0:T(8,128)S(1)}, f32[1,64,128]{2,1,0:T(8,128)S(1)}, u32[]{:S(2)}, u32[]{:S(2)}) collective-permute-start(f32[1,64,128]{2,1,0:T(8,128)S(1)} %bitcast.1), channel_id=1, source_target_pairs={{0,6},{1,7},{2,4},{3,5},{4,2},{5,3},{6,0},{7,1},{8,14},{9,15},{10,... | collective-permute-start | bytes 98312 | tf_op jit(solution)/shard_map/ppermute | solution.py:594
  8.2 6.7 %collective-permute-start.3 = (f32[1,64,128]{2,1,0:T(8,128)S(1)}, f32[1,64,128]{2,1,0:T(8,128)S(1)}, u32[]{:S(2)}, u32[]{:S(2)}) collective-permute-start(f32[1,64,128]{2,1,0:T(8,128)S(1)} %bitcast.2), channel_id=1, source_target_pairs={{0,4},{1,5},{2,6},{3,7},{4,0},{5,1},{6,2},{7,3},{8,12},{9,13},{10,... | collective-permute-start | bytes 98312 | tf_op jit(solution)/shard_map/ppermute | solution.py:594
  8.2 6.7 %collective-permute-start.2 = (f32[1,64,128]{2,1,0:T(8,128)S(1)}, f32[1,64,128]{2,1,0:T(8,128)S(1)}, u32[]{:S(2)}, u32[]{:S(2)}) collective-permute-start(f32[1,64,128]{2,1,0:T(8,128)S(1)} %bitcast.3), channel_id=1, source_target_pairs={{0,2},{1,3},{2,0},{3,1},{4,6},{5,7},{6,4},{7,5},{8,10},{9,11},{10,... | collective-permute-start | bytes 98312 | tf_op jit(solution)/shard_map/ppermute | solution.py:594
  15.0 5.1 %collective-permute-start.5 = (f32[4,64,128]{2,1,0:T(8,128)S(1)}, f32[4,64,128]{2,1,0:T(8,128)S(1)}, u32[]{:S(2)}, u32[]{:S(2)}) collective-permute-start(f32[4,64,128]{2,1,0:T(8,128)S(1)} %constant_dynamic-update-slice_fusion.same_0), channel_id=1, source_target_pairs={{0,8},{8,0},{16,24},{24,16},{1,9},{9,1},{17,25},{25,17},{2,10},{10... | collective-permute-start | bytes 393224 | tf_op jit(solution)/shard_map/ppermute | solution.py:598
  16.6 16.1 %all-to-all-start = ((f32[32,3,256]{2,1,0:T(4,128)}), f32[32,3,256]{2,1,0:T(4,128)S(1)}, u32[]{:S(2)}, u32[]{:S(2)}) async-start(f32[32,3,256]{2,1,0:T(4,128)} %wall_gradient.1), calls=%async_computation | async-start | bytes 262144 | tf_op jit(solution)/shard_map/all_to_all | solution.py:636
  20.0 1.4 %collective-permute-start.6 = (f32[4,64,128]{2,1,0:T(8,128)S(1)}, f32[4,64,128]{2,1,0:T(8,128)S(1)}, u32[]{:S(2)}, u32[]{:S(2)}) collective-permute-start(f32[4,64,128]{2,1,0:T(8,128)S(1)} %constant_dynamic-update-slice_fusion.same_0), channel_id=1, source_target_pairs={{0,1},{1,0},{2,3},{3,2},{4,5},{5,4},{6,7},{7,6},{8,9},{9,8},{10,11... | collective-permute-start | bytes 393224 | tf_op jit(solution)/shard_map/ppermute | solution.py:594
  20.1 1.5 %collective-permute-start.7 = (f32[4,64,128]{2,1,0:T(8,128)S(1)}, f32[4,64,128]{2,1,0:T(8,128)S(1)}, u32[]{:S(2)}, u32[]{:S(2)}) collective-permute-start(f32[4,64,128]{2,1,0:T(8,128)S(1)} %collective-permute-done.5.same_1), channel_id=1, source_target_pairs={{0,1},{1,0},{2,3},{3,2},{4,5},{5,4},{6,7},{7,6},{8,9},{9,8},{10,11... | collective-permute-start | bytes 393224 | tf_op jit(solution)/shard_map/ppermute | solution.py:594

commit v5 on v4

--- a/solution.py
+++ b/solution.py
@@ -58,7 +58,7 @@
         ]
     for copy in copies:
         copy.start()
-    for copy in copies:
+    for copy in copies[:2]:
         copy.wait()
     size = dmap.shape[1]
     delta = dmap[...] - iota(dmap.shape, 1)
@@ -75,12 +75,16 @@
     which = iota((STEPS, rows), 1) == iota((STEPS, rows), 0)
     offsets = jnp.sum(jnp.where(which, offset, 0.0), axis=0, keepdims=True)
     strip[STEPS : 2 * STEPS, :] = dweight[...]
+    for copy in copies[2:5]:
+        copy.wait()
     strip[ROW_K : ROW_K + 1, :] = offsets
     strip[ROW_K + 1 : ROW_K + UCOLS, :] = k_side[...].T[LANES - UCOLS + 1 :]
     for v in range(NV):
         a, b = ROW_U + v * UCOLS, ROW_L + v * LCOLS
         strip[a : a + UCOLS, :] = u_side[v].T[LANES - UCOLS :]
         strip[b : b + LCOLS, :] = l_side[v].T[LANES - LCOLS :]
+    for copy in copies[5:]:
+        copy.wait()
     for i, ref in enumerate((near, far)):
         last = lower if i == 0 else jnp.logical_not(lower)
 
@@ -395,11 +399,17 @@
         out[j * LANES : (j + 1) * LANES, :] = flip[:, j * LANES : (j + 1) * LANES].T
 
 
-def field_kernel(
-    u_hbm, l_hbm, k_hbm, near, far, same_0, same_1, other_0, other_1, c_hbm, out,
-    c, ext_u, ext_l, ext_k, kap, rest, states, tanhs, lam, scaled, terms, buf, turned, flip, sems,
+def wrap(ref):
+    chunks = ref.shape[1] - 2
+    for v in range(NV):
+        ref[v, 0] = pltpu.roll(ref[v, chunks], 1, 0)
+        ref[v, chunks + 1] = pltpu.roll(ref[v, 1], SUB - 1, 0)
+
+
+def stage_kernel(
+    u_own, l_own, k_own, near, far, state, lam, scaled, kap, rest, ext_u, ext_l, ext_k, sems
 ):
-    rows, radial = u_hbm.shape[2], u_hbm.shape[3]
+    rows, radial = u_own.shape[2], u_own.shape[3]
     chunks = kap.shape[0]
     tiles = radial // LANES
     own = pl.ds(HALO, rows)
@@ -407,21 +417,16 @@
     def cut(j):
         return slice(j * LANES, (j + 1) * LANES)
 
-    c_copy = pltpu.make_async_copy(c_hbm, c, sems.at[4, 0])
-    c_copy.start()
     copies = []
     for j in range(tiles):
         lanes = pl.ds(j * LANES, LANES)
         copies += [
-            pltpu.make_async_copy(u_hbm.at[:, 0, :, lanes], ext_u.at[:, j, own], sems.at[0, j]),
-            pltpu.make_async_copy(l_hbm.at[:, 0, :, lanes], ext_l.at[:, j, own], sems.at[1, j]),
-            pltpu.make_async_copy(k_hbm.at[0, :, lanes], ext_k.at[j, own], sems.at[2, j]),
+            pltpu.make_async_copy(u_own.at[:, 0, :, lanes], ext_u.at[:, j, own], sems.at[0, j]),
+            pltpu.make_async_copy(l_own.at[:, 0, :, lanes], ext_l.at[:, j, own], sems.at[1, j]),
+            pltpu.make_async_copy(k_own.at[0, :, lanes], ext_k.at[j, own], sems.at[2, j]),
         ]
     for copy in copies:
         copy.start()
-    face_terms(
-        (same_0, same_1), (other_0, other_1), c, terms, buf, turned, flip, rows, c_copy.wait
-    )
     lower = lax.axis_index("block") % 2 == 0
 
     def halo(a, b, cols):
@@ -449,21 +454,65 @@
             kap[i, :, cut(j)] = kappa
             rest[i, :, cut(j)] = 1.0 - 4.0 * kappa
             for v in range(NV):
-                states[0, v, i + 1, :, cut(j)] = ext_u[v, j, at, :]
+                state[v, i + 1, :, cut(j)] = ext_u[v, j, at, :]
                 x = ext_l[v, j, at, :]
                 lam[v, i, :, cut(j)] = x
-                scaled[0, v, i + 1, :, cut(j)] = kappa * x
+                scaled[v, i + 1, :, cut(j)] = kappa * x
         return carry
 
-    lax.fori_loop(0, chunks, load, 0, unroll=2)
-
-    def wrap(ref):
-        for v in range(NV):
-            ref[v, 0] = pltpu.roll(ref[v, chunks], 1, 0)
-            ref[v, chunks + 1] = pltpu.roll(ref[v, 1], SUB - 1, 0)
-
-    wrap(states.at[0])
-    wrap(scaled.at[0])
+    lax.fori_loop(0, chunks, load, 0, unroll=3)
+    wrap(state)
+    wrap(scaled)
+
+
+def stage(start_state, final_cotangent, diffusivity, near, far):
+    _, _, rows, radial = start_state.shape
+    ext = rows + 2 * HALO
+    chunks, tiles = ext // SUB, radial // LANES
+    f32 = jnp.float32
+    vm = pl.BlockSpec(memory_space=pltpu.VMEM)
+    outs = (
+        (NV, chunks + 2, SUB, radial),
+        (NV, chunks, SUB, radial),
+        (NV, chunks + 2, SUB, radial),
+        (chunks, SUB, radial),
+        (chunks, SUB, radial),
+    )
+    return pl.pallas_call(
+        stage_kernel,
+        in_specs=[vm] * 5,
+        out_specs=[vm] * len(outs),
+        out_shape=[jax.ShapeDtypeStruct(shape, f32) for shape in outs],
+        scratch_shapes=[
+            pltpu.VMEM((NV, tiles, ext, LANES), f32),
+            pltpu.VMEM((NV, tiles, ext, LANES), f32),
+            pltpu.VMEM((tiles, ext, LANES), f32),
+            pltpu.SemaphoreType.DMA((3, tiles)),
+        ],
+        compiler_params=params(24 * 1024 * 1024),
+        name="stage",
+    )(start_state, final_cotangent, diffusivity, near, far)
+
+
+def field_kernel(
+    state_0, lam_0, scaled_0, kap, rest, same_0, same_1, other_0, other_1, c_hbm, out,
+    c, leaving, states, tanhs, lam, scaled, terms, buf, turned, flip, sems,
+):
+    chunks, radial = kap.shape[0], kap.shape[2]
+    rows = chunks * SUB - 2 * HALO
+    tiles = radial // LANES
+    own = pl.ds(HALO, rows)
+
+    def cut(j):
+        return slice(j * LANES, (j + 1) * LANES)
+
+    c_copy = pltpu.make_async_copy(c_hbm, c, sems.at[NV, 0])
+    c_copy.start()
+    face_terms(
+        (same_0, same_1), (other_0, other_1), c, terms, buf, turned, flip, rows, c_copy.wait
+    )
+    state = [state_0] + [states.at[n] for n in range(STEPS - 1)]
+    spread = [scaled_0] + [scaled.at[n] for n in range(2)]
     lane = iota((SUB, LANES), 1)
     is_first, is_last = lane == 0, lane == LANES - 1
 
@@ -489,20 +538,20 @@
             cache = {}
             for j in range(tiles):
                 kappa = kap[i, :, cut(j)]
-                pairs = [neighbours(states.at[n], v, i, j, edge[v], cache) for v in range(NV)]
+                pairs = [neighbours(state[n], v, i, j, edge[v], cache) for v in range(NV)]
                 t = [jnp.tanh(x) for _, x in pairs]
                 for v in range(NV):
                     around, x = pairs[v]
                     tanhs[n, v, i, :, cut(j)] = t[v]
                     reaction = sum(c[v, w] * t[w] for w in range(NV))
-                    states[n + 1, v, i + 1, :, cut(j)] = (
+                    state[n + 1][v, i + 1, :, cut(j)] = (
                         rest[i, :, cut(j)] * x + kappa * around - reaction
                     )
             return carry
 
         lax.fori_loop(0, chunks, body, 0, unroll=chunks)
         if n + 1 < STEPS - 1:
-            wrap(states.at[n + 1])
+            wrap(state[n + 1])
 
     def backward(n, source, target, chosen):
         def body(i, carry):
@@ -510,40 +559,41 @@
             cache = {}
             for j in range(tiles):
                 kappa = kap[i, :, cut(j)]
-                x = [lam[v, i, :, cut(j)] for v in range(NV)]
+                x = [(lam_0 if n == STEPS - 1 else lam)[v, i, :, cut(j)] for v in range(NV)]
                 for v in chosen:
-                    around, _ = neighbours(scaled.at[source], v, i, j, edge[v], cache)
+                    around, _ = neighbours(spread[source], v, i, j, edge[v], cache)
                     if n < STEPS - 1:
                         t = tanhs[n, v, i, :, cut(j)]
                     else:
-                        t = jnp.tanh(states[n, v, i + 1, :, cut(j)])
+                        t = jnp.tanh(state[n][v, i + 1, :, cut(j)])
                     pulled = sum(c[w, v] * x[w] for w in range(NV))
                     new = rest[i, :, cut(j)] * x[v] + around - (1.0 - t * t) * pulled
                     if n > 0:
                         lam[v, i, :, cut(j)] = new
-                        scaled[target, v, i + 1, :, cut(j)] = kappa * new
+                        spread[target][v, i + 1, :, cut(j)] = kappa * new
                     else:
-                        ext_l[v, j, pl.ds(i, SUB, stride=chunks), :] = new
+                        leaving[v, j, pl.ds(i, SUB, stride=chunks), :] = new
             return carry
 
         lax.fori_loop(0, chunks, body, 0, unroll=chunks)
         if n > 0:
-            wrap(scaled.at[target])
+            wrap(spread[target])
 
     for n in range(STEPS - 1):
         forward(n)
     source = 0
     for n in reversed(range(1, STEPS)):
-        backward(n, source, 1 - source, range(NV))
-        source = 1 - source
+        target = 2 if source == 1 else 1
+        backward(n, source, target, range(NV))
+        source = target
     copies = []
     for v in range(NV):
-        backward(0, source, 1 - source, (v,))
+        backward(0, source, None, (v,))
         for j in range(tiles):
             lanes = pl.ds(j * LANES, LANES)
             copies.append(
                 pltpu.make_async_copy(
-                    ext_l.at[v, j, own], out.at[v, 0, :, lanes], sems.at[5 + v, j]
+                    leaving.at[v, j, own], out.at[v, 0, :, lanes], sems.at[v, j]
                 )
             )
             copies[-1].start()
@@ -551,10 +601,10 @@
         copy.wait()
 
 
-def field(start_state, final_cotangent, diffusivity, near, far, strips, coupling):
-    _, _, rows, radial = start_state.shape
-    ext = rows + 2 * HALO
-    chunks, tiles, blocks = ext // SUB, radial // LANES, 2 * strips[0].shape[0]
+def field(staged, strips, coupling):
+    _, chunks, _, radial = staged[1].shape
+    ext = chunks * SUB
+    rows, tiles, blocks = ext - 2 * HALO, radial // LANES, 2 * strips[0].shape[0]
     vm = pl.BlockSpec(memory_space=pltpu.VMEM)
     hbm = pl.BlockSpec(memory_space=pltpu.HBM)
     f32 = jnp.float32
@@ -562,15 +612,11 @@
         field_kernel,
         in_specs=[vm] * 9 + [hbm],
         out_specs=hbm,
-        out_shape=jax.ShapeDtypeStruct(start_state.shape, f32),
+        out_shape=jax.ShapeDtypeStruct((NV, 1, rows, radial), f32),
         scratch_shapes=[
             pltpu.SMEM(coupling.shape, f32),
             pltpu.VMEM((NV, tiles, ext, LANES), f32),
-            pltpu.VMEM((NV, tiles, ext, LANES), f32),
-            pltpu.VMEM((tiles, ext, LANES), f32),
-            pltpu.VMEM((chunks, SUB, radial), f32),
-            pltpu.VMEM((chunks, SUB, radial), f32),
-            pltpu.VMEM((STEPS, NV, chunks + 2, SUB, radial), f32),
+            pltpu.VMEM((STEPS - 1, NV, chunks + 2, SUB, radial), f32),
             pltpu.VMEM((STEPS - 1, NV, chunks, SUB, radial), f32),
             pltpu.VMEM((NV, chunks, SUB, radial), f32),
             pltpu.VMEM((2, NV, chunks + 2, SUB, radial), f32),
@@ -578,11 +624,11 @@
             pltpu.VMEM((2 * STRIP * blocks, LANES), f32),
             pltpu.VMEM(((2 * STEPS - 1) * SUB * blocks, LANES), f32),
             pltpu.VMEM((LANES, 2 * LANES), f32),
-            pltpu.SemaphoreType.DMA((5 + NV, tiles)),
+            pltpu.SemaphoreType.DMA((NV + 1, tiles)),
         ],
-        compiler_params=params(),
+        compiler_params=params(40 * 1024 * 1024),
         name="field",
-    )(start_state, final_cotangent, diffusivity, near, far, *strips, coupling)
+    )(*staged, *strips, coupling)
 
 
 def beyond(x):
@@ -598,7 +644,7 @@
     return lax.ppermute(x, "zone", [(i, i ^ 1) for i in range(lax.axis_size("zone"))])
 
 
-def gather_pair(strip, first):
+def gather_pair(strip, first, later):
     x = strip[None]
     bit, size = 1, lax.axis_size("block")
     while 2**bit < size:
@@ -608,7 +654,8 @@
         x = jnp.concatenate(pieces, axis=0)
         bit += 2 if wide == 4 else 1
     y = swapped(x)
-    return x, y, crossed(x, 1), crossed(y, 1)
+    y, later = lax.optimization_barrier((y, later))
+    return (x, y, crossed(x, 1), crossed(y, 1)), later
 
 
 def local(
@@ -632,10 +679,11 @@
         start_state, final_cotangent, diffusivity, near, far, coupling, wall_projection,
         wall_area, center_ids, center_dist, devices,
     )
-    strips = gather_pair(strip, points)
+    strips, (near, far) = gather_pair(strip, points, (near, far))
     points = lax.all_to_all(points, ("zone", "block"), 0, 0, tiled=True)
 
-    adjoint = field(start_state, final_cotangent, diffusivity, near, far, strips, coupling)
+    staged = stage(start_state, final_cotangent, diffusivity, near, far)
+    adjoint = field(staged, strips, coupling)
     adjoint, points = lax.optimization_barrier((adjoint, points))
     return adjoint, points.sum(axis=0)
 

time: 33.5 us -> 32.9 us (0.982)
  waiting for transfers between devices: 1.04 us -> 0.02 us
  Pallas kernels: 15.6 us -> 16 us
    pallas_call x0 -> x1, Pallas kernels: none -> 1.11 us  [stage(): pl.pallas_call(stage_kernel, in_specs=[vm] * 5, out_specs=[vm] * len(outs...]
    ppermute x6, waiting for transfers between devices: 1.03 us -> 0.02 us  [crossed(): lax.ppermute(x, 'block', [(i, i ^ mask) for i in range(lax.axis_size('blo...]
    pallas_call x1, Pallas kernels: 11.1 us -> 10.5 us  [field(): pl.pallas_call(field_kernel, in_specs=[vm] * 9 + [hbm], out_specs=hbm, ou...]
  transfers between devices with their start and end apart: 9 -> 9, of which waited for: 2 -> 0; matrix products, arithmetic and copies ran while one was open for 0% -> 0% of each run, Pallas kernels for 41% -> 44%
where the time goes in v5:
time: 32.9 us; the launch traced here: 32.7 us
  Pallas kernels  16 us (49%)
  starting transfers between devices  15.2 us (46%)
  between operations  0.85 us (3%)
  other arithmetic  0.64 us (2%)
    pallas_call x1, Pallas kernels, field(): pl.pallas_call(field_kernel, in_specs=[vm] * 9 + [hbm], out_specs=hbm, ou...  10.5 us
    ppermute x6, starting transfers between devices, crossed(): lax.ppermute(x, 'block', [(i, i ^ mask) for i in range(lax.axis_size('blo...  5.48 us
    ppermute x1, starting transfers between devices, beyond(): lax.ppermute(x, 'block', [(i, (i + (1 if i % 2 else -1)) % size) for i in...  4.71 us
    all_to_all x1, starting transfers between devices, local(): points = lax.all_to_all(points, ('zone', 'block'), 0, 0, tiled=True)  3.41 us
    pallas_call x1, Pallas kernels, wall_gradient(): pl.pallas_call(functools.partial(wall_kernel, devices=devices), in_specs=...  2.66 us
    pallas_call x1, Pallas kernels, pack(): pl.pallas_call(pack_kernel, in_specs=[pl.BlockSpec(memory_space=pltpu.HBM...  1.69 us
    ppermute x1, starting transfers between devices, swapped(): lax.ppermute(x, 'zone', [(i, i ^ 1) for i in range(lax.axis_size('zone'))])  1.56 us
    pallas_call x1, Pallas kernels, stage(): pl.pallas_call(stage_kernel, in_specs=[vm] * 5, out_specs=[vm] * len(outs...  1.11 us
  transfers between devices with their start and end apart: 9, of which 0 were waited for; matrix products, arithmetic and copies ran while one was open for 0% of the time, Pallas kernels for 44%

profile of v5, /device:TPU:0, one launch (start us, length us, event | category | flops | bytes accessed | tf_op | source)
XLA Modules:
  0.0 32.7 jit_solution(5270633028640857974)
XLA Ops:
  0.7 1.7 %pack.1 = (f32[64,128]{1,0:T(8,128)S(1)}, f32[56,512]{1,0:T(8,128)S(1)}, f32[56,512]{1,0:T(8,128)S(1)}) custom-call(f32[5,1,128,512]{3,2,1,0:T(8,128)} %u_own.3, f32[5,1,128,512]{3,2,1,0:T(8,128)} %l_own.3, f32[1,128,512]{2,1,0:T(8,128)} %k_own.3, s32[4,1,1024]{2,1,0:T(1,128)} %map_hbm.1, f32[4,1,1024]{2,1,0:T(1,128)} %weight_hbm.1), custom_call_target="tpu_custom_call" | custom-call | tf_op jit(solution)/shard_map/pack/pallas_call | solution.py:104
  2.4 0.5 %collective-permute-start.3 = (f32[56,512]{1,0:T(8,128)S(1)}, f32[56,512]{1,0:T(8,128)S(1)}, u32[]{:S(2)}, u32[]{:S(2)}) collective-permute-start(f32[56,512]{1,0:T(8,128)S(1)} %get-tuple-element.20), channel_id=1, source_target_pairs={{0,1},{1,0},{2,3},{3,2},{4,5},{5,4},{6,7},{7,6},{8,9},{9,8},{10,11... | collective-permute-start | bytes 344072 | tf_op jit(solution)/shard_map/ppermute | solution.py:640
  2.9 4.7 %collective-permute-start.4 = (f32[56,512]{1,0:T(8,128)S(1)}, f32[56,512]{1,0:T(8,128)S(1)}, u32[]{:S(2)}, u32[]{:S(2)}) collective-permute-start(f32[56,512]{1,0:T(8,128)S(1)} %get-tuple-element.21), channel_id=1, source_target_pairs={{0,7},{1,2},{2,1},{3,4},{4,3},{5,6},{6,5},{7,0},{8,15},{9,10},{10,... | collective-permute-start | bytes 344072 | tf_op jit(solution)/shard_map/ppermute | solution.py:636
  7.6 0.4 %collective-permute-start.2 = (f32[1,64,128]{2,1,0:T(8,128)S(1)}, f32[1,64,128]{2,1,0:T(8,128)S(1)}, u32[]{:S(2)}, u32[]{:S(2)}) collective-permute-start(f32[1,64,128]{2,1,0:T(8,128)S(1)} %bitcast.1), channel_id=1, source_target_pairs={{0,6},{1,7},{2,4},{3,5},{4,2},{5,3},{6,0},{7,1},{8,14},{9,15},{10,... | collective-permute-start | bytes 98312 | tf_op jit(solution)/shard_map/ppermute | solution.py:640
  8.1 0.0 collective-permute-start.1
  8.1 3.9 %collective-permute-start = (f32[1,64,128]{2,1,0:T(8,128)S(1)}, f32[1,64,128]{2,1,0:T(8,128)S(1)}, u32[]{:S(2)}, u32[]{:S(2)}) collective-permute-start(f32[1,64,128]{2,1,0:T(8,128)S(1)} %bitcast.3), channel_id=1, source_target_pairs={{0,2},{1,3},{2,0},{3,1},{4,6},{5,7},{6,4},{7,5},{8,10},{9,11},{10,... | collective-permute-start | bytes 98312 | tf_op jit(solution)/shard_map/ppermute | solution.py:640
  12.0 0.0 collective-permute-done.3.near
  12.0 0.0 collective-permute-done.4.far
  12.0 0.0 copy-done.1
  12.1 2.7 %wall_gradient.1 = f32[32,3,256]{2,1,0:T(4,128)} custom-call(f32[5,1,128,512]{3,2,1,0:T(8,128)S(1)} %copy-done, f32[5,1,128,512]{3,2,1,0:T(8,128)S(1)} %copy-done.1, f32[1,128,512]{2,1,0:T(8,128)S(1)} %copy-done.2, f32[56,512]{1,0:T(8,128)S(1)} %collective-permute-done.3.near, f32[56,512]{1,0:T(8,128)S(1)} %collective-permute-done.4.far, ...), custom_call_target="tpu_custom_call" | custom-call | tf_op jit(solution)/shard_map/wall_gradient/pallas_call | solution.py:237
  14.8 0.0 collective-permute-done.2
  14.8 0.0 collective-permute-done.1
  14.8 0.0 collective-permute-done
  14.8 1.6 %collective-permute-start.5 = (f32[4,64,128]{2,1,0:T(8,128)S(1)}, f32[4,64,128]{2,1,0:T(8,128)S(1)}, u32[]{:S(2)}, u32[]{:S(2)}) collective-permute-start(f32[4,64,128]{2,1,0:T(8,128)S(1)} %constant_dynamic-update-slice_fusion.same_0), channel_id=1, source_target_pairs={{0,8},{8,0},{16,24},{24,16},{1,9},{9,1},{17,25},{25,17},{2,10},{10... | collective-permute-start | bytes 393224 | tf_op jit(solution)/shard_map/ppermute | solution.py:644
  16.4 3.4 %all-to-all-start = ((f32[32,3,256]{2,1,0:T(4,128)}), f32[32,3,256]{2,1,0:T(4,128)S(1)}, u32[]{:S(2)}, u32[]{:S(2)}) async-start(f32[32,3,256]{2,1,0:T(4,128)} %wall_gradient.1), calls=%async_computation | async-start | bytes 262144 | tf_op jit(solution)/shard_map/all_to_all | solution.py:683
  19.8 0.1 collective-permute-start.6
  20.0 0.0 collective-permute-done.5.same_1
  20.0 0.4 %collective-permute-start.7 = (f32[4,64,128]{2,1,0:T(8,128)S(1)}, f32[4,64,128]{2,1,0:T(8,128)S(1)}, u32[]{:S(2)}, u32[]{:S(2)}) collective-permute-start(f32[4,64,128]{2,1,0:T(8,128)S(1)} %collective-permute-done.5.same_1), channel_id=1, source_target_pairs={{0,1},{1,0},{2,3},{3,2},{4,5},{5,4},{6,7},{7,6},{8,9},{9,8},{10,11... | collective-permute-start | bytes 393224 | tf_op jit(solution)/shard_map/ppermute | solution.py:640
  20.4 1.1 %stage.1 = (f32[5,20,8,512]{3,2,1,0:T(8,128)S(1)}, f32[5,18,8,512]{3,2,1,0:T(8,128)S(1)}, f32[5,20,8,512]{3,2,1,0:T(8,128)S(1)}, f32[18,8,512]{2,1,0:T(8,128)S(1)}, f32[18,8,512]{2,1,0:T(8,128)S(1)}) custom-call(f32[5,1,128,512]{3,2,1,0:T(8,128)S(1)} %copy-done, f32[5,1,128,512]{3,2,1,0:T(8,128)S(1)} %copy-done.1, f32[1,128,512]{2,1,0:T(8,128)S(1)} %copy-done.2, ...), custom_call_target="tpu_custom_call" | custom-call | tf_op jit(solution)/shard_map/stage/pallas_call | solution.py:481
  21.5 0.0 collective-permute-done.6.other_0
  21.5 0.0 collective-permute-done.7.other_1
  21.5 10.5 %field.1 = f32[5,1,128,512]{3,2,1,0:T(8,128)} custom-call(f32[5,20,8,512]{3,2,1,0:T(8,128)S(1)} %get-tuple-element.28.state_0, f32[5,18,8,512]{3,2,1,0:T(8,128)S(1)} %get-tuple-element.29.lam_0, f32[5,20,8,512]{3,2,1,0:T(8,128)S(1)} %get-tuple-element.30.scaled_0, f32[18,8,512]{2,1,0:T(8,128)S(1)} %get-tuple-element.31.kap, ...), custom_call_target="tpu_custom_call" | custom-call | tf_op jit(solution)/shard_map/field/pallas_call | solution.py:611
  32.1 0.0 all-to-all-done
  32.1 0.6 %reduce_sum.9 = f32[3,256]{1,0:T(4,128)} reduce(f32[32,3,256]{2,1,0:T(4,128)S(1)} %all-to-all-done, f32[]{:T(128)} %constant.0.clone.1), dimensions={0}, to_apply=%region_0.0 | reduce | flops 23808 | bytes 101380 | tf_op jit(solution)/shard_map/reduce_sum | solution.py:688
  (19 shorter events, 0.1 us)
Async XLA Ops:
  0.6 11.4 %copy-start.1 = (f32[5,1,128,512]{3,2,1,0:T(8,128)S(1)}, f32[5,1,128,512]{3,2,1,0:T(8,128)}, u32[]{:S(2)}) copy-start(f32[5,1,128,512]{3,2,1,0:T(8,128)} %l_own.3) | copy-start | bytes 3932164
  0.6 11.4 %copy-start.2 = (f32[1,128,512]{2,1,0:T(8,128)S(1)}, f32[1,128,512]{2,1,0:T(8,128)}, u32[]{:S(2)}) copy-start(f32[1,128,512]{2,1,0:T(8,128)} %k_own.3) | copy-start | bytes 786436
  0.7 11.4 %copy-start = (f32[5,1,128,512]{3,2,1,0:T(8,128)S(1)}, f32[5,1,128,512]{3,2,1,0:T(8,128)}, u32[]{:S(2)}) copy-start(f32[5,1,128,512]{3,2,1,0:T(8,128)} %u_own.3) | copy-start | bytes 3932164
  0.7 11.4 %copy-start.3 = (f32[5,5]{1,0:T(8,128)S(1)}, f32[5,5]{1,0:T(8,128)}, u32[]{:S(2)}) copy-start(f32[5,5]{1,0:T(8,128)} %c_hbm.1) | copy-start | bytes 304
  0.7 11.4 %copy-start.5 = (f32[1,8,384]{2,1,0:T(8,128)S(1)}, f32[1,8,384]{2,1,0:T(8,128)}, u32[]{:S(2)}) copy-start(f32[1,8,384]{2,1,0:T(8,128)} %dist.1) | copy-start | bytes 36868
  0.7 11.4 %copy-start.4 = (s32[1,8,384]{2,1,0:T(8,128)S(1)}, s32[1,8,384]{2,1,0:T(8,128)}, u32[]{:S(2)}) copy-start(s32[1,8,384]{2,1,0:T(8,128)} %ids.1) | copy-start | bytes 36868
  0.7 11.4 %copy-start.6 = (f32[3,5]{1,0:T(4,128)S(1)}, f32[3,5]{1,0:T(4,128)}, u32[]{:S(2)}) copy-start(f32[3,5]{1,0:T(4,128)} %proj_ref.1) | copy-start | bytes 184
  0.7 11.4 %copy-start.7 = (f32[1,384]{1,0:T(1,128)S(1)}, f32[1,384]{1,0:T(1,128)}, u32[]{:S(2)}) copy-start(f32[1,384]{1,0:T(1,128)} %area.1) | copy-start | bytes 4612
  2.4 9.6 %collective-permute-start.3 = (f32[56,512]{1,0:T(8,128)S(1)}, f32[56,512]{1,0:T(8,128)S(1)}, u32[]{:S(2)}, u32[]{:S(2)}) collective-permute-start(f32[56,512]{1,0:T(8,128)S(1)} %get-tuple-element.20), channel_id=1, source_target_pairs={{0,1},{1,0},{2,3},{3,2},{4,5},{5,4},{6,7},{7,6},{8,9},{9,8},{10,11... | collective-permute-start | bytes 344072 | tf_op jit(solution)/shard_map/ppermute | solution.py:640
  2.9 9.1 %collective-permute-start.4 = (f32[56,512]{1,0:T(8,128)S(1)}, f32[56,512]{1,0:T(8,128)S(1)}, u32[]{:S(2)}, u32[]{:S(2)}) collective-permute-start(f32[56,512]{1,0:T(8,128)S(1)} %get-tuple-element.21), channel_id=1, source_target_pairs={{0,7},{1,2},{2,1},{3,4},{4,3},{5,6},{6,5},{7,0},{8,15},{9,10},{10,... | collective-permute-start | bytes 344072 | tf_op jit(solution)/shard_map/ppermute | solution.py:636
  7.6 7.1 %collective-permute-start.2 = (f32[1,64,128]{2,1,0:T(8,128)S(1)}, f32[1,64,128]{2,1,0:T(8,128)S(1)}, u32[]{:S(2)}, u32[]{:S(2)}) collective-permute-start(f32[1,64,128]{2,1,0:T(8,128)S(1)} %bitcast.1), channel_id=1, source_target_pairs={{0,6},{1,7},{2,4},{3,5},{4,2},{5,3},{6,0},{7,1},{8,14},{9,15},{10,... | collective-permute-start | bytes 98312 | tf_op jit(solution)/shard_map/ppermute | solution.py:640
  8.1 6.7 %collective-permute-start.1 = (f32[1,64,128]{2,1,0:T(8,128)S(1)}, f32[1,64,128]{2,1,0:T(8,128)S(1)}, u32[]{:S(2)}, u32[]{:S(2)}) collective-permute-start(f32[1,64,128]{2,1,0:T(8,128)S(1)} %bitcast.2), channel_id=1, source_target_pairs={{0,4},{1,5},{2,6},{3,7},{4,0},{5,1},{6,2},{7,3},{8,12},{9,13},{10,... | collective-permute-start | bytes 98312 | tf_op jit(solution)/shard_map/ppermute | solution.py:640
  8.1 6.7 %collective-permute-start = (f32[1,64,128]{2,1,0:T(8,128)S(1)}, f32[1,64,128]{2,1,0:T(8,128)S(1)}, u32[]{:S(2)}, u32[]{:S(2)}) collective-permute-start(f32[1,64,128]{2,1,0:T(8,128)S(1)} %bitcast.3), channel_id=1, source_target_pairs={{0,2},{1,3},{2,0},{3,1},{4,6},{5,7},{6,4},{7,5},{8,10},{9,11},{10,... | collective-permute-start | bytes 98312 | tf_op jit(solution)/shard_map/ppermute | solution.py:640
  14.8 5.1 %collective-permute-start.5 = (f32[4,64,128]{2,1,0:T(8,128)S(1)}, f32[4,64,128]{2,1,0:T(8,128)S(1)}, u32[]{:S(2)}, u32[]{:S(2)}) collective-permute-start(f32[4,64,128]{2,1,0:T(8,128)S(1)} %constant_dynamic-update-slice_fusion.same_0), channel_id=1, source_target_pairs={{0,8},{8,0},{16,24},{24,16},{1,9},{9,1},{17,25},{25,17},{2,10},{10... | collective-permute-start | bytes 393224 | tf_op jit(solution)/shard_map/ppermute | solution.py:644
  16.4 15.7 %all-to-all-start = ((f32[32,3,256]{2,1,0:T(4,128)}), f32[32,3,256]{2,1,0:T(4,128)S(1)}, u32[]{:S(2)}, u32[]{:S(2)}) async-start(f32[32,3,256]{2,1,0:T(4,128)} %wall_gradient.1), calls=%async_computation | async-start | bytes 262144 | tf_op jit(solution)/shard_map/all_to_all | solution.py:683
  19.8 1.7 %collective-permute-start.6 = (f32[4,64,128]{2,1,0:T(8,128)S(1)}, f32[4,64,128]{2,1,0:T(8,128)S(1)}, u32[]{:S(2)}, u32[]{:S(2)}) collective-permute-start(f32[4,64,128]{2,1,0:T(8,128)S(1)} %constant_dynamic-update-slice_fusion.same_0), channel_id=1, source_target_pairs={{0,1},{1,0},{2,3},{3,2},{4,5},{5,4},{6,7},{7,6},{8,9},{9,8},{10,11... | collective-permute-start | bytes 393224 | tf_op jit(solution)/shard_map/ppermute | solution.py:640
  20.0 1.6 %collective-permute-start.7 = (f32[4,64,128]{2,1,0:T(8,128)S(1)}, f32[4,64,128]{2,1,0:T(8,128)S(1)}, u32[]{:S(2)}, u32[]{:S(2)}) collective-permute-start(f32[4,64,128]{2,1,0:T(8,128)S(1)} %collective-permute-done.5.same_1), channel_id=1, source_target_pairs={{0,1},{1,0},{2,3},{3,2},{4,5},{5,4},{6,7},{7,6},{8,9},{9,8},{10,11... | collective-permute-start | bytes 393224 | tf_op jit(solution)/shard_map/ppermute | solution.py:640

commit v6 on v5

--- a/solution.py
+++ b/solution.py
@@ -511,7 +511,7 @@
     face_terms(
         (same_0, same_1), (other_0, other_1), c, terms, buf, turned, flip, rows, c_copy.wait
     )
-    state = [state_0] + [states.at[n] for n in range(STEPS - 1)]
+    state = [state_0] + [states.at[n] for n in range(STEPS - 2)]
     spread = [scaled_0] + [scaled.at[n] for n in range(2)]
     lane = iota((SUB, LANES), 1)
     is_first, is_last = lane == 0, lane == LANES - 1
@@ -532,26 +532,40 @@
         e = terms[pl.ds(i, SUB, stride=chunks), :]
         return [pltpu.roll(e, (2 * LANES - 1 - (n * SUB + v)) % LANES, 1) for v in range(NV)]
 
+    def pull(v, i, j, x, t, around):
+        pulled = sum(c[w, v] * x[w] for w in range(NV))
+        return rest[i, :, cut(j)] * x[v] + around - (1.0 - t * t) * pulled
+
     def forward(n):
+        joined = n == STEPS - 2
+
         def body(i, carry):
             edge = edges(i, n)
-            cache = {}
+            cache, back_cache = {}, {}
+            if joined:
+                back_edge = edges(i, 2 * STEPS - 2)
             for j in range(tiles):
                 kappa = kap[i, :, cut(j)]
                 pairs = [neighbours(state[n], v, i, j, edge[v], cache) for v in range(NV)]
                 t = [jnp.tanh(x) for _, x in pairs]
+                if joined:
+                    lams = [lam_0[v, i, :, cut(j)] for v in range(NV)]
                 for v in range(NV):
                     around, x = pairs[v]
                     tanhs[n, v, i, :, cut(j)] = t[v]
                     reaction = sum(c[v, w] * t[w] for w in range(NV))
-                    state[n + 1][v, i + 1, :, cut(j)] = (
-                        rest[i, :, cut(j)] * x + kappa * around - reaction
-                    )
+                    new = rest[i, :, cut(j)] * x + kappa * around - reaction
+                    if joined:
+                        around, _ = neighbours(scaled_0, v, i, j, back_edge[v], back_cache)
+                        y = pull(v, i, j, lams, jnp.tanh(new), around)
+                        lam[v, i, :, cut(j)] = y
+                        spread[1][v, i + 1, :, cut(j)] = kappa * y
+                    else:
+                        state[n + 1][v, i + 1, :, cut(j)] = new
             return carry
 
         lax.fori_loop(0, chunks, body, 0, unroll=chunks)
-        if n + 1 < STEPS - 1:
-            wrap(state[n + 1])
+        wrap(spread[1] if joined else state[n + 1])
 
     def backward(n, source, target, chosen):
         def body(i, carry):
@@ -559,15 +573,10 @@
             cache = {}
             for j in range(tiles):
                 kappa = kap[i, :, cut(j)]
-                x = [(lam_0 if n == STEPS - 1 else lam)[v, i, :, cut(j)] for v in range(NV)]
+                x = [lam[v, i, :, cut(j)] for v in range(NV)]
                 for v in chosen:
                     around, _ = neighbours(spread[source], v, i, j, edge[v], cache)
-                    if n < STEPS - 1:
-                        t = tanhs[n, v, i, :, cut(j)]
-                    else:
-                        t = jnp.tanh(state[n][v, i + 1, :, cut(j)])
-                    pulled = sum(c[w, v] * x[w] for w in range(NV))
-                    new = rest[i, :, cut(j)] * x[v] + around - (1.0 - t * t) * pulled
+                    new = pull(v, i, j, x, tanhs[n, v, i, :, cut(j)], around)
                     if n > 0:
                         lam[v, i, :, cut(j)] = new
                         spread[target][v, i + 1, :, cut(j)] = kappa * new
@@ -581,8 +590,8 @@
 
     for n in range(STEPS - 1):
         forward(n)
-    source = 0
-    for n in reversed(range(1, STEPS)):
+    source = 1
+    for n in reversed(range(1, STEPS - 1)):
         target = 2 if source == 1 else 1
         backward(n, source, target, range(NV))
         source = target
@@ -616,7 +625,7 @@
         scratch_shapes=[
             pltpu.SMEM(coupling.shape, f32),
             pltpu.VMEM((NV, tiles, ext, LANES), f32),
-            pltpu.VMEM((STEPS - 1, NV, chunks + 2, SUB, radial), f32),
+            pltpu.VMEM((STEPS - 2, NV, chunks + 2, SUB, radial), f32),
             pltpu.VMEM((STEPS - 1, NV, chunks, SUB, radial), f32),
             pltpu.VMEM((NV, chunks, SUB, radial), f32),
             pltpu.VMEM((2, NV, chunks + 2, SUB, radial), f32),

time: 32.9 us -> 32.9 us (level)
  no operation moved by 1% of the time
where the time goes in v6:
time: 32.9 us; the launch traced here: 32.7 us
  Pallas kernels  16 us (49%)
  starting transfers between devices  15.2 us (46%)
  between operations  0.85 us (3%)
  other arithmetic  0.64 us (2%)
    pallas_call x1, Pallas kernels, field(): pl.pallas_call(field_kernel, in_specs=[vm] * 9 + [hbm], out_specs=hbm, ou...  10.5 us
    ppermute x6, starting transfers between devices, crossed(): lax.ppermute(x, 'block', [(i, i ^ mask) for i in range(lax.axis_size('blo...  5.48 us
    ppermute x1, starting transfers between devices, beyond(): lax.ppermute(x, 'block', [(i, (i + (1 if i % 2 else -1)) % size) for i in...  4.71 us
    all_to_all x1, starting transfers between devices, local(): points = lax.all_to_all(points, ('zone', 'block'), 0, 0, tiled=True)  3.41 us
    pallas_call x1, Pallas kernels, wall_gradient(): pl.pallas_call(functools.partial(wall_kernel, devices=devices), in_specs=...  2.66 us
    pallas_call x1, Pallas kernels, pack(): pl.pallas_call(pack_kernel, in_specs=[pl.BlockSpec(memory_space=pltpu.HBM...  1.69 us
    ppermute x1, starting transfers between devices, swapped(): lax.ppermute(x, 'zone', [(i, i ^ 1) for i in range(lax.axis_size('zone'))])  1.56 us
    pallas_call x1, Pallas kernels, stage(): pl.pallas_call(stage_kernel, in_specs=[vm] * 5, out_specs=[vm] * len(outs...  1.11 us
  transfers between devices with their start and end apart: 9, of which 0 were waited for; matrix products, arithmetic and copies ran while one was open for 0% of the time, Pallas kernels for 44%

profile of v6, /device:TPU:0, one launch (start us, length us, event | category | flops | bytes accessed | tf_op | source)
XLA Modules:
  0.0 32.7 jit_solution(6187547722329395760)
XLA Ops:
  0.7 1.7 %pack.1 = (f32[64,128]{1,0:T(8,128)S(1)}, f32[56,512]{1,0:T(8,128)S(1)}, f32[56,512]{1,0:T(8,128)S(1)}) custom-call(f32[5,1,128,512]{3,2,1,0:T(8,128)} %u_own.3, f32[5,1,128,512]{3,2,1,0:T(8,128)} %l_own.3, f32[1,128,512]{2,1,0:T(8,128)} %k_own.3, s32[4,1,1024]{2,1,0:T(1,128)} %map_hbm.1, f32[4,1,1024]{2,1,0:T(1,128)} %weight_hbm.1), custom_call_target="tpu_custom_call" | custom-call | tf_op jit(solution)/shard_map/pack/pallas_call | solution.py:104
  2.4 0.5 %collective-permute-start.3 = (f32[56,512]{1,0:T(8,128)S(1)}, f32[56,512]{1,0:T(8,128)S(1)}, u32[]{:S(2)}, u32[]{:S(2)}) collective-permute-start(f32[56,512]{1,0:T(8,128)S(1)} %get-tuple-element.20), channel_id=1, source_target_pairs={{0,1},{1,0},{2,3},{3,2},{4,5},{5,4},{6,7},{7,6},{8,9},{9,8},{10,11... | collective-permute-start | bytes 344072 | tf_op jit(solution)/shard_map/ppermute | solution.py:649
  2.9 4.7 %collective-permute-start.4 = (f32[56,512]{1,0:T(8,128)S(1)}, f32[56,512]{1,0:T(8,128)S(1)}, u32[]{:S(2)}, u32[]{:S(2)}) collective-permute-start(f32[56,512]{1,0:T(8,128)S(1)} %get-tuple-element.21), channel_id=1, source_target_pairs={{0,7},{1,2},{2,1},{3,4},{4,3},{5,6},{6,5},{7,0},{8,15},{9,10},{10,... | collective-permute-start | bytes 344072 | tf_op jit(solution)/shard_map/ppermute | solution.py:645
  7.6 0.4 %collective-permute-start.2 = (f32[1,64,128]{2,1,0:T(8,128)S(1)}, f32[1,64,128]{2,1,0:T(8,128)S(1)}, u32[]{:S(2)}, u32[]{:S(2)}) collective-permute-start(f32[1,64,128]{2,1,0:T(8,128)S(1)} %bitcast.1), channel_id=1, source_target_pairs={{0,6},{1,7},{2,4},{3,5},{4,2},{5,3},{6,0},{7,1},{8,14},{9,15},{10,... | collective-permute-start | bytes 98312 | tf_op jit(solution)/shard_map/ppermute | solution.py:649
  8.1 0.0 collective-permute-start.1
  8.1 3.9 %collective-permute-start = (f32[1,64,128]{2,1,0:T(8,128)S(1)}, f32[1,64,128]{2,1,0:T(8,128)S(1)}, u32[]{:S(2)}, u32[]{:S(2)}) collective-permute-start(f32[1,64,128]{2,1,0:T(8,128)S(1)} %bitcast.3), channel_id=1, source_target_pairs={{0,2},{1,3},{2,0},{3,1},{4,6},{5,7},{6,4},{7,5},{8,10},{9,11},{10,... | collective-permute-start | bytes 98312 | tf_op jit(solution)/shard_map/ppermute | solution.py:649
  12.0 0.0 collective-permute-done.3.near
  12.0 0.0 collective-permute-done.4.far
  12.0 0.0 copy-done.1
  12.1 2.7 %wall_gradient.1 = f32[32,3,256]{2,1,0:T(4,128)} custom-call(f32[5,1,128,512]{3,2,1,0:T(8,128)S(1)} %copy-done, f32[5,1,128,512]{3,2,1,0:T(8,128)S(1)} %copy-done.1, f32[1,128,512]{2,1,0:T(8,128)S(1)} %copy-done.2, f32[56,512]{1,0:T(8,128)S(1)} %collective-permute-done.3.near, f32[56,512]{1,0:T(8,128)S(1)} %collective-permute-done.4.far, ...), custom_call_target="tpu_custom_call" | custom-call | tf_op jit(solution)/shard_map/wall_gradient/pallas_call | solution.py:237
  14.8 0.0 collective-permute-done.2
  14.8 0.0 collective-permute-done.1
  14.8 0.0 collective-permute-done
  14.8 1.6 %collective-permute-start.5 = (f32[4,64,128]{2,1,0:T(8,128)S(1)}, f32[4,64,128]{2,1,0:T(8,128)S(1)}, u32[]{:S(2)}, u32[]{:S(2)}) collective-permute-start(f32[4,64,128]{2,1,0:T(8,128)S(1)} %constant_dynamic-update-slice_fusion.same_0), channel_id=1, source_target_pairs={{0,8},{8,0},{16,24},{24,16},{1,9},{9,1},{17,25},{25,17},{2,10},{10... | collective-permute-start | bytes 393224 | tf_op jit(solution)/shard_map/ppermute | solution.py:653
  16.4 3.4 %all-to-all-start = ((f32[32,3,256]{2,1,0:T(4,128)}), f32[32,3,256]{2,1,0:T(4,128)S(1)}, u32[]{:S(2)}, u32[]{:S(2)}) async-start(f32[32,3,256]{2,1,0:T(4,128)} %wall_gradient.1), calls=%async_computation | async-start | bytes 262144 | tf_op jit(solution)/shard_map/all_to_all | solution.py:692
  19.8 0.1 collective-permute-start.6
  20.0 0.0 collective-permute-done.5.same_1
  20.0 0.4 %collective-permute-start.7 = (f32[4,64,128]{2,1,0:T(8,128)S(1)}, f32[4,64,128]{2,1,0:T(8,128)S(1)}, u32[]{:S(2)}, u32[]{:S(2)}) collective-permute-start(f32[4,64,128]{2,1,0:T(8,128)S(1)} %collective-permute-done.5.same_1), channel_id=1, source_target_pairs={{0,1},{1,0},{2,3},{3,2},{4,5},{5,4},{6,7},{7,6},{8,9},{9,8},{10,11... | collective-permute-start | bytes 393224 | tf_op jit(solution)/shard_map/ppermute | solution.py:649
  20.4 1.1 %stage.1 = (f32[5,20,8,512]{3,2,1,0:T(8,128)S(1)}, f32[5,18,8,512]{3,2,1,0:T(8,128)S(1)}, f32[5,20,8,512]{3,2,1,0:T(8,128)S(1)}, f32[18,8,512]{2,1,0:T(8,128)S(1)}, f32[18,8,512]{2,1,0:T(8,128)S(1)}) custom-call(f32[5,1,128,512]{3,2,1,0:T(8,128)S(1)} %copy-done, f32[5,1,128,512]{3,2,1,0:T(8,128)S(1)} %copy-done.1, f32[1,128,512]{2,1,0:T(8,128)S(1)} %copy-done.2, ...), custom_call_target="tpu_custom_call" | custom-call | tf_op jit(solution)/shard_map/stage/pallas_call | solution.py:481
  21.5 0.0 collective-permute-done.6.other_0
  21.5 0.0 collective-permute-done.7.other_1
  21.5 10.5 %field.1 = f32[5,1,128,512]{3,2,1,0:T(8,128)} custom-call(f32[5,20,8,512]{3,2,1,0:T(8,128)S(1)} %get-tuple-element.28.state_0, f32[5,18,8,512]{3,2,1,0:T(8,128)S(1)} %get-tuple-element.29.lam_0, f32[5,20,8,512]{3,2,1,0:T(8,128)S(1)} %get-tuple-element.30.scaled_0, f32[18,8,512]{2,1,0:T(8,128)S(1)} %get-tuple-element.31.kap, ...), custom_call_target="tpu_custom_call" | custom-call | tf_op jit(solution)/shard_map/field/pallas_call | solution.py:620
  32.1 0.0 all-to-all-done
  32.1 0.6 %reduce_sum.9 = f32[3,256]{1,0:T(4,128)} reduce(f32[32,3,256]{2,1,0:T(4,128)S(1)} %all-to-all-done, f32[]{:T(128)} %constant.0.clone.1), dimensions={0}, to_apply=%region_0.0 | reduce | flops 23808 | bytes 101380 | tf_op jit(solution)/shard_map/reduce_sum | solution.py:697
  (19 shorter events, 0.1 us)
Async XLA Ops:
  0.6 11.4 %copy-start.1 = (f32[5,1,128,512]{3,2,1,0:T(8,128)S(1)}, f32[5,1,128,512]{3,2,1,0:T(8,128)}, u32[]{:S(2)}) copy-start(f32[5,1,128,512]{3,2,1,0:T(8,128)} %l_own.3) | copy-start | bytes 3932164
  0.6 11.4 %copy-start.2 = (f32[1,128,512]{2,1,0:T(8,128)S(1)}, f32[1,128,512]{2,1,0:T(8,128)}, u32[]{:S(2)}) copy-start(f32[1,128,512]{2,1,0:T(8,128)} %k_own.3) | copy-start | bytes 786436
  0.7 11.4 %copy-start = (f32[5,1,128,512]{3,2,1,0:T(8,128)S(1)}, f32[5,1,128,512]{3,2,1,0:T(8,128)}, u32[]{:S(2)}) copy-start(f32[5,1,128,512]{3,2,1,0:T(8,128)} %u_own.3) | copy-start | bytes 3932164
  0.7 11.4 %copy-start.3 = (f32[5,5]{1,0:T(8,128)S(1)}, f32[5,5]{1,0:T(8,128)}, u32[]{:S(2)}) copy-start(f32[5,5]{1,0:T(8,128)} %c_hbm.1) | copy-start | bytes 304
  0.7 11.4 %copy-start.5 = (f32[1,8,384]{2,1,0:T(8,128)S(1)}, f32[1,8,384]{2,1,0:T(8,128)}, u32[]{:S(2)}) copy-start(f32[1,8,384]{2,1,0:T(8,128)} %dist.1) | copy-start | bytes 36868
  0.7 11.4 %copy-start.4 = (s32[1,8,384]{2,1,0:T(8,128)S(1)}, s32[1,8,384]{2,1,0:T(8,128)}, u32[]{:S(2)}) copy-start(s32[1,8,384]{2,1,0:T(8,128)} %ids.1) | copy-start | bytes 36868
  0.7 11.4 %copy-start.6 = (f32[3,5]{1,0:T(4,128)S(1)}, f32[3,5]{1,0:T(4,128)}, u32[]{:S(2)}) copy-start(f32[3,5]{1,0:T(4,128)} %proj_ref.1) | copy-start | bytes 184
  0.7 11.4 %copy-start.7 = (f32[1,384]{1,0:T(1,128)S(1)}, f32[1,384]{1,0:T(1,128)}, u32[]{:S(2)}) copy-start(f32[1,384]{1,0:T(1,128)} %area.1) | copy-start | bytes 4612
  2.4 9.6 %collective-permute-start.3 = (f32[56,512]{1,0:T(8,128)S(1)}, f32[56,512]{1,0:T(8,128)S(1)}, u32[]{:S(2)}, u32[]{:S(2)}) collective-permute-start(f32[56,512]{1,0:T(8,128)S(1)} %get-tuple-element.20), channel_id=1, source_target_pairs={{0,1},{1,0},{2,3},{3,2},{4,5},{5,4},{6,7},{7,6},{8,9},{9,8},{10,11... | collective-permute-start | bytes 344072 | tf_op jit(solution)/shard_map/ppermute | solution.py:649
  2.9 9.1 %collective-permute-start.4 = (f32[56,512]{1,0:T(8,128)S(1)}, f32[56,512]{1,0:T(8,128)S(1)}, u32[]{:S(2)}, u32[]{:S(2)}) collective-permute-start(f32[56,512]{1,0:T(8,128)S(1)} %get-tuple-element.21), channel_id=1, source_target_pairs={{0,7},{1,2},{2,1},{3,4},{4,3},{5,6},{6,5},{7,0},{8,15},{9,10},{10,... | collective-permute-start | bytes 344072 | tf_op jit(solution)/shard_map/ppermute | solution.py:645
  7.6 7.1 %collective-permute-start.2 = (f32[1,64,128]{2,1,0:T(8,128)S(1)}, f32[1,64,128]{2,1,0:T(8,128)S(1)}, u32[]{:S(2)}, u32[]{:S(2)}) collective-permute-start(f32[1,64,128]{2,1,0:T(8,128)S(1)} %bitcast.1), channel_id=1, source_target_pairs={{0,6},{1,7},{2,4},{3,5},{4,2},{5,3},{6,0},{7,1},{8,14},{9,15},{10,... | collective-permute-start | bytes 98312 | tf_op jit(solution)/shard_map/ppermute | solution.py:649
  8.1 6.7 %collective-permute-start.1 = (f32[1,64,128]{2,1,0:T(8,128)S(1)}, f32[1,64,128]{2,1,0:T(8,128)S(1)}, u32[]{:S(2)}, u32[]{:S(2)}) collective-permute-start(f32[1,64,128]{2,1,0:T(8,128)S(1)} %bitcast.2), channel_id=1, source_target_pairs={{0,4},{1,5},{2,6},{3,7},{4,0},{5,1},{6,2},{7,3},{8,12},{9,13},{10,... | collective-permute-start | bytes 98312 | tf_op jit(solution)/shard_map/ppermute | solution.py:649
  8.1 6.7 %collective-permute-start = (f32[1,64,128]{2,1,0:T(8,128)S(1)}, f32[1,64,128]{2,1,0:T(8,128)S(1)}, u32[]{:S(2)}, u32[]{:S(2)}) collective-permute-start(f32[1,64,128]{2,1,0:T(8,128)S(1)} %bitcast.3), channel_id=1, source_target_pairs={{0,2},{1,3},{2,0},{3,1},{4,6},{5,7},{6,4},{7,5},{8,10},{9,11},{10,... | collective-permute-start | bytes 98312 | tf_op jit(solution)/shard_map/ppermute | solution.py:649
  14.8 5.1 %collective-permute-start.5 = (f32[4,64,128]{2,1,0:T(8,128)S(1)}, f32[4,64,128]{2,1,0:T(8,128)S(1)}, u32[]{:S(2)}, u32[]{:S(2)}) collective-permute-start(f32[4,64,128]{2,1,0:T(8,128)S(1)} %constant_dynamic-update-slice_fusion.same_0), channel_id=1, source_target_pairs={{0,8},{8,0},{16,24},{24,16},{1,9},{9,1},{17,25},{25,17},{2,10},{10... | collective-permute-start | bytes 393224 | tf_op jit(solution)/shard_map/ppermute | solution.py:653
  16.4 15.7 %all-to-all-start = ((f32[32,3,256]{2,1,0:T(4,128)}), f32[32,3,256]{2,1,0:T(4,128)S(1)}, u32[]{:S(2)}, u32[]{:S(2)}) async-start(f32[32,3,256]{2,1,0:T(4,128)} %wall_gradient.1), calls=%async_computation | async-start | bytes 262144 | tf_op jit(solution)/shard_map/all_to_all | solution.py:692
  19.8 1.7 %collective-permute-start.6 = (f32[4,64,128]{2,1,0:T(8,128)S(1)}, f32[4,64,128]{2,1,0:T(8,128)S(1)}, u32[]{:S(2)}, u32[]{:S(2)}) collective-permute-start(f32[4,64,128]{2,1,0:T(8,128)S(1)} %constant_dynamic-update-slice_fusion.same_0), channel_id=1, source_target_pairs={{0,1},{1,0},{2,3},{3,2},{4,5},{5,4},{6,7},{7,6},{8,9},{9,8},{10,11... | collective-permute-start | bytes 393224 | tf_op jit(solution)/shard_map/ppermute | solution.py:649
  20.0 1.6 %collective-permute-start.7 = (f32[4,64,128]{2,1,0:T(8,128)S(1)}, f32[4,64,128]{2,1,0:T(8,128)S(1)}, u32[]{:S(2)}, u32[]{:S(2)}) collective-permute-start(f32[4,64,128]{2,1,0:T(8,128)S(1)} %collective-permute-done.5.same_1), channel_id=1, source_target_pairs={{0,1},{1,0},{2,3},{3,2},{4,5},{5,4},{6,7},{7,6},{8,9},{9,8},{10,11... | collective-permute-start | bytes 393224 | tf_op jit(solution)/shard_map/ppermute | solution.py:649
